TPU v7x, 128 devices: a whole 4x4x4 slice. The times are simulated.
128 devices in a mesh: tp: 2 (over core), grp: 32 (over z, y, x_lo), rep: 2 (over x_hi).
Axes of the slice: x: 4 (x_hi: 2, x_lo: 2; x = x_hi * 2 + x_lo), y: 4, z: 4, core: 2. Of those that a mesh axis runs over, the one named last changes fastest.
Arguments:
- tokens: bfloat16 [8192, 4096], P(('rep', 'tp', 'grp')), parts along dimension 0, may hold values from -6 to 6
- qkv_weight: bfloat16 [4096, 5120], P(None, ('tp', 'grp')), may hold values from -0.09375 to 0.09375
- qkv_bias: bfloat16 [5120], replicated, may hold values from -3 to 3
- cache: bfloat16 [512, 1024, 1024], P(('rep', 'tp', 'grp')), parts along dimension 0, may hold values from -80 to 80
- lengths: int32 [512], P('rep'), parts along dimension 0, may hold values from 128 to 1024, as said below
- slot_stream: int32 [512], P('rep'), parts along dimension 0, may hold values from 0 to 255, each once
Outputs:
- attended: bfloat16 [8192, 4096], P(('rep', 'tp', 'grp')), parts along dimension 0
There are 2 independent parts, one for each index of `rep`. A program takes and returns all parts, laid end to end along the dimension named above; an argument that names none is the same for every part. Nothing has to cross between parts.
Inputs may be any that keep to these rules, and one draw needn't show every extreme that they name: `lengths`: cache length of each stream; some stream has exactly 1024 and some exactly 128. `slot_stream`: each stream appears in exactly one slot.
All inputs are finite; a program needn't handle non-finite values.
Results may differ from a plain program's by a relative error of at most 0.004.
The roundings to bfloat16 on the way count: a program that leaves them out, or rounds other values in their place, can miss the bound.
Values may be sent and summed in bfloat16 or wider, within the bound.
No kernel may reach another device: no remote copies, remote signals or barrier semaphores. Data moves between devices by JAX's collectives and lax.ppermute only.
A program may use at most 128 MiB of HBM per device.

v0:
```python
import jax
import jax.numpy as jnp
from jax import lax
from jax.sharding import PartitionSpec as P

HD = 128
HQ = 32
KVH = 4
STRETCH = 16
CAP = 1024
GROUP = 8


ROPE_THETA = 1000000.0


def rotate(vectors, positions):
    half_width = vectors.shape[-1] // 2
    frequency = ROPE_THETA ** (
        -(jnp.arange(half_width, dtype=jnp.float32) * 2.0) / vectors.shape[-1]
    )
    angles = positions.astype(jnp.float32)[:, None] * frequency[None, :]
    cosine = jnp.cos(angles)[:, None, :]
    sine_part = jnp.sin(angles)[:, None, :]
    front_half = vectors[..., :half_width]
    back_half = vectors[..., half_width:]
    return jnp.concatenate(
        [front_half * cosine - back_half * sine_part, back_half * cosine + front_half * sine_part],
        axis=-1,
    )


def attend(token_block, slot_cache, length):
    query_width = HQ * HD
    kv_width = KVH * HD
    positions = length + jnp.arange(STRETCH, dtype=jnp.int32)
    queries = rotate(
        token_block[:, :query_width].astype(jnp.float32).reshape(STRETCH, HQ, HD), positions
    ).astype(jnp.bfloat16)
    new_keys = rotate(
        token_block[:, query_width : query_width + kv_width]
        .astype(jnp.float32)
        .reshape(STRETCH, KVH, HD),
        positions,
    ).astype(jnp.bfloat16)
    new_values = token_block[:, query_width + kv_width :].reshape(STRETCH, KVH, HD)
    grouped = (
        queries.reshape(STRETCH, KVH, GROUP, HD)
        .transpose(1, 0, 2, 3)
        .reshape(KVH, STRETCH * GROUP, HD)
    )
    score_scale = HD ** (-0.5)
    query_token = jnp.arange(STRETCH * GROUP, dtype=jnp.int32) // GROUP
    scores = (
        jnp.einsum("krd,jkd->krj", grouped, new_keys, preferred_element_type=jnp.float32)
        * score_scale
    )
    causal = jnp.arange(STRETCH, dtype=jnp.int32)[None, :] <= query_token[:, None]
    scores = jnp.where(causal[None], scores, -jnp.inf)
    row_max = jnp.max(scores, axis=-1)
    exponent = jnp.exp(scores - row_max[..., None])
    row_total = jnp.sum(exponent, axis=-1)
    running = jnp.einsum(
        "krj,jkd->krd",
        exponent.astype(jnp.bfloat16),
        new_values,
        preferred_element_type=jnp.float32,
    )
    key_span = min(CAP, 256)
    key_part = slot_cache[:, :kv_width]
    value_part = slot_cache[:, kv_width:]

    def visit(block_index, running_state):
        old_max, old_total, old_sum = running_state
        offset = block_index * key_span
        key_block = lax.dynamic_slice_in_dim(key_part, offset, key_span, 0).reshape(
            key_span, KVH, HD
        )
        value_block = lax.dynamic_slice_in_dim(value_part, offset, key_span, 0).reshape(
            key_span, KVH, HD
        )
        block_scores = (
            jnp.einsum("krd,jkd->krj", grouped, key_block, preferred_element_type=jnp.float32)
            * score_scale
        )
        in_cache = offset + jnp.arange(key_span, dtype=jnp.int32) < length
        block_scores = jnp.where(in_cache[None, None, :], block_scores, -jnp.inf)
        new_max = jnp.maximum(old_max, jnp.max(block_scores, axis=-1))
        rescale = jnp.exp(old_max - new_max)
        block_exp = jnp.exp(block_scores - new_max[..., None])
        new_total = old_total * rescale + jnp.sum(block_exp, axis=-1)
        new_sum = old_sum * rescale[..., None] + jnp.einsum(
            "krj,jkd->krd",
            block_exp.astype(jnp.bfloat16),
            value_block,
            preferred_element_type=jnp.float32,
        )
        return (new_max, new_total, new_sum)

    block_count = CAP // key_span
    row_max, row_total, running = lax.fori_loop(
        0, block_count, visit, (row_max, row_total, running)
    )
    result = running / row_total[..., None]
    return (
        result.reshape(KVH, STRETCH, GROUP, HD)
        .transpose(1, 0, 2, 3)
        .reshape(STRETCH, HQ * HD)
        .astype(jnp.bfloat16)
    )


def on_device(tokens, qkv_weight, qkv_bias, cache, lengths, slot_stream):
    my_index = lax.axis_index(("tp", "grp"))
    grp_index = lax.axis_index("grp")
    tp_count = lax.axis_size("tp")
    grp_count = lax.axis_size("grp")
    per_device = cache.shape[0]
    local_rows = per_device * STRETCH
    shard_cols = qkv_weight.shape[1]
    weight_cols = lax.all_gather(qkv_weight, "tp", axis=1, tiled=True)
    bias_table = qkv_bias.reshape(tp_count, grp_count, shard_cols)
    bias_cols = (
        lax.dynamic_index_in_dim(bias_table, grp_index, 1, keepdims=False)
        .reshape(-1)
        .astype(jnp.float32)
    )
    partial_cols = jnp.dot(
        lax.all_gather(tokens, "grp", axis=0, tiled=True),
        weight_cols,
        preferred_element_type=jnp.float32,
    )
    rounded_cols = (partial_cols + bias_cols[None, :]).astype(jnp.bfloat16)
    received = lax.all_to_all(rounded_cols, "grp", split_axis=0, concat_axis=1, tiled=True)
    projected_qkv = (
        received.reshape(local_rows, grp_count, tp_count, shard_cols)
        .transpose(0, 2, 1, 3)
        .reshape(local_rows, -1)
    )
    my_slots = my_index * per_device + jnp.arange(per_device, dtype=jnp.int32)
    my_lengths = jnp.take(lengths, jnp.take(slot_stream, my_slots))
    attended = jnp.concatenate(
        [
            attend(
                projected_qkv[slot_index * STRETCH : (slot_index + 1) * STRETCH],
                cache[slot_index],
                my_lengths[slot_index],
            )
            for slot_index in range(per_device)
        ],
        axis=0,
    )
    return attended


def solution(mesh):
    in_specs = (
        P(("rep", "tp", "grp"), None),
        P(None, ("tp", "grp")),
        P(),
        P(("rep", "tp", "grp"), None, None),
        P("rep"),
        P("rep"),
    )
    out_specs = P(("rep", "tp", "grp"), None)
    return jax.shard_map(
        on_device, mesh=mesh, in_specs=in_specs, out_specs=out_specs, check_vma=False
    )
```

profile of v0, /device:TPU:1, one launch (start us, length us, event | category | flops | bytes accessed | tf_op | source)
XLA Modules:
  0.0 482.2 jit_solution(10885012108823817912)
XLA Ops:
  6.5 0.7 all-gather.5.cloned.1.call-update
  7.3 0.7 all-gather.3.cloned.1.call-update
  8.0 0.8 reshape.476
  8.9 5.6 %fusion.89 = (bf16[1,1024,1024]{2,1,0:T(8,128)(2,1)}, bf16[1,1024,1024]{2,1,0:T(8,128)(2,1)}, bf16[1,1024,1024]{2,1,0:T(8,128)(2,1)}, bf16[1,1024,1024]{2,1,0:T(8,128)(2,1)S(1)}) fusion(bf16[4,1024,1024]{2,1,0:T(8,128)(2,1)} %param.19), kind=kLoop, calls=%fused_computation.195 | loop fusion | bytes 16777216 | tf_op jit(solution)/shard_map/slice | solution.py:146
  14.6 2.6 copy.114
  17.1 2.9 copy.111
  20.0 0.6 gather_fusion
  20.7 0.6 gather_fusion.1
  21.4 0.7 fusion.99
  22.1 0.6 add_convert_fusion.11
  22.7 0.6 add_convert_fusion.10
  23.3 0.6 add_convert_fusion.9
  23.8 0.7 add_convert_fusion.8
  24.7 3.0 fusion.93
  27.8 1.5 fusion.92
  29.3 361.6 %all-gather.3.cloned.1.call-done = bf16[2048,4096]{1,0:T(8,128)(2,1)} async-done(((bf16[64,4096]{1,0:T(8,128)(2,1)}), bf16[2048,4096]{1,0:T(8,128)(2,1)}) %all-gather.3.cloned.1.call-update) | async-done | bytes 16777232 | tf_op jit(solution)/shard_map/all_gather | solution.py:129
  390.9 11.8 %fusion.24 = bf16[2048,160]{0,1:T(8,128)(2,1)S(1)} fusion(bf16[2048,4096]{1,0:T(8,128)(2,1)} %all-gather.3.cloned.1.call-done, bf16[4096,160]{0,1:T(8,128)(2,1)} %all-gather.5.cloned.1.call-done, f32[160]{0:T(256)S(1)} %reshape.502), kind=kOutput, calls=%fused_computation.55 | convolution fusion | flops 2685009920 | bytes 18743936 | tf_op jit(solution)/shard_map/dot_general | solution.py:128
  402.7 1.3 copy.102
  404.0 4.9 %all-to-all-start = ((bf16[32,64,160]{2,1,0:T(8,128)(2,1)}), bf16[32,64,160]{2,1,0:T(8,128)(2,1)}, u32[]{:S(2)}, u32[]{:S(2)}) async-start(bf16[32,64,160]{2,1,0:T(8,128)(2,1)} %bitcast.12), calls=%async_computation | async-start | bytes 2097152 | tf_op jit(solution)/shard_map/all_to_all | solution.py:134
  408.9 2.6 copy.108
  411.5 2.9 copy.105
  414.3 3.0 fusion.91
  417.3 1.1 fusion.90
  418.5 7.0 %all-to-all-done = bf16[32,64,160]{2,1,0:T(8,128)(2,1)} async-done(((bf16[32,64,160]{2,1,0:T(8,128)(2,1)}), bf16[32,64,160]{2,1,0:T(8,128)(2,1)}, u32[]{:S(2)}, u32[]{:S(2)}) %all-to-all-start) | async-done | bytes 655392 | tf_op jit(solution)/shard_map/all_to_all | solution.py:134
  425.5 1.6 reshape.477
  427.1 1.2 copy.180
  428.4 0.3 slice.183
  431.2 10.3 %while.71 = (s32[]{:T(128)}, f32[4,128]{1,0:T(4,128)S(1)}, f32[4,128]{1,0:T(4,128)S(1)}, f32[4,128,128]{2,1,0:T(8,128)S(1)}, s32[]{:T(128)}, /*index=5*/bf16[102...) while((s32[]{:T(128)}, f32[4,128]{1,0:T(4,128)S(1)}, ...), condition=%wide.region_23.25_spmd, body=%wide.region_20.24_spmd.sunk | while | flops 68158976 | bytes 3834551 | solution.py:101
  431.2 1.1 constant_dynamic-slice_fusion.15
  432.3 0.7 add_compare_fusion.11
  433.8 1.1 constant_dynamic-slice_fusion.15
  434.9 0.7 add_compare_fusion.11
  436.4 1.1 constant_dynamic-slice_fusion.15
  437.5 0.7 add_compare_fusion.11
  439.0 1.1 constant_dynamic-slice_fusion.15
  440.0 0.7 add_compare_fusion.11
  442.4 9.8 %while.70 = (s32[]{:T(128)}, f32[4,128]{1,0:T(4,128)S(1)}, f32[4,128]{1,0:T(4,128)S(1)}, f32[4,128,128]{2,1,0:T(8,128)S(1)}, s32[]{:T(128)}, /*index=5*/bf16[102...) while((s32[]{:T(128)}, f32[4,128]{1,0:T(4,128)S(1)}, ...), condition=%wide.region_17.19_spmd, body=%wide.region_14.18_spmd.sunk | while | flops 68158976 | bytes 3834551 | solution.py:101
  442.5 1.1 constant_dynamic-slice_fusion.14
  443.5 0.6 add_compare_fusion.10
  444.9 1.1 constant_dynamic-slice_fusion.14
  446.0 0.6 add_compare_fusion.10
  447.4 1.1 constant_dynamic-slice_fusion.14
  448.5 0.6 add_compare_fusion.10
  449.8 1.1 constant_dynamic-slice_fusion.14
  450.9 0.6 add_compare_fusion.10
  453.8 9.7 %while.69 = (s32[]{:T(128)}, f32[4,128]{1,0:T(4,128)S(1)}, f32[4,128]{1,0:T(4,128)S(1)}, f32[4,128,128]{2,1,0:T(8,128)S(1)}, s32[]{:T(128)}, /*index=5*/bf16[102...) while((s32[]{:T(128)}, f32[4,128]{1,0:T(4,128)S(1)}, ...), condition=%wide.region_11.13_spmd, body=%wide.region_8.12_spmd.sunk | while | flops 68158976 | bytes 3834551 | solution.py:101
  453.8 1.1 constant_dynamic-slice_fusion.13
  454.9 0.6 add_compare_fusion.9
  456.3 1.1 constant_dynamic-slice_fusion.13
  457.3 0.6 add_compare_fusion.9
  458.7 1.1 constant_dynamic-slice_fusion.13
  459.8 0.6 add_compare_fusion.9
  461.1 1.1 constant_dynamic-slice_fusion.13
  462.2 0.6 add_compare_fusion.9
  464.5 9.8 %while.68 = (s32[]{:T(128)}, f32[4,128]{1,0:T(4,128)S(1)}, f32[4,128]{1,0:T(4,128)S(1)}, f32[4,128,128]{2,1,0:T(8,128)S(1)}, s32[]{:T(128)}, /*index=5*/bf16[102...) while((s32[]{:T(128)}, f32[4,128]{1,0:T(4,128)S(1)}, ...), condition=%wide.region_5.7_spmd, body=%wide.region_2.6_spmd.sunk | while | flops 68158976 | bytes 3834551 | solution.py:101
  464.5 1.0 constant_dynamic-slice_fusion.12
  465.5 0.6 add_compare_fusion.8
  466.9 1.0 constant_dynamic-slice_fusion.12
  468.0 0.6 add_compare_fusion.8
  469.4 1.0 constant_dynamic-slice_fusion.12
  470.4 0.6 add_compare_fusion.8
  471.9 1.0 constant_dynamic-slice_fusion.12
  472.9 0.6 add_compare_fusion.8
  474.5 0.8 pad_maximum_fusion
  (174 shorter events, 18.2 us)
Async XLA Ops:
  6.5 13.5 %copy-start = (s32[256]{0:T(256)S(1)}, s32[256]{0:T(256)}, u32[]{:S(2)}) copy-start(s32[256]{0:T(256)} %param.21) | copy-start | bytes 3076
  6.5 22.7 %all-gather.5.cloned.1.call-start = ((), (), s32[]{:S(2)}) async-start(), calls=%async_computation.2 | async-start | bytes 1966080 | tf_op jit(solution)/shard_map/all_gather | solution.py:121
  7.3 383.7 %all-gather.3.cloned.1.call-start = ((), (), s32[]{:S(2)}) async-start(), calls=%async_computation.1 | async-start | bytes 17301504 | tf_op jit(solution)/shard_map/all_gather | solution.py:129
  17.1 3.6 copy-start.2
  402.7 6.2 %copy-start.3 = (bf16[1,1024,1024]{2,1,0:T(8,128)(2,1)S(1)}, bf16[1,1024,1024]{2,1,0:T(8,128)(2,1)}, u32[]{:S(2)}) copy-start(bf16[1,1024,1024]{2,1,0:T(8,128)(2,1)} %get-tuple-element.664) | copy-start | bytes 6291460
  404.0 21.4 %all-to-all-start = ((bf16[32,64,160]{2,1,0:T(8,128)(2,1)}), bf16[32,64,160]{2,1,0:T(8,128)(2,1)}, u32[]{:S(2)}, u32[]{:S(2)}) async-start(bf16[32,64,160]{2,1,0:T(8,128)(2,1)} %bitcast.12), calls=%async_computation | async-start | bytes 2097152 | tf_op jit(solution)/shard_map/all_to_all | solution.py:134
  474.3 1.1 copy-start.1
Sparse Core Ops, SparseCore 0:
  9.0 15.7 all-gather.4
  26.5 364.4 all-gather.2
where the time goes:
time: 484 us; the launch traced here: 482 us
  waiting for transfers between devices  370 us (76%)
  local copies, waits for them, and re-layouts  51.5 us (11%)
  matrix products  23.9 us (5%)
  other arithmetic  17 us (4%)
  between operations  13.9 us (3%)
  starting transfers between devices  4.9 us (1%)
    all_gather x1, waiting for transfers between devices, on_device(): lax.all_gather(tokens, 'grp', axis=0, tiled=True)  362 us
    dynamic_slice x16, local copies, waits for them, and re-layouts, visit(): lax.dynamic_slice_in_dim(value_part, offset, key_span, 0)  16.9 us
    dot_general x1, matrix products, on_device(): jnp.dot(lax.all_gather(tokens, 'grp', axis=0, tiled=True), weight_cols, p...  11.8 us
    unnamed x20, local copies, waits for them, and re-layouts  11.3 us
    lt x16, other arithmetic, visit(): in_cache = offset + jnp.arange(key_span, dtype=jnp.int32) < length  9.86 us
  transfers between devices with their start and end apart: 3, of which 2 were waited for; matrix products, arithmetic and copies ran while one was open for 6% of the time, Pallas kernels for 0%

commit v1 on v0

v1 whole, which is shorter than its diff:
```python
import functools

import jax
import jax.numpy as jnp
from jax import lax
from jax.experimental import pallas as pl
from jax.experimental.pallas import tpu as pltpu
from jax.sharding import Mesh, PartitionSpec as P

D = 4096
HD = 128
HQ = 32
KVH = 4
STRETCH = 16
CAP = 1024
GROUP = 8
SLOTS = 4
ROWS = SLOTS * STRETCH
COLS = 80
SHARDS = 8
WIDE = COLS * SHARDS
HEADS = WIDE // HD
HALF = D // 2
ROPE_THETA = 1000000.0
LOG2E = 1.4426950408889634
AXES = ("tp", "z", "y", "xl", "xh")
VMEM_LIMIT = 48 * 1024 * 1024
NT = (((1,), (1,)), ((), ()))


def device_index(t, z, y, x):
    x = x % 4
    return ((((t % 2) * 4 + z % 4) * 4 + y % 4) * 2 + x % 2) * 2 + x // 2


def shift(array, dt=0, dz=0, dy=0, dx=0):
    pairs = [
        (device_index(t, z, y, x), device_index(t + dt, z + dz, y + dy, x + dx))
        for t in range(2)
        for z in range(4)
        for y in range(4)
        for x in range(4)
    ]
    return lax.ppermute(array, AXES, pairs)


def turn_kernel(w_ref, whole_ref, low_ref, high_ref):
    turned = w_ref[...].T
    whole_ref[...] = turned
    step = pl.program_id(0)
    half = pl.num_programs(0) // 2

    @pl.when(step < half)
    def _():
        low_ref[...] = turned

    @pl.when(step >= half)
    def _():
        high_ref[...] = turned


def turn(weight):
    steps = 8
    block = D // steps
    half = steps // 2
    return pl.pallas_call(
        turn_kernel,
        grid=(steps,),
        in_specs=[pl.BlockSpec((block, COLS), lambda i: (i, 0))],
        out_specs=[
            pl.BlockSpec((COLS, block), lambda i: (0, i)),
            pl.BlockSpec((COLS, block), lambda i: (0, jnp.minimum(i, half - 1))),
            pl.BlockSpec((COLS, block), lambda i: (0, jnp.maximum(i - half, 0))),
        ],
        out_shape=[
            jax.ShapeDtypeStruct((COLS, D), jnp.bfloat16),
            jax.ShapeDtypeStruct((COLS, HALF), jnp.bfloat16),
            jax.ShapeDtypeStruct((COLS, HALF), jnp.bfloat16),
        ],
        name="turn",
    )(weight)


def project_kernel(where, at_ref, bias_ref, *refs):
    count = len(where)
    pieces = refs[:count]
    rows = refs[count : count + 8]
    outs = refs[count + 8 : count + 16]
    weights, sem = refs[count + 16 :]
    copies = []
    for i, (piece, (dy, side, low, width)) in enumerate(zip(pieces, where)):
        start = pl.multiple_of(at_ref[dy * 2 + side] * COLS, 16)
        copies.append(
            pltpu.make_async_copy(
                piece,
                weights.at[pl.ds(start, COLS), pl.ds(low, width)],
                sem.at[i],
            )
        )
    for copy in copies:
        copy.start()
    for copy in copies:
        copy.wait()
    for row, out in zip(rows, outs):
        product = lax.dot_general(
            row[...], weights[...], NT, preferred_element_type=jnp.float32
        )
        out[...] = (product + bias_ref[...]).astype(jnp.bfloat16)


def project(places, bias, pieces, where, rows):
    return pl.pallas_call(
        functools.partial(project_kernel, where),
        in_specs=[
            pl.BlockSpec(memory_space=pltpu.SMEM),
            pl.BlockSpec(memory_space=pltpu.VMEM),
        ]
        + [pl.BlockSpec(memory_space=pl.ANY)] * len(pieces)
        + [pl.BlockSpec(memory_space=pltpu.VMEM)] * 8,
        out_specs=[pl.BlockSpec(memory_space=pltpu.VMEM)] * 8,
        out_shape=[jax.ShapeDtypeStruct((ROWS, WIDE), jnp.bfloat16)] * 8,
        scratch_shapes=[
            pltpu.VMEM((WIDE, D), jnp.bfloat16),
            pltpu.SemaphoreType.DMA((len(pieces),)),
        ],
        compiler_params=pltpu.CompilerParams(vmem_limit_bytes=VMEM_LIMIT),
        name="project",
    )(places, bias, *pieces, *rows)


def attend_kernel(group_ref, length_ref, cos_ref, sin_ref, *refs):
    blocks = refs[:8]
    cache_ref, out_ref, qkv = refs[8:]
    slot = pl.program_id(0)

    @pl.when(slot == 0)
    def _():
        for i, block in enumerate(blocks):
            qkv[group_ref[i]] = block[...]

    at = pl.ds(pl.multiple_of(slot * STRETCH, STRETCH), STRETCH)
    cosine = cos_ref[at, :]
    sine = sin_ref[at, :]
    length = length_ref[slot]

    def head(h):
        low = (h % HEADS) * HD
        return qkv[h // HEADS, at, low : low + HD]

    def rotated(h):
        u = head(h).astype(jnp.float32)
        return (u * cosine + pltpu.roll(u, HD // 2, 1) * sine).astype(jnp.bfloat16)

    scale = HD ** (-0.5) * LOG2E
    key_at = lax.broadcasted_iota(jnp.int32, (1, CAP), 1)
    hidden = jnp.where(key_at < length, 0.0, -jnp.inf)
    token = lax.broadcasted_iota(jnp.int32, (GROUP * STRETCH, STRETCH), 0) % STRETCH
    new_at = lax.broadcasted_iota(jnp.int32, (GROUP * STRETCH, STRETCH), 1)
    causal = new_at <= token
    for k in range(KVH):
        queries = jnp.concatenate(
            [rotated(k * GROUP + g) for g in range(GROUP)], axis=0
        )
        new_keys = rotated(HQ + k)
        new_values = head(HQ + KVH + k)
        keys = cache_ref[0, :, k * HD : (k + 1) * HD]
        values = cache_ref[0, :, (KVH + k) * HD : (KVH + k + 1) * HD]
        scores = (
            lax.dot_general(queries, keys, NT, preferred_element_type=jnp.float32)
            + hidden
        )
        new_scores = lax.dot_general(
            queries, new_keys, NT, preferred_element_type=jnp.float32
        )
        new_scores = jnp.where(causal, new_scores, -jnp.inf)
        top = jnp.maximum(
            jnp.max(scores, axis=1, keepdims=True),
            jnp.max(new_scores, axis=1, keepdims=True),
        )
        weights = jnp.exp2((scores - top) * scale)
        new_weights = jnp.exp2((new_scores - top) * scale)
        total = jnp.sum(weights, axis=1, keepdims=True) + jnp.sum(
            new_weights, axis=1, keepdims=True
        )
        mixed = jnp.dot(
            weights.astype(jnp.bfloat16), values, preferred_element_type=jnp.float32
        ) + jnp.dot(
            new_weights.astype(jnp.bfloat16),
            new_values,
            preferred_element_type=jnp.float32,
        )
        mixed = (mixed / total).astype(jnp.bfloat16)
        for g in range(GROUP):
            low = (k * GROUP + g) * HD
            out_ref[:, low : low + HD] = mixed[g * STRETCH : (g + 1) * STRETCH]


def attend(groups, lengths, cosine, sine, blocks, cache):
    whole = lambda shape: pl.BlockSpec(shape, lambda j: (0,) * len(shape))
    return pl.pallas_call(
        attend_kernel,
        grid=(SLOTS,),
        in_specs=[
            pl.BlockSpec(memory_space=pltpu.SMEM),
            pl.BlockSpec(memory_space=pltpu.SMEM),
            whole((ROWS, HD)),
            whole((ROWS, HD)),
        ]
        + [whole((ROWS, WIDE))] * 8
        + [pl.BlockSpec((1, CAP, 2 * KVH * HD), lambda j: (j, 0, 0))],
        out_specs=pl.BlockSpec((STRETCH, HQ * HD), lambda j: (j, 0)),
        out_shape=jax.ShapeDtypeStruct((ROWS, HQ * HD), jnp.bfloat16),
        scratch_shapes=[pltpu.VMEM((8, ROWS, WIDE), jnp.bfloat16)],
        compiler_params=pltpu.CompilerParams(vmem_limit_bytes=VMEM_LIMIT),
        name="attend",
    )(groups, lengths, cosine, sine, *blocks, cache)


def on_device(tokens, weight, bias, cache, lengths, slot_stream):
    t = lax.axis_index("tp")
    z = lax.axis_index("z")
    y = lax.axis_index("y")
    xl = lax.axis_index("xl")
    group = t * 4 + z
    index = (group * 4 + y) * 2 + xl

    along = {dz: shift(tokens, dz=dz) for dz in (1, 3, 2)}
    along[0] = tokens
    steps = [(dt, dz) for dt in range(2) for dz in range(4)]
    rows = [along[dz] if dt == 0 else shift(along[dz], dt=1) for dt, dz in steps]

    whole, low, high = turn(weight)
    one, three = shift(whole, dy=1), shift(whole, dy=3)
    two_low, two_high = shift(low, dy=2), shift(high, dy=2)
    pieces = [
        (whole, 0, 0, 0, D),
        (one, 1, 0, 0, D),
        (three, 3, 0, 0, D),
        (two_low, 2, 0, 0, HALF),
        (two_high, 2, 0, HALF, HALF),
        (shift(low, dx=1), 0, 1, 0, HALF),
        (shift(high, dx=3), 0, 1, HALF, HALF),
        (shift(one, dx=1), 1, 1, 0, D),
        (shift(three, dx=3), 3, 1, 0, D),
        (shift(two_low, dx=1), 2, 1, 0, HALF),
        (shift(two_high, dx=3), 2, 1, HALF, HALF),
    ]
    places = jnp.stack(
        [
            ((y - dy) % 4) * 2 + (xl if side == 0 else 1 - xl)
            for dy in range(4)
            for side in range(2)
        ]
    ).astype(jnp.int32)
    bias_cols = lax.dynamic_slice_in_dim(bias, group * WIDE, WIDE, 0)
    bias_cols = bias_cols.astype(jnp.float32)[None, :]

    my_slots = index * SLOTS + jnp.arange(SLOTS, dtype=jnp.int32)
    my_lengths = jnp.take(lengths, jnp.take(slot_stream, my_slots)).astype(jnp.int32)
    positions = (my_lengths[:, None] + jnp.arange(STRETCH, dtype=jnp.int32)).reshape(-1)
    frequency = ROPE_THETA ** (
        -(jnp.arange(HD // 2, dtype=jnp.float32) * 2.0) / HD
    )
    angles = positions.astype(jnp.float32)[:, None] * frequency[None, :]
    cosine, sine = jnp.cos(angles), jnp.sin(angles)
    cosine = jnp.concatenate([cosine, cosine], axis=1)
    sine = jnp.concatenate([-sine, sine], axis=1)

    parts = project(
        places, bias_cols, [p[0] for p in pieces], tuple(p[1:] for p in pieces), rows
    )
    home = [
        part if (dt, dz) == (0, 0) else shift(part, dt=-dt, dz=-dz)
        for part, (dt, dz) in zip(parts, steps)
    ]
    groups = jnp.stack(
        [((t + dt) % 2) * 4 + (z + dz) % 4 for dt, dz in steps]
    ).astype(jnp.int32)
    return attend(groups, my_lengths, cosine, sine, home, cache)


def solution(mesh):
    fine = Mesh(mesh.devices.reshape(2, 4, 4, 2, 2), AXES)
    part = ("xh", "tp", "z", "y", "xl")
    in_specs = (
        P(part, None),
        P(None, ("tp", "z", "y", "xl")),
        P(),
        P(part, None, None),
        P("xh"),
        P("xh"),
    )
    return jax.shard_map(
        on_device,
        mesh=fine,
        in_specs=in_specs,
        out_specs=P(part, None),
        check_vma=False,
    )
```

time: 484 us -> 117 us (0.24)
  waiting for transfers between devices: 370 us -> 29.5 us
  local copies, waits for them, and re-layouts: 51.5 us -> 10.8 us
  starting transfers between devices: 4.9 us -> 43.4 us
  Pallas kernels: 0 us -> 31.5 us
  matrix products: 23.9 us -> 0 us
  other arithmetic: 17 us -> 1.16 us
  between operations: 13.9 us -> 0.19 us
    all_gather x2 -> x0, waiting for transfers between devices: 362 us -> none  [the longest x1 362 us: on_device(): lax.all_gather(tokens, 'grp', axis=0, tiled=True)]
    ppermute x0 -> x24, starting transfers between devices: none -> 43.4 us  [shift(): return lax.ppermute(array, AXES, pairs)]
    pallas_call x0 -> x3, Pallas kernels: none -> 31.5 us  [the longest x1 16.3 us: project(): pl.pallas_call(functools.partial(project_kernel, where), in_specs=[pl.Blo...]
    ppermute x0 -> x24, waiting for transfers between devices: none -> 29.5 us  [shift(): return lax.ppermute(array, AXES, pairs)]
    dot_general x41 -> x0, matrix products: 23.9 us -> none  [the longest x1 11.8 us: on_device(): jnp.dot(lax.all_gather(tokens, 'grp', axis=0, tiled=True), weight_cols, p...]
    dynamic_slice x16 -> x0, local copies, waits for them, and re-layouts: 16.9 us -> none  [visit(): lax.dynamic_slice_in_dim(value_part, offset, key_span, 0)]
    slice x15 -> x0, local copies, waits for them, and re-layouts: 16.8 us -> none  [the longest x4 8.7 us: attend(): value_part = slot_cache[:, kv_width:]]
    lt x16 -> x0, other arithmetic: 9.86 us -> none  [visit(): in_cache = offset + jnp.arange(key_span, dtype=jnp.int32) < length]
  transfers between devices with their start and end apart: 3 -> 24, of which waited for: 2 -> 10; matrix products, arithmetic and copies ran while one was open for 6% -> 3% of each run, Pallas kernels for 0% -> 0%
where the time goes in v1:
time: 117 us; the launch traced here: 116 us
  starting transfers between devices  43.4 us (37%)
  Pallas kernels  31.5 us (27%)
  waiting for transfers between devices  29.5 us (25%)
  local copies, waits for them, and re-layouts  10.8 us (9%)
    ppermute x24, starting transfers between devices, shift(): return lax.ppermute(array, AXES, pairs)  43.4 us
    ppermute x24, waiting for transfers between devices, shift(): return lax.ppermute(array, AXES, pairs)  29.5 us
    pallas_call x1, Pallas kernels, project(): pl.pallas_call(functools.partial(project_kernel, where), in_specs=[pl.Blo...  16.3 us
    pallas_call x1, Pallas kernels, attend(): pl.pallas_call(attend_kernel, grid=(SLOTS,), in_specs=[pl.BlockSpec(memor...  9.67 us
    unnamed x19, local copies, waits for them, and re-layouts  8.56 us
    pallas_call x1, Pallas kernels, turn(): pl.pallas_call(turn_kernel, grid=(steps,), in_specs=[pl.BlockSpec((block,...  5.53 us
  transfers between devices with their start and end apart: 24, of which 10 were waited for; matrix products, arithmetic and copies ran while one was open for 3% of the time, Pallas kernels for 0%

profile of v1, /device:TPU:1, one launch (start us, length us, event | category | flops | bytes accessed | tf_op | source)
XLA Modules:
  0.0 116.5 jit_solution(6576739109170820538)
XLA Ops:
  0.0 2.2 %copy.8.w_ref = bf16[4096,80]{1,0:T(8,128)(2,1)} copy(bf16[4096,80]{0,1:T(8,128)(2,1)} %param.9) | data formatting | bytes 1310720 | tf_op args[1]
  2.2 5.5 %turn.1 = (bf16[80,4096]{1,0:T(8,128)(2,1)}, bf16[80,2048]{1,0:T(8,128)(2,1)}, bf16[80,2048]{1,0:T(8,128)(2,1)}) custom-call(bf16[4096,80]{1,0:T(8,128)(2,1)} %copy.8.w_ref), custom_call_target="tpu_custom_call" | custom-call | tf_op jit(solution)/shard_map/turn/pallas_call | solution.py:66
  7.8 3.7 %collective-permute-start.2 = (bf16[80,2048]{1,0:T(8,128)(2,1)}, bf16[80,2048]{1,0:T(8,128)(2,1)S(1)}, u32[]{:S(2)}, u32[]{:S(2)}) collective-permute-start(bf16[80,2048]{1,0:T(8,128)(2,1)} %get-tuple-element.18), channel_id=1, source_target_pairs={{0,8},{2,10},{1,9},{3,11},{4,12},{6,14},{5,13},{7,15},{8,0},{10,2}... | collective-permute-start | bytes 983048 | tf_op jit(solution)/shard_map/ppermute | solution.py:44
  11.5 0.0 collective-permute-start.3
  11.5 1.2 %collective-permute-start.4 = (bf16[80,2048]{1,0:T(8,128)(2,1)}, bf16[80,2048]{1,0:T(8,128)(2,1)S(1)}, u32[]{:S(2)}, u32[]{:S(2)}) collective-permute-start(bf16[80,2048]{1,0:T(8,128)(2,1)} %get-tuple-element.18), channel_id=1, source_target_pairs={{0,2},{2,1},{1,3},{3,0},{4,6},{6,5},{5,7},{7,4},{8,10},{10,9},{9,1... | collective-permute-start | bytes 983048 | tf_op jit(solution)/shard_map/ppermute | solution.py:44
  12.8 1.5 %collective-permute-start.5 = (bf16[80,2048]{1,0:T(8,128)(2,1)}, bf16[80,2048]{1,0:T(8,128)(2,1)S(1)}, u32[]{:S(2)}, u32[]{:S(2)}) collective-permute-start(bf16[80,2048]{1,0:T(8,128)(2,1)} %get-tuple-element.19), channel_id=1, source_target_pairs={{0,3},{2,0},{1,2},{3,1},{4,7},{6,4},{5,6},{7,5},{8,11},{10,8},{9,1... | collective-permute-start | bytes 983048 | tf_op jit(solution)/shard_map/ppermute | solution.py:44
  14.2 1.7 %collective-permute-start.10 = (bf16[64,4096]{1,0:T(8,128)(2,1)}, bf16[64,4096]{1,0:T(8,128)(2,1)S(1)}, u32[]{:S(2)}, u32[]{:S(2)}) collective-permute-start(bf16[64,4096]{1,0:T(8,128)(2,1)} %refs_11_.1), channel_id=1, source_target_pairs={{0,16},{2,18},{1,17},{3,19},{4,20},{6,22},{5,21},{7,23},{8,24},{10... | collective-permute-start | bytes 1572872 | tf_op jit(solution)/shard_map/ppermute | solution.py:44
  15.9 3.0 %collective-permute-done.2.refs_3_ = bf16[80,2048]{1,0:T(8,128)(2,1)S(1)} collective-permute-done((bf16[80,2048]{1,0:T(8,128)(2,1)}, bf16[80,2048]{1,0:T(8,128)(2,1)S(1)}, u32[]{:S(2)}, u32[]{:S(2)}) %collective-permute-start.2) | collective-permute-done | bytes 327712 | tf_op jit(solution)/shard_map/ppermute | solution.py:44
  18.9 3.6 %collective-permute-start.11 = (bf16[64,4096]{1,0:T(8,128)(2,1)}, bf16[64,4096]{1,0:T(8,128)(2,1)S(1)}, u32[]{:S(2)}, u32[]{:S(2)}) collective-permute-start(bf16[64,4096]{1,0:T(8,128)(2,1)} %refs_11_.1), channel_id=1, source_target_pairs={{0,32},{2,34},{1,33},{3,35},{4,36},{6,38},{5,37},{7,39},{8,40},{10... | collective-permute-start | bytes 1572872 | tf_op jit(solution)/shard_map/ppermute | solution.py:44
  22.5 3.4 %collective-permute-done.3.refs_4_ = bf16[80,2048]{1,0:T(8,128)(2,1)S(1)} collective-permute-done((bf16[80,2048]{1,0:T(8,128)(2,1)}, bf16[80,2048]{1,0:T(8,128)(2,1)S(1)}, u32[]{:S(2)}, u32[]{:S(2)}) %collective-permute-start.3) | collective-permute-done | bytes 327712 | tf_op jit(solution)/shard_map/ppermute | solution.py:44
  25.9 3.8 %collective-permute-start.12 = (bf16[64,4096]{1,0:T(8,128)(2,1)}, bf16[64,4096]{1,0:T(8,128)(2,1)S(1)}, u32[]{:S(2)}, u32[]{:S(2)}) collective-permute-start(bf16[64,4096]{1,0:T(8,128)(2,1)} %refs_11_.1), channel_id=1, source_target_pairs={{0,48},{2,50},{1,49},{3,51},{4,52},{6,54},{5,53},{7,55},{8,56},{10... | collective-permute-start | bytes 1572872 | tf_op jit(solution)/shard_map/ppermute | solution.py:44
  29.7 0.0 collective-permute-done.4.refs_5_
  29.7 0.7 copy-done.2
  30.4 1.3 %collective-permute-start = (bf16[80,4096]{1,0:T(8,128)(2,1)}, bf16[80,4096]{1,0:T(8,128)(2,1)}, u32[]{:S(2)}, u32[]{:S(2)}) collective-permute-start(bf16[80,4096]{1,0:T(8,128)(2,1)} %get-tuple-element.17.refs_0_), channel_id=1, source_target_pairs={{0,4},{2,6},{1,5},{3,7},{4,8},{6,10},{5,9},{7,11},{8,12},{10,14},{... | collective-permute-start | bytes 1966088 | tf_op jit(solution)/shard_map/ppermute | solution.py:44
  31.7 0.0 collective-permute-done.5.refs_6_
  31.7 0.7 copy-done.4
  32.4 1.4 %collective-permute-start.1 = (bf16[80,4096]{1,0:T(8,128)(2,1)}, bf16[80,4096]{1,0:T(8,128)(2,1)}, u32[]{:S(2)}, u32[]{:S(2)}) collective-permute-start(bf16[80,4096]{1,0:T(8,128)(2,1)} %get-tuple-element.17.refs_0_), channel_id=1, source_target_pairs={{0,12},{2,14},{1,13},{3,15},{4,0},{6,2},{5,1},{7,3},{8,4},{10,6},{... | collective-permute-start | bytes 1966088 | tf_op jit(solution)/shard_map/ppermute | solution.py:44
  33.9 0.8 dynamic-slice_convert_fusion
  34.6 0.0 collective-permute-done.10.refs_12_
  34.6 2.4 %collective-permute-start.13 = (bf16[64,4096]{1,0:T(8,128)(2,1)}, bf16[64,4096]{1,0:T(8,128)(2,1)S(1)}, u32[]{:S(2)}, u32[]{:S(2)}) collective-permute-start(bf16[64,4096]{1,0:T(8,128)(2,1)} %refs_11_.1), channel_id=1, source_target_pairs={{0,64},{2,66},{1,65},{3,67},{4,68},{6,70},{5,69},{7,71},{8,72},{10... | collective-permute-start | bytes 1572872 | tf_op jit(solution)/shard_map/ppermute | solution.py:44
  37.0 0.6 gather_fusion
  37.7 3.1 %collective-permute-done.11.refs_13_ = bf16[64,4096]{1,0:T(8,128)(2,1)S(1)} collective-permute-done((bf16[64,4096]{1,0:T(8,128)(2,1)}, bf16[64,4096]{1,0:T(8,128)(2,1)S(1)}, u32[]{:S(2)}, u32[]{:S(2)}) %collective-permute-start.11) | collective-permute-done | bytes 524320 | tf_op jit(solution)/shard_map/ppermute | solution.py:44
  40.8 0.0 collective-permute-start.8
  40.8 5.0 %collective-permute-done.12.refs_14_ = bf16[64,4096]{1,0:T(8,128)(2,1)S(1)} collective-permute-done((bf16[64,4096]{1,0:T(8,128)(2,1)}, bf16[64,4096]{1,0:T(8,128)(2,1)S(1)}, u32[]{:S(2)}, u32[]{:S(2)}) %collective-permute-start.12) | collective-permute-done | bytes 524320 | tf_op jit(solution)/shard_map/ppermute | solution.py:44
  45.8 2.5 %collective-permute-start.9 = (bf16[80,2048]{1,0:T(8,128)(2,1)S(1)}, bf16[80,2048]{1,0:T(8,128)(2,1)}, u32[]{:S(2)}, u32[]{:S(2)}) collective-permute-start(bf16[80,2048]{1,0:T(8,128)(2,1)S(1)} %collective-permute-done.3.refs_4_), channel_id=1, source_target_pairs={{0,3},{2,0},{1,2},{3,1},{4,7},{6,4},{5,6},{7,5},{8,11},{10,8},{9,1... | collective-permute-start | bytes 983048 | tf_op jit(solution)/shard_map/ppermute | solution.py:44
  48.3 0.0 collective-permute-done.refs_1_
  48.3 0.1 collective-permute-start.6
  48.4 0.0 collective-permute-done.1.refs_2_
  48.4 2.7 %collective-permute-start.7 = (bf16[80,4096]{1,0:T(8,128)(2,1)}, bf16[80,4096]{1,0:T(8,128)(2,1)}, u32[]{:S(2)}, u32[]{:S(2)}) collective-permute-start(bf16[80,4096]{1,0:T(8,128)(2,1)} %collective-permute-done.1.refs_2_), channel_id=1, source_target_pairs={{0,3},{2,0},{1,2},{3,1},{4,7},{6,4},{5,6},{7,5},{8,11},{10,8},{9,1... | collective-permute-start | bytes 1966088 | tf_op jit(solution)/shard_map/ppermute | solution.py:44
  51.0 1.3 %gather_fusion.1 = s32[4]{0:T(128)S(1)} fusion(s32[256]{0:T(256)} %param.12, s32[1024]{0:T(1024)S(1)} %pad_clamp_fusion), kind=kCustom, calls=%fused_computation.1.clone | custom fusion | bytes 48 | tf_op jit(solution)/shard_map/jit(_take)/gather | solution.py:259
  52.4 0.0 collective-permute-done.13.refs_15_
  52.4 2.6 %collective-permute-start.14 = (bf16[64,4096]{1,0:T(8,128)(2,1)S(1)}, bf16[64,4096]{1,0:T(8,128)(2,1)S(1)}, u32[]{:S(2)}, u32[]{:S(2)}) collective-permute-start(bf16[64,4096]{1,0:T(8,128)(2,1)S(1)} %collective-permute-done.10.refs_12_), channel_id=1, source_target_pairs={{0,64},{2,66},{1,65},{3,67},{4,68},{6,70},{5,69},{7,71},{8,72},{10... | collective-permute-start | bytes 1572872 | tf_op jit(solution)/shard_map/ppermute | solution.py:44
  55.0 0.1 collective-permute-start.15
  55.1 3.4 %collective-permute-start.16 = (bf16[64,4096]{1,0:T(8,128)(2,1)S(1)}, bf16[64,4096]{1,0:T(8,128)(2,1)}, u32[]{:S(2)}, u32[]{:S(2)}) collective-permute-start(bf16[64,4096]{1,0:T(8,128)(2,1)S(1)} %collective-permute-done.12.refs_14_), channel_id=1, source_target_pairs={{0,64},{2,66},{1,65},{3,67},{4,68},{6,70},{5,69},{7,71},{8,72},{10... | collective-permute-start | bytes 1572872 | tf_op jit(solution)/shard_map/ppermute | solution.py:44
  58.5 0.1 add_convert_fusion
  58.6 0.1 convert_element_type.12
  58.6 0.1 stack.71.at_ref
  58.8 1.4 %collective-permute-done.16.refs_18_ = bf16[64,4096]{1,0:T(8,128)(2,1)} collective-permute-done((bf16[64,4096]{1,0:T(8,128)(2,1)S(1)}, bf16[64,4096]{1,0:T(8,128)(2,1)}, u32[]{:S(2)}, u32[]{:S(2)}) %collective-permute-start.16) | collective-permute-done | bytes 524320 | tf_op jit(solution)/shard_map/ppermute | solution.py:44
  60.1 4.0 %collective-permute-done.6.refs_7_ = bf16[80,4096]{1,0:T(8,128)(2,1)} collective-permute-done((bf16[80,4096]{1,0:T(8,128)(2,1)}, bf16[80,4096]{1,0:T(8,128)(2,1)}, u32[]{:S(2)}, u32[]{:S(2)}) %collective-permute-start.6) | collective-permute-done | bytes 655392 | tf_op jit(solution)/shard_map/ppermute | solution.py:44
  64.1 3.6 %collective-permute-done.7.refs_8_ = bf16[80,4096]{1,0:T(8,128)(2,1)} collective-permute-done((bf16[80,4096]{1,0:T(8,128)(2,1)}, bf16[80,4096]{1,0:T(8,128)(2,1)}, u32[]{:S(2)}, u32[]{:S(2)}) %collective-permute-start.7) | collective-permute-done | bytes 655392 | tf_op jit(solution)/shard_map/ppermute | solution.py:44
  67.7 1.0 copy-done.1
  68.7 1.0 copy-done.3
  69.7 1.0 copy-done.5
  70.7 16.3 %project.1 = (bf16[64,640]{1,0:T(8,128)(2,1)S(1)}, bf16[64,640]{1,0:T(8,128)(2,1)}, bf16[64,640]{1,0:T(8,128)(2,1)}, bf16[64,640]{1,0:T(8,128)(2,1)S(1)}, bf16[6...) custom-call(s32[8]{0:T(128)S(1)} %stack.71.at_ref, ...), custom_call_target="tpu_custom_call" | custom-call | tf_op jit(solution)/shard_map/project/pallas_call | solution.py:112
  87.0 0.6 copy-done.6
  87.6 0.6 copy-done.7
  88.2 0.6 copy-done.8
  88.8 4.2 %collective-permute-start.17 = (bf16[64,640]{1,0:T(8,128)(2,1)}, bf16[64,640]{1,0:T(8,128)(2,1)S(1)}, u32[]{:S(2)}, u32[]{:S(2)}) collective-permute-start(bf16[64,640]{1,0:T(8,128)(2,1)} %get-tuple-element.21), channel_id=1, source_target_pairs={{0,48},{2,50},{1,49},{3,51},{4,52},{6,54},{5,53},{7,55},{8,56},{10... | collective-permute-start | bytes 245768 | tf_op jit(solution)/shard_map/ppermute | solution.py:44
  93.1 0.6 collective-permute-start.18
  93.7 0.2 fusion
  93.9 0.1 stack.62.group_ref
  94.0 0.0 collective-permute-start.19
  94.0 2.3 %collective-permute-start.20 = (bf16[64,640]{1,0:T(8,128)(2,1)}, bf16[64,640]{1,0:T(8,128)(2,1)S(1)}, u32[]{:S(2)}, u32[]{:S(2)}) collective-permute-start(bf16[64,640]{1,0:T(8,128)(2,1)} %copy-done.7), channel_id=1, source_target_pairs={{0,64},{2,66},{1,65},{3,67},{4,68},{6,70},{5,69},{7,71},{8,72},{10... | collective-permute-start | bytes 245768 | tf_op jit(solution)/shard_map/ppermute | solution.py:44
  96.3 2.4 %collective-permute-start.21 = (bf16[64,640]{1,0:T(8,128)(2,1)}, bf16[64,640]{1,0:T(8,128)(2,1)S(1)}, u32[]{:S(2)}, u32[]{:S(2)}) collective-permute-start(bf16[64,640]{1,0:T(8,128)(2,1)} %copy-done.6), channel_id=1, source_target_pairs={{0,112},{2,114},{1,113},{3,115},{4,116},{6,118},{5,117},{7,119},{8... | collective-permute-start | bytes 245768 | tf_op jit(solution)/shard_map/ppermute | solution.py:44
  98.7 0.0 collective-permute-done.17.refs_1_
  98.7 2.0 %collective-permute-start.22 = (bf16[64,640]{1,0:T(8,128)(2,1)S(1)}, bf16[64,640]{1,0:T(8,128)(2,1)S(1)}, u32[]{:S(2)}, u32[]{:S(2)}) collective-permute-start(bf16[64,640]{1,0:T(8,128)(2,1)S(1)} %get-tuple-element.26), channel_id=1, source_target_pairs={{0,96},{2,98},{1,97},{3,99},{4,100},{6,102},{5,101},{7,103},{8,104... | collective-permute-start | bytes 245768 | tf_op jit(solution)/shard_map/ppermute | solution.py:44
  100.7 0.0 collective-permute-done.18.refs_2_
  100.7 0.0 collective-permute-start.23
  100.7 0.1 pad_maximum_fusion
  100.8 0.0 collective-permute-done.19.refs_3_
  100.8 0.9 collective-permute-done.21.refs_5_
  101.7 3.2 %collective-permute-done.22.refs_6_ = bf16[64,640]{1,0:T(8,128)(2,1)S(1)} collective-permute-done((bf16[64,640]{1,0:T(8,128)(2,1)S(1)}, bf16[64,640]{1,0:T(8,128)(2,1)S(1)}, u32[]{:S(2)}, u32[]{:S(2)}) %collective-permute-start.22) | collective-permute-done | bytes 81952 | tf_op jit(solution)/shard_map/ppermute | solution.py:44
  104.9 1.9 %collective-permute-done.23.refs_7_ = bf16[64,640]{1,0:T(8,128)(2,1)S(1)} collective-permute-done((bf16[64,640]{1,0:T(8,128)(2,1)S(1)}, bf16[64,640]{1,0:T(8,128)(2,1)S(1)}, u32[]{:S(2)}, u32[]{:S(2)}) %collective-permute-start.23) | collective-permute-done | bytes 81952 | tf_op jit(solution)/shard_map/ppermute | solution.py:44
  106.8 9.7 %attend.1 = bf16[64,4096]{1,0:T(8,128)(2,1)} custom-call(s32[8]{0:T(128)S(1)} %stack.62.group_ref, s32[4]{0:T(128)S(1)} %and_select_fusion.length_ref, f32[64,128]{1,0:T(8,128)S(1)} %get-tuple-element.31.cos_ref, f32[64,128]{1,0:T(8,128)S(1)} %get-tuple-element.32.sin_ref, bf16[64,640]{1,0:T(8,128)(2,1)S(1)} %get-tuple-element.20.refs_0_, ...), custom_call_target="tpu_custom_call" | custom-call | tf_op jit(solution)/shard_map/attend/pallas_call | solution.py:200
  (22 shorter events, 0.1 us)
Async XLA Ops:
  0.0 37.0 %copy-start = (s32[256]{0:T(256)S(1)}, s32[256]{0:T(256)}, u32[]{:S(2)}) copy-start(s32[256]{0:T(256)} %param.13) | copy-start | bytes 3076
  7.8 11.1 %collective-permute-start.2 = (bf16[80,2048]{1,0:T(8,128)(2,1)}, bf16[80,2048]{1,0:T(8,128)(2,1)S(1)}, u32[]{:S(2)}, u32[]{:S(2)}) collective-permute-start(bf16[80,2048]{1,0:T(8,128)(2,1)} %get-tuple-element.18), channel_id=1, source_target_pairs={{0,8},{2,10},{1,9},{3,11},{4,12},{6,14},{5,13},{7,15},{8,0},{10,2}... | collective-permute-start | bytes 983048 | tf_op jit(solution)/shard_map/ppermute | solution.py:44
  11.5 14.4 %collective-permute-start.3 = (bf16[80,2048]{1,0:T(8,128)(2,1)}, bf16[80,2048]{1,0:T(8,128)(2,1)S(1)}, u32[]{:S(2)}, u32[]{:S(2)}) collective-permute-start(bf16[80,2048]{1,0:T(8,128)(2,1)} %get-tuple-element.19), channel_id=1, source_target_pairs={{0,8},{2,10},{1,9},{3,11},{4,12},{6,14},{5,13},{7,15},{8,0},{10,2}... | collective-permute-start | bytes 983048 | tf_op jit(solution)/shard_map/ppermute | solution.py:44
  11.5 18.1 %collective-permute-start.4 = (bf16[80,2048]{1,0:T(8,128)(2,1)}, bf16[80,2048]{1,0:T(8,128)(2,1)S(1)}, u32[]{:S(2)}, u32[]{:S(2)}) collective-permute-start(bf16[80,2048]{1,0:T(8,128)(2,1)} %get-tuple-element.18), channel_id=1, source_target_pairs={{0,2},{2,1},{1,3},{3,0},{4,6},{6,5},{5,7},{7,4},{8,10},{10,9},{9,1... | collective-permute-start | bytes 983048 | tf_op jit(solution)/shard_map/ppermute | solution.py:44
  12.8 18.9 %collective-permute-start.5 = (bf16[80,2048]{1,0:T(8,128)(2,1)}, bf16[80,2048]{1,0:T(8,128)(2,1)S(1)}, u32[]{:S(2)}, u32[]{:S(2)}) collective-permute-start(bf16[80,2048]{1,0:T(8,128)(2,1)} %get-tuple-element.19), channel_id=1, source_target_pairs={{0,3},{2,0},{1,2},{3,1},{4,7},{6,4},{5,6},{7,5},{8,11},{10,8},{9,1... | collective-permute-start | bytes 983048 | tf_op jit(solution)/shard_map/ppermute | solution.py:44
  14.2 20.4 %collective-permute-start.10 = (bf16[64,4096]{1,0:T(8,128)(2,1)}, bf16[64,4096]{1,0:T(8,128)(2,1)S(1)}, u32[]{:S(2)}, u32[]{:S(2)}) collective-permute-start(bf16[64,4096]{1,0:T(8,128)(2,1)} %refs_11_.1), channel_id=1, source_target_pairs={{0,16},{2,18},{1,17},{3,19},{4,20},{6,22},{5,21},{7,23},{8,24},{10... | collective-permute-start | bytes 1572872 | tf_op jit(solution)/shard_map/ppermute | solution.py:44
  18.9 21.9 %collective-permute-start.11 = (bf16[64,4096]{1,0:T(8,128)(2,1)}, bf16[64,4096]{1,0:T(8,128)(2,1)S(1)}, u32[]{:S(2)}, u32[]{:S(2)}) collective-permute-start(bf16[64,4096]{1,0:T(8,128)(2,1)} %refs_11_.1), channel_id=1, source_target_pairs={{0,32},{2,34},{1,33},{3,35},{4,36},{6,38},{5,37},{7,39},{8,40},{10... | collective-permute-start | bytes 1572872 | tf_op jit(solution)/shard_map/ppermute | solution.py:44
  25.9 19.9 %collective-permute-start.12 = (bf16[64,4096]{1,0:T(8,128)(2,1)}, bf16[64,4096]{1,0:T(8,128)(2,1)S(1)}, u32[]{:S(2)}, u32[]{:S(2)}) collective-permute-start(bf16[64,4096]{1,0:T(8,128)(2,1)} %refs_11_.1), channel_id=1, source_target_pairs={{0,48},{2,50},{1,49},{3,51},{4,52},{6,54},{5,53},{7,55},{8,56},{10... | collective-permute-start | bytes 1572872 | tf_op jit(solution)/shard_map/ppermute | solution.py:44
  29.7 0.7 copy-start.2
  30.4 17.9 %collective-permute-start = (bf16[80,4096]{1,0:T(8,128)(2,1)}, bf16[80,4096]{1,0:T(8,128)(2,1)}, u32[]{:S(2)}, u32[]{:S(2)}) collective-permute-start(bf16[80,4096]{1,0:T(8,128)(2,1)} %get-tuple-element.17.refs_0_), channel_id=1, source_target_pairs={{0,4},{2,6},{1,5},{3,7},{4,8},{6,10},{5,9},{7,11},{8,12},{10,14},{... | collective-permute-start | bytes 1966088 | tf_op jit(solution)/shard_map/ppermute | solution.py:44
  31.7 0.7 copy-start.4
  32.4 15.9 %collective-permute-start.1 = (bf16[80,4096]{1,0:T(8,128)(2,1)}, bf16[80,4096]{1,0:T(8,128)(2,1)}, u32[]{:S(2)}, u32[]{:S(2)}) collective-permute-start(bf16[80,4096]{1,0:T(8,128)(2,1)} %get-tuple-element.17.refs_0_), channel_id=1, source_target_pairs={{0,12},{2,14},{1,13},{3,15},{4,0},{6,2},{5,1},{7,3},{8,4},{10,6},{... | collective-permute-start | bytes 1966088 | tf_op jit(solution)/shard_map/ppermute | solution.py:44
  34.6 17.7 %collective-permute-start.13 = (bf16[64,4096]{1,0:T(8,128)(2,1)}, bf16[64,4096]{1,0:T(8,128)(2,1)S(1)}, u32[]{:S(2)}, u32[]{:S(2)}) collective-permute-start(bf16[64,4096]{1,0:T(8,128)(2,1)} %refs_11_.1), channel_id=1, source_target_pairs={{0,64},{2,66},{1,65},{3,67},{4,68},{6,70},{5,69},{7,71},{8,72},{10... | collective-permute-start | bytes 1572872 | tf_op jit(solution)/shard_map/ppermute | solution.py:44
  40.8 14.2 %collective-permute-start.8 = (bf16[80,2048]{1,0:T(8,128)(2,1)S(1)}, bf16[80,2048]{1,0:T(8,128)(2,1)}, u32[]{:S(2)}, u32[]{:S(2)}) collective-permute-start(bf16[80,2048]{1,0:T(8,128)(2,1)S(1)} %collective-permute-done.2.refs_3_), channel_id=1, source_target_pairs={{0,2},{2,1},{1,3},{3,0},{4,6},{6,5},{5,7},{7,4},{8,10},{10,9},{9,1... | collective-permute-start | bytes 983048 | tf_op jit(solution)/shard_map/ppermute | solution.py:44
  45.8 9.3 %collective-permute-start.9 = (bf16[80,2048]{1,0:T(8,128)(2,1)S(1)}, bf16[80,2048]{1,0:T(8,128)(2,1)}, u32[]{:S(2)}, u32[]{:S(2)}) collective-permute-start(bf16[80,2048]{1,0:T(8,128)(2,1)S(1)} %collective-permute-done.3.refs_4_), channel_id=1, source_target_pairs={{0,3},{2,0},{1,2},{3,1},{4,7},{6,4},{5,6},{7,5},{8,11},{10,8},{9,1... | collective-permute-start | bytes 983048 | tf_op jit(solution)/shard_map/ppermute | solution.py:44
  48.3 15.8 %collective-permute-start.6 = (bf16[80,4096]{1,0:T(8,128)(2,1)}, bf16[80,4096]{1,0:T(8,128)(2,1)}, u32[]{:S(2)}, u32[]{:S(2)}) collective-permute-start(bf16[80,4096]{1,0:T(8,128)(2,1)} %collective-permute-done.refs_1_), channel_id=1, source_target_pairs={{0,2},{2,1},{1,3},{3,0},{4,6},{6,5},{5,7},{7,4},{8,10},{10,9},{9,1... | collective-permute-start | bytes 1966088 | tf_op jit(solution)/shard_map/ppermute | solution.py:44
  48.4 19.3 %collective-permute-start.7 = (bf16[80,4096]{1,0:T(8,128)(2,1)}, bf16[80,4096]{1,0:T(8,128)(2,1)}, u32[]{:S(2)}, u32[]{:S(2)}) collective-permute-start(bf16[80,4096]{1,0:T(8,128)(2,1)} %collective-permute-done.1.refs_2_), channel_id=1, source_target_pairs={{0,3},{2,0},{1,2},{3,1},{4,7},{6,4},{5,6},{7,5},{8,11},{10,8},{9,1... | collective-permute-start | bytes 1966088 | tf_op jit(solution)/shard_map/ppermute | solution.py:44
  52.4 6.4 %collective-permute-start.14 = (bf16[64,4096]{1,0:T(8,128)(2,1)S(1)}, bf16[64,4096]{1,0:T(8,128)(2,1)S(1)}, u32[]{:S(2)}, u32[]{:S(2)}) collective-permute-start(bf16[64,4096]{1,0:T(8,128)(2,1)S(1)} %collective-permute-done.10.refs_12_), channel_id=1, source_target_pairs={{0,64},{2,66},{1,65},{3,67},{4,68},{6,70},{5,69},{7,71},{8,72},{10... | collective-permute-start | bytes 1572872 | tf_op jit(solution)/shard_map/ppermute | solution.py:44
  55.0 3.7 %collective-permute-start.15 = (bf16[64,4096]{1,0:T(8,128)(2,1)S(1)}, bf16[64,4096]{1,0:T(8,128)(2,1)}, u32[]{:S(2)}, u32[]{:S(2)}) collective-permute-start(bf16[64,4096]{1,0:T(8,128)(2,1)S(1)} %collective-permute-done.11.refs_13_), channel_id=1, source_target_pairs={{0,64},{2,66},{1,65},{3,67},{4,68},{6,70},{5,69},{7,71},{8,72},{10... | collective-permute-start | bytes 1572872 | tf_op jit(solution)/shard_map/ppermute | solution.py:44
  55.1 5.0 %collective-permute-start.16 = (bf16[64,4096]{1,0:T(8,128)(2,1)S(1)}, bf16[64,4096]{1,0:T(8,128)(2,1)}, u32[]{:S(2)}, u32[]{:S(2)}) collective-permute-start(bf16[64,4096]{1,0:T(8,128)(2,1)S(1)} %collective-permute-done.12.refs_14_), channel_id=1, source_target_pairs={{0,64},{2,66},{1,65},{3,67},{4,68},{6,70},{5,69},{7,71},{8,72},{10... | collective-permute-start | bytes 1572872 | tf_op jit(solution)/shard_map/ppermute | solution.py:44
  67.7 1.0 copy-start.1
  68.7 1.0 copy-start.3
  69.7 1.0 copy-start.5
  86.9 0.6 copy-start.6
  87.6 0.6 copy-start.7
  88.2 0.6 copy-start.8
  88.8 9.8 %collective-permute-start.17 = (bf16[64,640]{1,0:T(8,128)(2,1)}, bf16[64,640]{1,0:T(8,128)(2,1)S(1)}, u32[]{:S(2)}, u32[]{:S(2)}) collective-permute-start(bf16[64,640]{1,0:T(8,128)(2,1)} %get-tuple-element.21), channel_id=1, source_target_pairs={{0,48},{2,50},{1,49},{3,51},{4,52},{6,54},{5,53},{7,55},{8,56},{10... | collective-permute-start | bytes 245768 | tf_op jit(solution)/shard_map/ppermute | solution.py:44
  93.1 7.6 %collective-permute-start.18 = (bf16[64,640]{1,0:T(8,128)(2,1)}, bf16[64,640]{1,0:T(8,128)(2,1)S(1)}, u32[]{:S(2)}, u32[]{:S(2)}) collective-permute-start(bf16[64,640]{1,0:T(8,128)(2,1)} %get-tuple-element.22), channel_id=1, source_target_pairs={{0,32},{2,34},{1,33},{3,35},{4,36},{6,38},{5,37},{7,39},{8,40},{10... | collective-permute-start | bytes 245768 | tf_op jit(solution)/shard_map/ppermute | solution.py:44
  94.0 6.8 %collective-permute-start.19 = (bf16[64,640]{1,0:T(8,128)(2,1)}, bf16[64,640]{1,0:T(8,128)(2,1)S(1)}, u32[]{:S(2)}, u32[]{:S(2)}) collective-permute-start(bf16[64,640]{1,0:T(8,128)(2,1)} %copy-done.8), channel_id=1, source_target_pairs={{0,16},{2,18},{1,17},{3,19},{4,20},{6,22},{5,21},{7,23},{8,24},{10... | collective-permute-start | bytes 245768 | tf_op jit(solution)/shard_map/ppermute | solution.py:44
  94.0 6.8 %collective-permute-start.20 = (bf16[64,640]{1,0:T(8,128)(2,1)}, bf16[64,640]{1,0:T(8,128)(2,1)S(1)}, u32[]{:S(2)}, u32[]{:S(2)}) collective-permute-start(bf16[64,640]{1,0:T(8,128)(2,1)} %copy-done.7), channel_id=1, source_target_pairs={{0,64},{2,66},{1,65},{3,67},{4,68},{6,70},{5,69},{7,71},{8,72},{10... | collective-permute-start | bytes 245768 | tf_op jit(solution)/shard_map/ppermute | solution.py:44
  96.3 5.4 %collective-permute-start.21 = (bf16[64,640]{1,0:T(8,128)(2,1)}, bf16[64,640]{1,0:T(8,128)(2,1)S(1)}, u32[]{:S(2)}, u32[]{:S(2)}) collective-permute-start(bf16[64,640]{1,0:T(8,128)(2,1)} %copy-done.6), channel_id=1, source_target_pairs={{0,112},{2,114},{1,113},{3,115},{4,116},{6,118},{5,117},{7,119},{8... | collective-permute-start | bytes 245768 | tf_op jit(solution)/shard_map/ppermute | solution.py:44
  98.7 6.2 %collective-permute-start.22 = (bf16[64,640]{1,0:T(8,128)(2,1)S(1)}, bf16[64,640]{1,0:T(8,128)(2,1)S(1)}, u32[]{:S(2)}, u32[]{:S(2)}) collective-permute-start(bf16[64,640]{1,0:T(8,128)(2,1)S(1)} %get-tuple-element.26), channel_id=1, source_target_pairs={{0,96},{2,98},{1,97},{3,99},{4,100},{6,102},{5,101},{7,103},{8,104... | collective-permute-start | bytes 245768 | tf_op jit(solution)/shard_map/ppermute | solution.py:44
  100.7 6.1 %collective-permute-start.23 = (bf16[64,640]{1,0:T(8,128)(2,1)S(1)}, bf16[64,640]{1,0:T(8,128)(2,1)S(1)}, u32[]{:S(2)}, u32[]{:S(2)}) collective-permute-start(bf16[64,640]{1,0:T(8,128)(2,1)S(1)} %get-tuple-element.27), channel_id=1, source_target_pairs={{0,80},{2,82},{1,81},{3,83},{4,84},{6,86},{5,85},{7,87},{8,88},{10... | collective-permute-start | bytes 245768 | tf_op jit(solution)/shard_map/ppermute | solution.py:44

commit v2 on v1

v2 whole, which is shorter than its diff:
```python
import functools

import jax
import jax.numpy as jnp
from jax import lax
from jax.experimental import pallas as pl
from jax.experimental.pallas import tpu as pltpu
from jax.sharding import Mesh, PartitionSpec as P

D = 4096
HD = 128
HQ = 32
KVH = 4
STRETCH = 16
CAP = 1024
GROUP = 8
SLOTS = 4
ROWS = SLOTS * STRETCH
COLS = 80
SHARDS = 8
WIDE = COLS * SHARDS
HEADS = WIDE // HD
HALF = D // 2
ROPE_THETA = 1000000.0
LOG2E = 1.4426950408889634
AXES = ("tp", "z", "y", "xl", "xh")
NEAR = 4 * ROWS
PROJECT_VMEM = 56 * 1024 * 1024
ATTEND_VMEM = 56 * 1024 * 1024
NT = (((1,), (1,)), ((), ()))


def device_index(t, z, y, x):
    x = x % 4
    return ((((t % 2) * 4 + z % 4) * 4 + y % 4) * 2 + x % 2) * 2 + x // 2


def shift(array, dt=0, dz=0, dy=0, dx=0):
    pairs = [
        (device_index(t, z, y, x), device_index(t + dt, z + dz, y + dy, x + dx))
        for t in range(2)
        for z in range(4)
        for y in range(4)
        for x in range(4)
    ]
    return lax.ppermute(array, AXES, pairs)


def project_kernel(where, at_ref, bias_ref, *refs):
    count = len(where)
    pieces = refs[:count]
    rows = refs[count : count + 2]
    out = refs[count + 2]
    tokens, weights, sem = refs[count + 3 :]
    copies = [[], []]
    for i, row in enumerate(rows):
        for half in range(2):
            span = pl.ds(half * HALF, HALF)
            copies[half].append(
                pltpu.make_async_copy(
                    row.at[:, span],
                    tokens.at[pl.ds(i * NEAR, NEAR), span],
                    sem.at[half * 20 + i],
                )
            )
    for i, (piece, (dy, side, *halves)) in enumerate(zip(pieces, where)):
        start = pl.multiple_of(at_ref[dy * 2 + side] * COLS, 16)
        for half in halves:
            span = pl.ds((half - halves[0]) * HALF, HALF)
            copies[half].append(
                pltpu.make_async_copy(
                    piece.at[:, span],
                    weights.at[pl.ds(start, COLS), pl.ds(half * HALF, HALF)],
                    sem.at[half * 20 + 2 + i],
                )
            )
    for half in range(2):
        for copy in copies[half]:
            copy.start()
    total = bias_ref[...]
    for half in range(2):
        for copy in copies[half]:
            copy.wait()
        span = pl.ds(half * HALF, HALF)
        total = total + lax.dot_general(
            tokens[:, span], weights[:, span], NT, preferred_element_type=jnp.float32
        )
    total = total.astype(jnp.bfloat16)
    mine = at_ref[8]
    out[pl.ds(mine * 4, 4)] = total[:NEAR].reshape(4, ROWS, WIDE)
    out[pl.ds((1 - mine) * 4, 4)] = total[NEAR:].reshape(4, ROWS, WIDE)


def project(places, bias, pieces, where, rows):
    return pl.pallas_call(
        functools.partial(project_kernel, where),
        in_specs=[
            pl.BlockSpec(memory_space=pltpu.SMEM),
            pl.BlockSpec(memory_space=pltpu.VMEM),
        ]
        + [pl.BlockSpec(memory_space=pltpu.HBM)] * (len(pieces) + 2),
        out_specs=pl.BlockSpec(memory_space=pltpu.VMEM),
        out_shape=jax.ShapeDtypeStruct((8, ROWS, WIDE), jnp.bfloat16),
        scratch_shapes=[
            pltpu.VMEM((2 * NEAR, D), jnp.bfloat16),
            pltpu.VMEM((WIDE, D), jnp.bfloat16),
            pltpu.SemaphoreType.DMA((40,)),
        ],
        compiler_params=pltpu.CompilerParams(vmem_limit_bytes=PROJECT_VMEM),
        name="project",
    )(places, bias, *pieces, *rows)


def attend_kernel(length_ref, cos_ref, sin_ref, qkv, cache_ref, out_ref):
    slot = pl.program_id(0)
    at = pl.ds(pl.multiple_of(slot * STRETCH, STRETCH), STRETCH)
    cosine = cos_ref[at, :]
    sine = sin_ref[at, :]
    length = length_ref[slot]

    def head(h):
        low = (h % HEADS) * HD
        return qkv[h // HEADS, at, low : low + HD]

    def rotated(h):
        u = head(h).astype(jnp.float32)
        return (u * cosine + pltpu.roll(u, HD // 2, 1) * sine).astype(jnp.bfloat16)

    scale = HD ** (-0.5) * LOG2E
    key_at = lax.broadcasted_iota(jnp.int32, (1, CAP), 1)
    hidden = jnp.where(key_at < length, 0.0, -jnp.inf)
    token = lax.broadcasted_iota(jnp.int32, (GROUP * STRETCH, STRETCH), 0) % STRETCH
    new_at = lax.broadcasted_iota(jnp.int32, (GROUP * STRETCH, STRETCH), 1)
    causal = new_at <= token
    for k in range(KVH):
        queries = jnp.concatenate(
            [rotated(k * GROUP + g) for g in range(GROUP)], axis=0
        )
        new_keys = rotated(HQ + k)
        new_values = head(HQ + KVH + k)
        keys = cache_ref[0, :, k * HD : (k + 1) * HD]
        values = cache_ref[0, :, (KVH + k) * HD : (KVH + k + 1) * HD]
        scores = (
            lax.dot_general(queries, keys, NT, preferred_element_type=jnp.float32)
            + hidden
        )
        new_scores = lax.dot_general(
            queries, new_keys, NT, preferred_element_type=jnp.float32
        )
        new_scores = jnp.where(causal, new_scores, -jnp.inf)
        top = jnp.maximum(
            jnp.max(scores, axis=1, keepdims=True),
            jnp.max(new_scores, axis=1, keepdims=True),
        )
        weights = jnp.exp2((scores - top) * scale)
        new_weights = jnp.exp2((new_scores - top) * scale)
        total = jnp.sum(weights, axis=1, keepdims=True) + jnp.sum(
            new_weights, axis=1, keepdims=True
        )
        mixed = jnp.dot(
            weights.astype(jnp.bfloat16), values, preferred_element_type=jnp.float32
        ) + jnp.dot(
            new_weights.astype(jnp.bfloat16),
            new_values,
            preferred_element_type=jnp.float32,
        )
        mixed = (mixed / total).astype(jnp.bfloat16)
        for g in range(GROUP):
            low = (k * GROUP + g) * HD
            out_ref[:, low : low + HD] = mixed[g * STRETCH : (g + 1) * STRETCH]


def attend(lengths, cosine, sine, qkv, cache):
    whole = lambda shape: pl.BlockSpec(shape, lambda j: (0,) * len(shape))
    return pl.pallas_call(
        attend_kernel,
        grid=(SLOTS,),
        in_specs=[
            pl.BlockSpec(memory_space=pltpu.SMEM),
            whole((ROWS, HD)),
            whole((ROWS, HD)),
            whole((8, ROWS, WIDE)),
            pl.BlockSpec((1, CAP, 2 * KVH * HD), lambda j: (j, 0, 0)),
        ],
        out_specs=pl.BlockSpec((STRETCH, HQ * HD), lambda j: (j, 0)),
        out_shape=jax.ShapeDtypeStruct((ROWS, HQ * HD), jnp.bfloat16),
        compiler_params=pltpu.CompilerParams(vmem_limit_bytes=ATTEND_VMEM),
        name="attend",
    )(lengths, cosine, sine, qkv, cache)


def on_device(tokens, weight, bias, cache, lengths, slot_stream):
    t = lax.axis_index("tp")
    z = lax.axis_index("z")
    y = lax.axis_index("y")
    xl = lax.axis_index("xl")
    group = t * 4 + z
    index = (group * 4 + y) * 2 + xl

    copies = jnp.broadcast_to(tokens[None], (4, ROWS, D)).reshape(NEAR, D)
    mine = lax.all_to_all(copies, "z", split_axis=0, concat_axis=0, tiled=True)

    own = weight.T
    one, three, own_side = shift(own, dy=1), shift(own, dy=3), shift(own, dx=1)
    one, three, own_side, own = lax.optimization_barrier((one, three, own_side, own))
    two, one_side, three_side = shift(own, dy=2), shift(one, dx=3), shift(three, dx=1)
    two, one_side, three_side, mine = lax.optimization_barrier(
        (two, one_side, three_side, mine)
    )
    rows = [mine, shift(mine, dt=1)]
    two_low, two_high = shift(two[:, :HALF], dx=1), shift(two[:, HALF:], dx=3)
    pieces = [own, one, three, two, own_side, one_side, three_side, two_low, two_high]
    where = [
        (0, 0, 0, 1),
        (1, 0, 0, 1),
        (3, 0, 0, 1),
        (2, 0, 0, 1),
        (0, 1, 0, 1),
        (1, 1, 0, 1),
        (3, 1, 0, 1),
        (2, 1, 0),
        (2, 1, 1),
    ]

    places = jnp.stack(
        [
            ((y - dy) % 4) * 2 + (xl if side == 0 else 1 - xl)
            for dy in range(4)
            for side in range(2)
        ]
        + [t]
    ).astype(jnp.int32)
    bias_cols = lax.dynamic_slice_in_dim(bias, group * WIDE, WIDE, 0)
    bias_cols = bias_cols.astype(jnp.float32)[None, :]

    my_slots = index * SLOTS + jnp.arange(SLOTS, dtype=jnp.int32)
    my_lengths = jnp.take(lengths, jnp.take(slot_stream, my_slots)).astype(jnp.int32)
    positions = (my_lengths[:, None] + jnp.arange(STRETCH, dtype=jnp.int32)).reshape(-1)
    frequency = ROPE_THETA ** (
        -(jnp.arange(HD // 2, dtype=jnp.float32) * 2.0) / HD
    )
    angles = positions.astype(jnp.float32)[:, None] * frequency[None, :]
    cosine, sine = jnp.cos(angles), jnp.sin(angles)
    cosine = jnp.concatenate([cosine, cosine], axis=1)
    sine = jnp.concatenate([-sine, sine], axis=1)

    parts = project(places, bias_cols, pieces, tuple(where), rows)
    qkv = lax.all_to_all(parts, ("tp", "z"), split_axis=0, concat_axis=0, tiled=True)
    return attend(my_lengths, cosine, sine, qkv, cache)


def solution(mesh):
    fine = Mesh(mesh.devices.reshape(2, 4, 4, 2, 2), AXES)
    part = ("xh", "tp", "z", "y", "xl")
    in_specs = (
        P(part, None),
        P(None, ("tp", "z", "y", "xl")),
        P(),
        P(part, None, None),
        P("xh"),
        P("xh"),
    )
    return jax.shard_map(
        on_device,
        mesh=fine,
        in_specs=in_specs,
        out_specs=P(part, None),
        check_vma=False,
    )
```

time: 117 us -> 98.9 us (0.85)
  starting transfers between devices: 43.4 us -> 24.7 us
  waiting for transfers between devices: 29.5 us -> 44.7 us
  Pallas kernels: 31.5 us -> 18.6 us
  local copies, waits for them, and re-layouts: 10.8 us -> 8.71 us
    ppermute x24 -> x9, starting transfers between devices: 43.4 us -> 13.5 us  [shift(): return lax.ppermute(array, AXES, pairs)]
    all_to_all x0 -> x2, starting transfers between devices: none -> 11.2 us  [the longest x1 5.99 us: on_device(): mine = lax.all_to_all(copies, 'z', split_axis=0, concat_axis=0, tiled=True)]
    all_to_all x0 -> x2, waiting for transfers between devices: none -> 9.69 us  [the longest x1 9.69 us: on_device(): lax.all_to_all(parts, ('tp', 'z'), split_axis=0, concat_axis=0, tiled=True)]
    pallas_call x1, Pallas kernels: 16.3 us -> 8.81 us  [project(): pl.pallas_call(functools.partial(project_kernel, where), in_specs=[pl.Blo...]
    unnamed x19 -> x24, local copies, waits for them, and re-layouts: 8.56 us -> 2.53 us
    pallas_call x1 -> x0, Pallas kernels: 5.53 us -> none  [turn(): pl.pallas_call(turn_kernel, grid=(steps,), in_specs=[pl.BlockSpec((block,...]
    ppermute x24 -> x9, waiting for transfers between devices: 29.5 us -> 35 us  [shift(): return lax.ppermute(array, AXES, pairs)]
    broadcast_in_dim x0 -> x1, local copies, waits for them, and re-layouts: none -> 2.64 us  [on_device(): copies = jnp.broadcast_to(tokens[None], (4, ROWS, D)).reshape(NEAR, D)]
  transfers between devices with their start and end apart: 24 -> 11, of which waited for: 10 -> 6; matrix products, arithmetic and copies ran while one was open for 3% -> 5% of each run, Pallas kernels for 0% -> 0%
where the time goes in v2:
time: 98.9 us; the launch traced here: 98.6 us
  waiting for transfers between devices  44.7 us (45%)
  starting transfers between devices  24.7 us (25%)
  Pallas kernels  18.6 us (19%)
  local copies, waits for them, and re-layouts  8.71 us (9%)
  other arithmetic  1.79 us (2%)
    ppermute x9, waiting for transfers between devices, shift(): return lax.ppermute(array, AXES, pairs)  35 us
    ppermute x9, starting transfers between devices, shift(): return lax.ppermute(array, AXES, pairs)  13.5 us
    pallas_call x1, Pallas kernels, attend(): pl.pallas_call(attend_kernel, grid=(SLOTS,), in_specs=[pl.BlockSpec(memor...  9.76 us
    all_to_all x1, waiting for transfers between devices, on_device(): lax.all_to_all(parts, ('tp', 'z'), split_axis=0, concat_axis=0, tiled=True)  9.69 us
    pallas_call x1, Pallas kernels, project(): pl.pallas_call(functools.partial(project_kernel, where), in_specs=[pl.Blo...  8.81 us
    all_to_all x1, starting transfers between devices, on_device(): mine = lax.all_to_all(copies, 'z', split_axis=0, concat_axis=0, tiled=True)  5.99 us
    all_to_all x1, starting transfers between devices, on_device(): lax.all_to_all(parts, ('tp', 'z'), split_axis=0, concat_axis=0, tiled=True)  5.2 us
    broadcast_in_dim x1, local copies, waits for them, and re-layouts, on_device(): copies = jnp.broadcast_to(tokens[None], (4, ROWS, D)).reshape(NEAR, D)  2.64 us
  transfers between devices with their start and end apart: 11, of which 6 were waited for; matrix products, arithmetic and copies ran while one was open for 5% of the time, Pallas kernels for 0%

profile of v2, /device:TPU:1, one launch (start us, length us, event | category | flops | bytes accessed | tf_op | source)
XLA Modules:
  0.0 98.6 jit_solution(18022119120110529657)
XLA Ops:
  0.0 0.0 copy-start
  0.0 2.6 %broadcast_in_dim.20 = bf16[4,64,4096]{2,1,0:T(8,128)(2,1)} broadcast(bf16[64,4096]{1,0:T(8,128)(2,1)} %param.8), dimensions={1,2} | broadcast | bytes 2621440 | tf_op jit(solution)/shard_map/broadcast_in_dim | solution.py:200
  2.6 0.0 copy-start.5
  2.6 0.0 copy-start.1
  2.6 6.0 %all-to-all-start = ((bf16[4,64,4096]{2,1,0:T(8,128)(2,1)}), bf16[4,64,4096]{2,1,0:T(8,128)(2,1)S(1)}, u32[]{:S(2)}, u32[]{:S(2)}) async-start(bf16[4,64,4096]{2,1,0:T(8,128)(2,1)} %broadcast_in_dim.20), calls=%async_computation | async-start | bytes 4194304 | tf_op jit(solution)/shard_map/all_to_all | solution.py:201
  8.6 0.0 copy-done.5
  8.6 1.3 %collective-permute-start = (bf16[80,4096]{1,0:T(8,128)(2,1)S(1)}, bf16[80,4096]{1,0:T(8,128)(2,1)S(1)}, u32[]{:S(2)}, u32[]{:S(2)}) collective-permute-start(bf16[80,4096]{1,0:T(8,128)(2,1)S(1)} %bitcast.14), channel_id=1, source_target_pairs={{0,4},{2,6},{1,5},{3,7},{4,8},{6,10},{5,9},{7,11},{8,12},{10,14},{... | collective-permute-start | bytes 1966088 | tf_op jit(solution)/shard_map/ppermute | solution.py:46
  9.9 1.5 %collective-permute-start.1 = (bf16[80,4096]{1,0:T(8,128)(2,1)S(1)}, bf16[80,4096]{1,0:T(8,128)(2,1)S(1)}, u32[]{:S(2)}, u32[]{:S(2)}) collective-permute-start(bf16[80,4096]{1,0:T(8,128)(2,1)S(1)} %bitcast.15), channel_id=1, source_target_pairs={{0,12},{2,14},{1,13},{3,15},{4,0},{6,2},{5,1},{7,3},{8,4},{10,6},{... | collective-permute-start | bytes 1966088 | tf_op jit(solution)/shard_map/ppermute | solution.py:46
  11.4 1.2 %collective-permute-start.2 = (bf16[80,4096]{1,0:T(8,128)(2,1)S(1)}, bf16[80,4096]{1,0:T(8,128)(2,1)}, u32[]{:S(2)}, u32[]{:S(2)}) collective-permute-start(bf16[80,4096]{1,0:T(8,128)(2,1)S(1)} %bitcast.16), channel_id=1, source_target_pairs={{0,2},{2,1},{1,3},{3,0},{4,6},{6,5},{5,7},{7,4},{8,10},{10,9},{9,1... | collective-permute-start | bytes 1966088 | tf_op jit(solution)/shard_map/ppermute | solution.py:46
  12.7 12.7 %collective-permute-done.refs_1_ = bf16[80,4096]{1,0:T(8,128)(2,1)S(1)} collective-permute-done((bf16[80,4096]{1,0:T(8,128)(2,1)S(1)}, bf16[80,4096]{1,0:T(8,128)(2,1)S(1)}, u32[]{:S(2)}, u32[]{:S(2)}) %collective-permute-start) | collective-permute-done | bytes 655392 | tf_op jit(solution)/shard_map/ppermute | solution.py:46
  25.4 0.0 copy-start.6
  25.4 0.0 collective-permute-done.1.refs_2_
  25.4 0.0 copy-start.7
  25.4 2.2 %collective-permute-done.2.refs_4_ = bf16[80,4096]{1,0:T(8,128)(2,1)} collective-permute-done((bf16[80,4096]{1,0:T(8,128)(2,1)S(1)}, bf16[80,4096]{1,0:T(8,128)(2,1)}, u32[]{:S(2)}, u32[]{:S(2)}) %collective-permute-start.2) | collective-permute-done | bytes 655392 | tf_op jit(solution)/shard_map/ppermute | solution.py:46
  27.6 1.4 %collective-permute-start.3 = (bf16[80,4096]{1,0:T(8,128)(2,1)S(1)}, bf16[80,4096]{1,0:T(8,128)(2,1)S(1)}, u32[]{:S(2)}, u32[]{:S(2)}) collective-permute-start(bf16[80,4096]{1,0:T(8,128)(2,1)S(1)} %bitcast.17), channel_id=1, source_target_pairs={{0,8},{2,10},{1,9},{3,11},{4,12},{6,14},{5,13},{7,15},{8,0},{10,2}... | collective-permute-start | bytes 1966088 | tf_op jit(solution)/shard_map/ppermute | solution.py:46
  29.0 1.3 %collective-permute-start.4 = (bf16[80,4096]{1,0:T(8,128)(2,1)S(1)}, bf16[80,4096]{1,0:T(8,128)(2,1)S(1)}, u32[]{:S(2)}, u32[]{:S(2)}) collective-permute-start(bf16[80,4096]{1,0:T(8,128)(2,1)S(1)} %collective-permute-done.refs_1_), channel_id=1, source_target_pairs={{0,3},{2,0},{1,2},{3,1},{4,7},{6,4},{5,6},{7,5},{8,11},{10,8},{9,1... | collective-permute-start | bytes 1966088 | tf_op jit(solution)/shard_map/ppermute | solution.py:46
  30.3 0.2 collective-permute-start.5
  30.5 12.5 %collective-permute-done.3.refs_3_ = bf16[80,4096]{1,0:T(8,128)(2,1)S(1)} collective-permute-done((bf16[80,4096]{1,0:T(8,128)(2,1)S(1)}, bf16[80,4096]{1,0:T(8,128)(2,1)S(1)}, u32[]{:S(2)}, u32[]{:S(2)}) %collective-permute-start.3) | collective-permute-done | bytes 655392 | tf_op jit(solution)/shard_map/ppermute | solution.py:46
  43.0 0.0 copy-start.3
  43.0 0.0 collective-permute-done.4.refs_5_
  43.0 0.0 copy-done.6
  43.0 0.0 copy-done.7
  43.1 0.0 copy-start.8
  43.1 0.9 copy-done.8
  43.9 0.9 collective-permute-done.5.refs_6_
  44.9 0.0 all-to-all-done
  44.9 0.0 copy-start.2
  44.9 3.9 %collective-permute-start.8 = (bf16[256,4096]{1,0:T(8,128)(2,1)S(1)}, bf16[256,4096]{1,0:T(8,128)(2,1)}, u32[]{:S(2)}, u32[]{:S(2)}) collective-permute-start(bf16[256,4096]{1,0:T(8,128)(2,1)S(1)} %bitcast.11), channel_id=1, source_target_pairs={{0,64},{2,66},{1,65},{3,67},{4,68},{6,70},{5,69},{7,71},{8,72},{10... | collective-permute-start | bytes 6291464 | tf_op jit(solution)/shard_map/ppermute | solution.py:46
  48.8 0.8 dynamic-slice_convert_fusion
  49.5 0.6 reshape.33.bias_ref
  50.2 0.0 copy-done
  50.2 0.6 gather_fusion
  50.8 0.9 fusion.1
  51.7 0.0 collective-permute-start.6
  51.7 2.7 %collective-permute-start.7 = (bf16[80,2048]{1,0:T(8,128)(2,1)}, bf16[80,2048]{1,0:T(8,128)(2,1)S(1)}, u32[]{:S(2)}, u32[]{:S(2)}) collective-permute-start(bf16[80,2048]{1,0:T(8,128)(2,1)} %get-tuple-element.22), channel_id=1, source_target_pairs={{0,3},{2,0},{1,2},{3,1},{4,7},{6,4},{5,6},{7,5},{8,11},{10,8},{9,1... | collective-permute-start | bytes 983048 | tf_op jit(solution)/shard_map/ppermute | solution.py:46
  54.4 0.0 copy-done.1
  54.4 0.6 gather_fusion.1
  55.1 0.7 stack.39.at_ref
  55.7 0.0 copy-start.11
  55.7 6.6 %collective-permute-done.6.refs_7_ = bf16[80,2048]{1,0:T(8,128)(2,1)S(1)} collective-permute-done((bf16[80,2048]{1,0:T(8,128)(2,1)}, bf16[80,2048]{1,0:T(8,128)(2,1)S(1)}, u32[]{:S(2)}, u32[]{:S(2)}) %collective-permute-start.6) | collective-permute-done | bytes 327712 | tf_op jit(solution)/shard_map/ppermute | solution.py:46
  62.3 0.0 copy-start.9
  62.3 0.0 collective-permute-done.7.refs_8_
  62.3 0.0 copy-start.10
  62.3 0.0 collective-permute-done.8.refs_10_
  62.3 0.0 copy-done.3
  62.4 0.0 copy-done.2
  62.4 0.7 copy-done.9
  63.1 0.1 copy-done.10
  63.2 8.8 %project.1 = bf16[8,64,640]{2,1,0:T(8,128)(2,1)} custom-call(s32[9]{0:T(128)} %stack.39.at_ref, f32[1,640]{1,0:T(1,128)} %reshape.33.bias_ref, bf16[80,4096]{1,0:T(8,128)(2,1)} %bitcast.13, bf16[80,4096]{1,0:T(8,128)(2,1)} %copy-done.6, bf16[80,4096]{1,0:T(8,128)(2,1)} %copy-done.7, bf16[80,4096]{1,0:T(8,128)(2,1)} %copy-done.3, ...), custom_call_target="tpu_custom_call" | custom-call | tf_op jit(solution)/shard_map/project/pallas_call | solution.py:95
  72.0 5.2 %all-to-all-start.1 = ((bf16[8,64,640]{2,1,0:T(8,128)(2,1)}), bf16[8,64,640]{2,1,0:T(8,128)(2,1)S(1)}, u32[]{:S(2)}, u32[]{:S(2)}) async-start(bf16[8,64,640]{2,1,0:T(8,128)(2,1)} %project.1), calls=%async_computation.1 | async-start | bytes 1310720 | tf_op jit(solution)/shard_map/all_to_all | solution.py:248
  77.2 0.1 add_convert_fusion
  77.3 0.1 convert_element_type.12
  77.3 0.2 fusion
  77.6 0.7 pad_maximum_fusion
  78.3 9.7 %all-to-all-done.1.qkv = bf16[8,64,640]{2,1,0:T(8,128)(2,1)S(1)} async-done(((bf16[8,64,640]{2,1,0:T(8,128)(2,1)}), bf16[8,64,640]{2,1,0:T(8,128)(2,1)S(1)}, u32[]{:S(2)}, u32[]{:S(2)}) %all-to-all-start.1) | async-done | bytes 655392 | tf_op jit(solution)/shard_map/all_to_all | solution.py:248
  88.0 0.0 copy-start.4
  88.0 0.0 copy-done.11
  88.0 0.8 copy-done.4
  88.8 9.8 %attend.1 = bf16[64,4096]{1,0:T(8,128)(2,1)} custom-call(s32[4]{0:T(128)} %copy-done.11, f32[64,128]{1,0:T(8,128)} %get-tuple-element.27.cos_ref, f32[64,128]{1,0:T(8,128)} %get-tuple-element.28.sin_ref, bf16[8,64,640]{2,1,0:T(8,128)(2,1)} %copy-done.4, bf16[4,1024,1024]{2,1,0:T(8,128)(2,1)} %cache_ref.1), custom_call_target="tpu_custom_call" | custom-call | tf_op jit(solution)/shard_map/attend/pallas_call | solution.py:175
  (6 shorter events, 0.0 us)
Async XLA Ops:
  0.0 50.2 %copy-start = (s32[256]{0:T(256)S(1)}, s32[256]{0:T(256)}, u32[]{:S(2)}) copy-start(s32[256]{0:T(256)} %param.13) | copy-start | bytes 3076
  2.6 6.0 %copy-start.5 = (bf16[4096,80]{0,1:T(8,128)(2,1)S(1)}, bf16[4096,80]{0,1:T(8,128)(2,1)}, u32[]{:S(2)}) copy-start(bf16[4096,80]{0,1:T(8,128)(2,1)} %param.9) | copy-start | bytes 1966084
  2.6 51.8 %copy-start.1 = (s32[256]{0:T(256)S(1)}, s32[256]{0:T(256)}, u32[]{:S(2)}) copy-start(s32[256]{0:T(256)} %param.12) | copy-start | bytes 3076
  2.6 42.2 %all-to-all-start = ((bf16[4,64,4096]{2,1,0:T(8,128)(2,1)}), bf16[4,64,4096]{2,1,0:T(8,128)(2,1)S(1)}, u32[]{:S(2)}, u32[]{:S(2)}) async-start(bf16[4,64,4096]{2,1,0:T(8,128)(2,1)} %broadcast_in_dim.20), calls=%async_computation | async-start | bytes 4194304 | tf_op jit(solution)/shard_map/all_to_all | solution.py:201
  8.6 16.7 %collective-permute-start = (bf16[80,4096]{1,0:T(8,128)(2,1)S(1)}, bf16[80,4096]{1,0:T(8,128)(2,1)S(1)}, u32[]{:S(2)}, u32[]{:S(2)}) collective-permute-start(bf16[80,4096]{1,0:T(8,128)(2,1)S(1)} %bitcast.14), channel_id=1, source_target_pairs={{0,4},{2,6},{1,5},{3,7},{4,8},{6,10},{5,9},{7,11},{8,12},{10,14},{... | collective-permute-start | bytes 1966088 | tf_op jit(solution)/shard_map/ppermute | solution.py:46
  9.9 15.4 %collective-permute-start.1 = (bf16[80,4096]{1,0:T(8,128)(2,1)S(1)}, bf16[80,4096]{1,0:T(8,128)(2,1)S(1)}, u32[]{:S(2)}, u32[]{:S(2)}) collective-permute-start(bf16[80,4096]{1,0:T(8,128)(2,1)S(1)} %bitcast.15), channel_id=1, source_target_pairs={{0,12},{2,14},{1,13},{3,15},{4,0},{6,2},{5,1},{7,3},{8,4},{10,6},{... | collective-permute-start | bytes 1966088 | tf_op jit(solution)/shard_map/ppermute | solution.py:46
  11.4 16.2 %collective-permute-start.2 = (bf16[80,4096]{1,0:T(8,128)(2,1)S(1)}, bf16[80,4096]{1,0:T(8,128)(2,1)}, u32[]{:S(2)}, u32[]{:S(2)}) collective-permute-start(bf16[80,4096]{1,0:T(8,128)(2,1)S(1)} %bitcast.16), channel_id=1, source_target_pairs={{0,2},{2,1},{1,3},{3,0},{4,6},{6,5},{5,7},{7,4},{8,10},{10,9},{9,1... | collective-permute-start | bytes 1966088 | tf_op jit(solution)/shard_map/ppermute | solution.py:46
  25.4 17.7 %copy-start.6 = (bf16[80,4096]{1,0:T(8,128)(2,1)}, bf16[80,4096]{1,0:T(8,128)(2,1)S(1)}, u32[]{:S(2)}) copy-start(bf16[80,4096]{1,0:T(8,128)(2,1)S(1)} %collective-permute-done.refs_1_) | copy-start | bytes 1966084
  25.4 17.7 %copy-start.7 = (bf16[80,4096]{1,0:T(8,128)(2,1)}, bf16[80,4096]{1,0:T(8,128)(2,1)S(1)}, u32[]{:S(2)}) copy-start(bf16[80,4096]{1,0:T(8,128)(2,1)S(1)} %collective-permute-done.1.refs_2_) | copy-start | bytes 1966084
  27.6 15.4 %collective-permute-start.3 = (bf16[80,4096]{1,0:T(8,128)(2,1)S(1)}, bf16[80,4096]{1,0:T(8,128)(2,1)S(1)}, u32[]{:S(2)}, u32[]{:S(2)}) collective-permute-start(bf16[80,4096]{1,0:T(8,128)(2,1)S(1)} %bitcast.17), channel_id=1, source_target_pairs={{0,8},{2,10},{1,9},{3,11},{4,12},{6,14},{5,13},{7,15},{8,0},{10,2}... | collective-permute-start | bytes 1966088 | tf_op jit(solution)/shard_map/ppermute | solution.py:46
  29.0 14.0 %collective-permute-start.4 = (bf16[80,4096]{1,0:T(8,128)(2,1)S(1)}, bf16[80,4096]{1,0:T(8,128)(2,1)S(1)}, u32[]{:S(2)}, u32[]{:S(2)}) collective-permute-start(bf16[80,4096]{1,0:T(8,128)(2,1)S(1)} %collective-permute-done.refs_1_), channel_id=1, source_target_pairs={{0,3},{2,0},{1,2},{3,1},{4,7},{6,4},{5,6},{7,5},{8,11},{10,8},{9,1... | collective-permute-start | bytes 1966088 | tf_op jit(solution)/shard_map/ppermute | solution.py:46
  30.3 14.5 %collective-permute-start.5 = (bf16[80,4096]{1,0:T(8,128)(2,1)S(1)}, bf16[80,4096]{1,0:T(8,128)(2,1)}, u32[]{:S(2)}, u32[]{:S(2)}) collective-permute-start(bf16[80,4096]{1,0:T(8,128)(2,1)S(1)} %collective-permute-done.1.refs_2_), channel_id=1, source_target_pairs={{0,2},{2,1},{1,3},{3,0},{4,6},{6,5},{5,7},{7,4},{8,10},{10,9},{9,1... | collective-permute-start | bytes 1966088 | tf_op jit(solution)/shard_map/ppermute | solution.py:46
  43.0 19.3 %copy-start.3 = (bf16[80,4096]{1,0:T(8,128)(2,1)}, bf16[80,4096]{1,0:T(8,128)(2,1)S(1)}, u32[]{:S(2)}) copy-start(bf16[80,4096]{1,0:T(8,128)(2,1)S(1)} %collective-permute-done.3.refs_3_) | copy-start | bytes 1966084
  43.1 0.9 copy-start.8
  44.9 17.5 %copy-start.2 = (bf16[4,64,4096]{2,1,0:T(8,128)(2,1)}, bf16[4,64,4096]{2,1,0:T(8,128)(2,1)S(1)}, u32[]{:S(2)}) copy-start(bf16[4,64,4096]{2,1,0:T(8,128)(2,1)S(1)} %all-to-all-done) | copy-start | bytes 6291460
  44.9 17.5 %collective-permute-start.8 = (bf16[256,4096]{1,0:T(8,128)(2,1)S(1)}, bf16[256,4096]{1,0:T(8,128)(2,1)}, u32[]{:S(2)}, u32[]{:S(2)}) collective-permute-start(bf16[256,4096]{1,0:T(8,128)(2,1)S(1)} %bitcast.11), channel_id=1, source_target_pairs={{0,64},{2,66},{1,65},{3,67},{4,68},{6,70},{5,69},{7,71},{8,72},{10... | collective-permute-start | bytes 6291464 | tf_op jit(solution)/shard_map/ppermute | solution.py:46
  51.7 10.6 %collective-permute-start.6 = (bf16[80,2048]{1,0:T(8,128)(2,1)}, bf16[80,2048]{1,0:T(8,128)(2,1)S(1)}, u32[]{:S(2)}, u32[]{:S(2)}) collective-permute-start(bf16[80,2048]{1,0:T(8,128)(2,1)} %get-tuple-element.23), channel_id=1, source_target_pairs={{0,2},{2,1},{1,3},{3,0},{4,6},{6,5},{5,7},{7,4},{8,10},{10,9},{9,1... | collective-permute-start | bytes 983048 | tf_op jit(solution)/shard_map/ppermute | solution.py:46
  51.7 10.6 %collective-permute-start.7 = (bf16[80,2048]{1,0:T(8,128)(2,1)}, bf16[80,2048]{1,0:T(8,128)(2,1)S(1)}, u32[]{:S(2)}, u32[]{:S(2)}) collective-permute-start(bf16[80,2048]{1,0:T(8,128)(2,1)} %get-tuple-element.22), channel_id=1, source_target_pairs={{0,3},{2,0},{1,2},{3,1},{4,7},{6,4},{5,6},{7,5},{8,11},{10,8},{9,1... | collective-permute-start | bytes 983048 | tf_op jit(solution)/shard_map/ppermute | solution.py:46
  55.7 32.2 %copy-start.11 = (s32[4]{0:T(128)}, s32[4]{0:T(128)S(1)}, u32[]{:S(2)}) copy-start(s32[4]{0:T(128)S(1)} %and_select_fusion.length_ref) | copy-start | bytes 52
  62.3 0.8 copy-start.9
  62.3 0.8 copy-start.10
  72.0 16.0 %all-to-all-start.1 = ((bf16[8,64,640]{2,1,0:T(8,128)(2,1)}), bf16[8,64,640]{2,1,0:T(8,128)(2,1)S(1)}, u32[]{:S(2)}, u32[]{:S(2)}) async-start(bf16[8,64,640]{2,1,0:T(8,128)(2,1)} %project.1), calls=%async_computation.1 | async-start | bytes 1310720 | tf_op jit(solution)/shard_map/all_to_all | solution.py:248
  88.0 0.8 copy-start.4

commit v3 on v2

--- a/solution.py
+++ b/solution.py
@@ -25,6 +25,7 @@
 LOG2E = 1.4426950408889634
 AXES = ("tp", "z", "y", "xl", "xh")
 NEAR = 4 * ROWS
+WINDOW = 256
 PROJECT_VMEM = 56 * 1024 * 1024
 ATTEND_VMEM = 56 * 1024 * 1024
 NT = (((1,), (1,)), ((), ()))
@@ -46,38 +47,28 @@
     return lax.ppermute(array, AXES, pairs)
 
 
-def project_kernel(where, at_ref, bias_ref, *refs):
-    count = len(where)
-    pieces = refs[:count]
-    rows = refs[count : count + 2]
-    out = refs[count + 2]
-    tokens, weights, sem = refs[count + 3 :]
+def load(near, other, pieces, where, at_ref, tokens, weights, sem):
     copies = [[], []]
-    for i, row in enumerate(rows):
-        for half in range(2):
-            span = pl.ds(half * HALF, HALF)
-            copies[half].append(
-                pltpu.make_async_copy(
-                    row.at[:, span],
-                    tokens.at[pl.ds(i * NEAR, NEAR), span],
-                    sem.at[half * 20 + i],
-                )
-            )
-    for i, (piece, (dy, side, *halves)) in enumerate(zip(pieces, where)):
-        start = pl.multiple_of(at_ref[dy * 2 + side] * COLS, 16)
-        for half in halves:
-            span = pl.ds((half - halves[0]) * HALF, HALF)
-            copies[half].append(
-                pltpu.make_async_copy(
-                    piece.at[:, span],
-                    weights.at[pl.ds(start, COLS), pl.ds(half * HALF, HALF)],
-                    sem.at[half * 20 + 2 + i],
-                )
-            )
+    count = 0
+    for half in range(2):
+        span = pl.ds(half * HALF, HALF)
+        moves = [(near.at[:, span], tokens.at[pl.ds(0, NEAR), span])]
+        moves.append((other.at[:, span], tokens.at[pl.ds(NEAR, NEAR), span]))
+        for piece, (place, *halves) in zip(pieces, where):
+            if half in halves:
+                start = pl.multiple_of(at_ref[place], 16)
+                source = piece.at[:, pl.ds((half - halves[0]) * HALF, HALF)]
+                moves.append((source, weights.at[pl.ds(start, COLS), span]))
+        for source, target in moves:
+            copies[half].append(pltpu.make_async_copy(source, target, sem.at[count]))
+            count += 1
     for half in range(2):
         for copy in copies[half]:
             copy.start()
-    total = bias_ref[...]
+    return copies
+
+
+def multiply(copies, tokens, weights, total):
     for half in range(2):
         for copy in copies[half]:
             copy.wait()
@@ -85,30 +76,75 @@
         total = total + lax.dot_general(
             tokens[:, span], weights[:, span], NT, preferred_element_type=jnp.float32
         )
-    total = total.astype(jnp.bfloat16)
-    mine = at_ref[8]
-    out[pl.ds(mine * 4, 4)] = total[:NEAR].reshape(4, ROWS, WIDE)
-    out[pl.ds((1 - mine) * 4, 4)] = total[NEAR:].reshape(4, ROWS, WIDE)
-
-
-def project(places, bias, pieces, where, rows):
+    return total
+
+
+def project_first_kernel(where, at_ref, bias_ref, near, other, *refs):
+    pieces = refs[:-4]
+    out, tokens, weights, sem = refs[-4:]
+    copies = load(near, other, pieces, where, at_ref, tokens, weights, sem)
+    start = pl.multiple_of(at_ref[16], 16)
+    weights[pl.ds(start, 2 * COLS), :] = jnp.zeros((2 * COLS, D), jnp.bfloat16)
+    out[...] = multiply(copies, tokens, weights, bias_ref[...])
+
+
+def project_last_kernel(where, at_ref, total_ref, near, other, *refs):
+    pieces = refs[:-4]
+    out, tokens, weights, sem = refs[-4:]
+    copies = load(near, other, pieces, where, at_ref, tokens, weights, sem)
+    shift_by = at_ref[17]
+    for k in range(4):
+
+        @pl.when(shift_by == 2 * k * STRETCH)
+        def _():
+            if k:
+                weights[: 2 * k * STRETCH, :] = jnp.zeros(
+                    (2 * k * STRETCH, D), jnp.bfloat16
+                )
+            rest = 2 * k * STRETCH + 2 * COLS
+            if rest < WINDOW:
+                weights[rest:, :] = jnp.zeros((WINDOW - rest, D), jnp.bfloat16)
+
+    total = multiply(copies, tokens, weights, jnp.zeros((1, WINDOW), jnp.float32))
+    for block in range(8):
+        out[at_ref[8 + block]] = total_ref[pl.ds(block * ROWS, ROWS), :].astype(
+            jnp.bfloat16
+        )
+    for k in range(4):
+
+        @pl.when(shift_by == 2 * k * STRETCH)
+        def _():
+            window = slice(k * HD, k * HD + WINDOW)
+            done = (total_ref[:, window] + total).astype(jnp.bfloat16)
+            for block in range(8):
+                out[at_ref[8 + block], :, window] = done[
+                    block * ROWS : (block + 1) * ROWS
+                ]
+
+
+def project(kernel, width, out_shape, places, whole, near, other, pieces, where):
     return pl.pallas_call(
-        functools.partial(project_kernel, where),
+        functools.partial(kernel, where),
         in_specs=[
             pl.BlockSpec(memory_space=pltpu.SMEM),
             pl.BlockSpec(memory_space=pltpu.VMEM),
         ]
         + [pl.BlockSpec(memory_space=pltpu.HBM)] * (len(pieces) + 2),
         out_specs=pl.BlockSpec(memory_space=pltpu.VMEM),
-        out_shape=jax.ShapeDtypeStruct((8, ROWS, WIDE), jnp.bfloat16),
+        out_shape=out_shape,
         scratch_shapes=[
             pltpu.VMEM((2 * NEAR, D), jnp.bfloat16),
-            pltpu.VMEM((WIDE, D), jnp.bfloat16),
-            pltpu.SemaphoreType.DMA((40,)),
+            pltpu.VMEM((width, D), jnp.bfloat16),
+            pltpu.SemaphoreType.DMA((20,)),
         ],
         compiler_params=pltpu.CompilerParams(vmem_limit_bytes=PROJECT_VMEM),
-        name="project",
-    )(places, bias, *pieces, *rows)
+        cost_estimate=pl.CostEstimate(
+            flops=4 * NEAR * width * D,
+            bytes_accessed=2 * D * (2 * NEAR + width),
+            transcendentals=0,
+        ),
+        name=kernel.__name__.removesuffix("_kernel"),
+    )(places, whole, near, other, *pieces)
 
 
 def attend_kernel(length_ref, cos_ref, sin_ref, qkv, cache_ref, out_ref):
@@ -197,39 +233,15 @@
     group = t * 4 + z
     index = (group * 4 + y) * 2 + xl
 
-    copies = jnp.broadcast_to(tokens[None], (4, ROWS, D)).reshape(NEAR, D)
-    mine = lax.all_to_all(copies, "z", split_axis=0, concat_axis=0, tiled=True)
-
-    own = weight.T
-    one, three, own_side = shift(own, dy=1), shift(own, dy=3), shift(own, dx=1)
-    one, three, own_side, own = lax.optimization_barrier((one, three, own_side, own))
-    two, one_side, three_side = shift(own, dy=2), shift(one, dx=3), shift(three, dx=1)
-    two, one_side, three_side, mine = lax.optimization_barrier(
-        (two, one_side, three_side, mine)
-    )
-    rows = [mine, shift(mine, dt=1)]
-    two_low, two_high = shift(two[:, :HALF], dx=1), shift(two[:, HALF:], dx=3)
-    pieces = [own, one, three, two, own_side, one_side, three_side, two_low, two_high]
-    where = [
-        (0, 0, 0, 1),
-        (1, 0, 0, 1),
-        (3, 0, 0, 1),
-        (2, 0, 0, 1),
-        (0, 1, 0, 1),
-        (1, 1, 0, 1),
-        (3, 1, 0, 1),
-        (2, 1, 0),
-        (2, 1, 1),
-    ]
-
-    places = jnp.stack(
-        [
-            ((y - dy) % 4) * 2 + (xl if side == 0 else 1 - xl)
-            for dy in range(4)
-            for side in range(2)
-        ]
-        + [t]
-    ).astype(jnp.int32)
+    far_y = (y + 2) % 4
+    places = []
+    for dy in range(4):
+        base = far_y * 2 * STRETCH if dy == 2 else (y - dy) % 4 * 2 * COLS
+        places += [base + xl * COLS, base + (1 - xl) * COLS]
+    for core in (t, 1 - t):
+        places += [core * 4 + (z - dz) % 4 for dz in (0, 1, 3, 2)]
+    places += [far_y * 2 * COLS, far_y * 2 * STRETCH]
+    places = jnp.stack(places).astype(jnp.int32)
     bias_cols = lax.dynamic_slice_in_dim(bias, group * WIDE, WIDE, 0)
     bias_cols = bias_cols.astype(jnp.float32)[None, :]
 
@@ -244,7 +256,46 @@
     cosine = jnp.concatenate([cosine, cosine], axis=1)
     sine = jnp.concatenate([-sine, sine], axis=1)
 
-    parts = project(places, bias_cols, pieces, tuple(where), rows)
+    own = weight.T
+    one, three, own_side = shift(own, dy=1), shift(own, dy=3), shift(own, dx=1)
+    up, down = shift(tokens, dz=1), shift(tokens, dz=3)
+    one, three, own_side, up, down, tokens, small = lax.optimization_barrier(
+        (one, three, own_side, up, down, tokens, (places, bias_cols, my_lengths, cosine, sine))
+    )
+    places, bias_cols, my_lengths, cosine, sine = small
+    two_side = shift(own_side, dy=2)
+    one_side, three_side = shift(one, dx=3), shift(three, dx=1)
+    far = shift(tokens, dz=2)
+    near = jnp.concatenate([tokens, up, down, far])
+    low, high = one[:, :HALF], three[:, HALF:]
+    near, one_side, three_side, two_side, low, high = lax.optimization_barrier(
+        (near, one_side, three_side, two_side, low, high)
+    )
+    two_low, two_high = shift(low, dy=1), shift(high, dy=3)
+    other = shift(near, dt=1)
+
+    total = project(
+        project_first_kernel,
+        WIDE,
+        jax.ShapeDtypeStruct((2 * NEAR, WIDE), jnp.float32),
+        places,
+        bias_cols,
+        near,
+        other,
+        [own, own_side, one, one_side, three, three_side],
+        tuple((place, 0, 1) for place in (0, 1, 2, 3, 6, 7)),
+    )
+    parts = project(
+        project_last_kernel,
+        WINDOW,
+        jax.ShapeDtypeStruct((8, ROWS, WIDE), jnp.bfloat16),
+        places,
+        total,
+        near,
+        other,
+        [two_low, two_high, two_side],
+        ((4, 0), (4, 1), (5, 0, 1)),
+    )
     qkv = lax.all_to_all(parts, ("tp", "z"), split_axis=0, concat_axis=0, tiled=True)
     return attend(my_lengths, cosine, sine, qkv, cache)
 

time: 98.9 us -> 92.6 us (0.936)
  waiting for transfers between devices: 44.7 us -> 24.1 us
  blocking collectives: 0 us -> 15.3 us
  starting transfers between devices: 24.7 us -> 17.8 us
  Pallas kernels: 18.6 us -> 24.7 us
  local copies, waits for them, and re-layouts: 8.71 us -> 6.99 us
  other arithmetic: 1.79 us -> 3.06 us
    all_to_all x0 -> x1, blocking collectives: none -> 15.3 us  [on_device(): lax.all_to_all(parts, ('tp', 'z'), split_axis=0, concat_axis=0, tiled=True)]
    all_to_all x2 -> x0, starting transfers between devices: 11.2 us -> none  [the longest x1 5.99 us: on_device(): mine = lax.all_to_all(copies, 'z', split_axis=0, concat_axis=0, tiled=True)]
    ppermute x9 -> x12, waiting for transfers between devices: 35 us -> 24.1 us  [shift(): return lax.ppermute(array, AXES, pairs)]
    all_to_all x2 -> x0, waiting for transfers between devices: 9.69 us -> none  [the longest x1 9.69 us: on_device(): lax.all_to_all(parts, ('tp', 'z'), split_axis=0, concat_axis=0, tiled=True)]
    pallas_call x1 -> x2, Pallas kernels: 8.81 us -> 14.9 us  [project(): pl.pallas_call(functools.partial(kernel, where), in_specs=[pl.BlockSpec(m...]
    ppermute x9 -> x12, starting transfers between devices: 13.5 us -> 17.8 us  [shift(): return lax.ppermute(array, AXES, pairs)]
    broadcast_in_dim x1 -> x0, local copies, waits for them, and re-layouts: 2.64 us -> none  [on_device(): copies = jnp.broadcast_to(tokens[None], (4, ROWS, D)).reshape(NEAR, D)]
    concatenate x0 -> x1, other arithmetic: none -> 1.27 us  [on_device(): near = jnp.concatenate([tokens, up, down, far])]
  transfers between devices with their start and end apart: 11 -> 12, of which waited for: 6 -> 7; matrix products, arithmetic and copies ran while one was open for 5% -> 7% of each run, Pallas kernels for 0% -> 9%
where the time goes in v3:
time: 92.6 us; the launch traced here: 92.2 us
  Pallas kernels  24.7 us (27%)
  waiting for transfers between devices  24.1 us (26%)
  starting transfers between devices  17.8 us (19%)
  blocking collectives  15.3 us (17%)
  local copies, waits for them, and re-layouts  6.99 us (8%)
  other arithmetic  3.06 us (3%)
    ppermute x12, waiting for transfers between devices, shift(): return lax.ppermute(array, AXES, pairs)  24.1 us
    ppermute x12, starting transfers between devices, shift(): return lax.ppermute(array, AXES, pairs)  17.8 us
    all_to_all x1, blocking collectives, on_device(): lax.all_to_all(parts, ('tp', 'z'), split_axis=0, concat_axis=0, tiled=True)  15.3 us
    pallas_call x2, Pallas kernels, project(): pl.pallas_call(functools.partial(kernel, where), in_specs=[pl.BlockSpec(m...  14.9 us
    pallas_call x1, Pallas kernels, attend(): pl.pallas_call(attend_kernel, grid=(SLOTS,), in_specs=[pl.BlockSpec(memor...  9.77 us
    unnamed x20, local copies, waits for them, and re-layouts  3.63 us
  transfers between devices with their start and end apart: 12, of which 7 were waited for; matrix products, arithmetic and copies ran while one was open for 7% of the time, Pallas kernels for 9%

profile of v3, /device:TPU:1, one launch (start us, length us, event | category | flops | bytes accessed | tf_op | source)
XLA Modules:
  0.0 92.2 jit_solution(16359150585822496169)
XLA Ops:
  0.0 0.0 copy-start
  0.0 2.5 %collective-permute-start.3 = (bf16[64,4096]{1,0:T(8,128)(2,1)}, bf16[64,4096]{1,0:T(8,128)(2,1)S(1)}, u32[]{:S(2)}, u32[]{:S(2)}) collective-permute-start(bf16[64,4096]{1,0:T(8,128)(2,1)} %param.8), channel_id=1, source_target_pairs={{0,16},{2,18},{1,17},{3,19},{4,20},{6,22},{5,21},{7,23},{8,24},{10... | collective-permute-start | bytes 1572872 | tf_op jit(solution)/shard_map/ppermute | solution.py:47
  2.5 2.2 %collective-permute-start.4 = (bf16[64,4096]{1,0:T(8,128)(2,1)}, bf16[64,4096]{1,0:T(8,128)(2,1)S(1)}, u32[]{:S(2)}, u32[]{:S(2)}) collective-permute-start(bf16[64,4096]{1,0:T(8,128)(2,1)} %param.8), channel_id=1, source_target_pairs={{0,48},{2,50},{1,49},{3,51},{4,52},{6,54},{5,53},{7,55},{8,56},{10... | collective-permute-start | bytes 1572872 | tf_op jit(solution)/shard_map/ppermute | solution.py:47
  4.7 1.2 %collective-permute-start.2 = (bf16[80,4096]{1,0:T(8,128)(2,1)}, bf16[80,4096]{1,0:T(8,128)(2,1)}, u32[]{:S(2)}, u32[]{:S(2)}) collective-permute-start(bf16[80,4096]{1,0:T(8,128)(2,1)} %bitcast.19), channel_id=1, source_target_pairs={{0,2},{2,1},{1,3},{3,0},{4,6},{6,5},{5,7},{7,4},{8,10},{10,9},{9,1... | collective-permute-start | bytes 1966088 | tf_op jit(solution)/shard_map/ppermute | solution.py:47
  5.9 2.7 %collective-permute-start.1 = (bf16[80,4096]{1,0:T(8,128)(2,1)}, bf16[80,4096]{1,0:T(8,128)(2,1)S(1)}, u32[]{:S(2)}, u32[]{:S(2)}) collective-permute-start(bf16[80,4096]{1,0:T(8,128)(2,1)} %bitcast.20), channel_id=1, source_target_pairs={{0,12},{2,14},{1,13},{3,15},{4,0},{6,2},{5,1},{7,3},{8,4},{10,6},{... | collective-permute-start | bytes 1966088 | tf_op jit(solution)/shard_map/ppermute | solution.py:47
  8.6 0.0 collective-permute-start
  8.6 0.0 copy-done
  8.6 0.6 gather_fusion
  9.3 1.3 %gather_fusion.1 = s32[4]{0:T(128)S(1)} fusion(s32[256]{0:T(256)} %param.12, s32[1024]{0:T(1024)S(1)} %pad_clamp_fusion), kind=kCustom, calls=%fused_computation.1.clone | custom fusion | bytes 48 | tf_op jit(solution)/shard_map/jit(_take)/gather | solution.py:249
  10.6 0.0 copy-start.8
  10.6 0.1 add_convert_fusion
  10.8 0.1 convert_element_type.12
  10.9 0.8 dynamic-slice_convert_fusion
  11.6 0.6 reshape.28.bias_ref
  12.2 0.7 stack.75.at_ref
  12.9 0.2 fusion
  13.1 0.7 pad_maximum_fusion.1
  13.8 2.7 %collective-permute-done.3 = bf16[64,4096]{1,0:T(8,128)(2,1)S(1)} collective-permute-done((bf16[64,4096]{1,0:T(8,128)(2,1)}, bf16[64,4096]{1,0:T(8,128)(2,1)S(1)}, u32[]{:S(2)}, u32[]{:S(2)}) %collective-permute-start.3) | collective-permute-done | bytes 524320 | tf_op jit(solution)/shard_map/ppermute | solution.py:47
  16.6 0.0 collective-permute-done.4
  16.6 4.9 %collective-permute-done.2.refs_1_ = bf16[80,4096]{1,0:T(8,128)(2,1)} collective-permute-done((bf16[80,4096]{1,0:T(8,128)(2,1)}, bf16[80,4096]{1,0:T(8,128)(2,1)}, u32[]{:S(2)}, u32[]{:S(2)}) %collective-permute-start.2) | collective-permute-done | bytes 655392 | tf_op jit(solution)/shard_map/ppermute | solution.py:47
  21.5 0.2 collective-permute-done.1.refs_4_
  21.7 0.0 copy-start.6
  21.7 3.0 %collective-permute-done.refs_2_ = bf16[80,4096]{1,0:T(8,128)(2,1)S(1)} collective-permute-done((bf16[80,4096]{1,0:T(8,128)(2,1)}, bf16[80,4096]{1,0:T(8,128)(2,1)S(1)}, u32[]{:S(2)}, u32[]{:S(2)}) %collective-permute-start) | collective-permute-done | bytes 655392 | tf_op jit(solution)/shard_map/ppermute | solution.py:47
  24.7 0.0 copy-start.7
  24.7 1.0 %collective-permute-start.5 = (bf16[64,4096]{1,0:T(8,128)(2,1)}, bf16[64,4096]{1,0:T(8,128)(2,1)S(1)}, u32[]{:S(2)}, u32[]{:S(2)}) collective-permute-start(bf16[64,4096]{1,0:T(8,128)(2,1)} %param.8), channel_id=1, source_target_pairs={{0,32},{2,34},{1,33},{3,35},{4,36},{6,38},{5,37},{7,39},{8,40},{10... | collective-permute-start | bytes 1572872 | tf_op jit(solution)/shard_map/ppermute | solution.py:47
  25.7 0.0 collective-permute-start.8
  25.7 1.5 %collective-permute-start.6 = (bf16[80,4096]{1,0:T(8,128)(2,1)S(1)}, bf16[80,4096]{1,0:T(8,128)(2,1)S(1)}, u32[]{:S(2)}, u32[]{:S(2)}) collective-permute-start(bf16[80,4096]{1,0:T(8,128)(2,1)S(1)} %collective-permute-done.refs_2_), channel_id=1, source_target_pairs={{0,3},{2,0},{1,2},{3,1},{4,7},{6,4},{5,6},{7,5},{8,11},{10,8},{9,1... | collective-permute-start | bytes 1966088 | tf_op jit(solution)/shard_map/ppermute | solution.py:47
  27.2 0.0 collective-permute-start.7
  27.2 10.2 %collective-permute-done.5 = bf16[64,4096]{1,0:T(8,128)(2,1)S(1)} collective-permute-done((bf16[64,4096]{1,0:T(8,128)(2,1)}, bf16[64,4096]{1,0:T(8,128)(2,1)S(1)}, u32[]{:S(2)}, u32[]{:S(2)}) %collective-permute-start.5) | collective-permute-done | bytes 524320 | tf_op jit(solution)/shard_map/ppermute | solution.py:47
  37.4 1.3 %pad_maximum_fusion.near = bf16[256,4096]{1,0:T(8,128)(2,1)S(1)} fusion(bf16[64,4096]{1,0:T(8,128)(2,1)S(1)} %collective-permute-done.5, bf16[64,4096]{1,0:T(8,128)(2,1)S(1)} %collective-permute-done.4, bf16[64,4096]{1,0:T(8,128)(2,1)S(1)} %collective-permute-done.3, bf16[64,4096]{1,0:T(8,128)(2,1)} %param.8), kind=kLoop, calls=%fused_computation.2 | loop fusion | flops 8388608 | bytes 4194304 | tf_op jit(solution)/shard_map/concatenate | solution.py:269
  38.7 0.0 copy-start.1
  38.7 1.9 %collective-permute-done.8.refs_2_ = bf16[80,4096]{1,0:T(8,128)(2,1)S(1)} collective-permute-done((bf16[80,4096]{1,0:T(8,128)(2,1)}, bf16[80,4096]{1,0:T(8,128)(2,1)S(1)}, u32[]{:S(2)}, u32[]{:S(2)}) %collective-permute-start.8) | collective-permute-done | bytes 655392 | tf_op jit(solution)/shard_map/ppermute | solution.py:47
  40.6 0.0 copy-start.3
  40.6 0.0 collective-permute-done.6.refs_3_
  40.6 0.0 copy-start.9
  40.6 0.9 copy-done.9
  41.5 0.0 collective-permute-done.7.refs_5_
  41.5 4.1 %collective-permute-start.9 = (bf16[256,4096]{1,0:T(8,128)(2,1)S(1)}, bf16[256,4096]{1,0:T(8,128)(2,1)S(1)}, u32[]{:S(2)}, u32[]{:S(2)}) collective-permute-start(bf16[256,4096]{1,0:T(8,128)(2,1)S(1)} %pad_maximum_fusion.near), channel_id=1, source_target_pairs={{0,64},{2,66},{1,65},{3,67},{4,68},{6,70},{5,69},{7,71},{8,72},{10... | collective-permute-start | bytes 6291464 | tf_op jit(solution)/shard_map/ppermute | solution.py:47
  45.6 0.9 %collective-permute-start.10 = (bf16[80,2048]{1,0:T(8,128)(2,1)S(1)}, bf16[80,2048]{1,0:T(8,128)(2,1)S(1)}, u32[]{:S(2)}, u32[]{:S(2)}) collective-permute-start(bf16[80,2048]{1,0:T(8,128)(2,1)S(1)} %slice.6), channel_id=1, source_target_pairs={{0,4},{2,6},{1,5},{3,7},{4,8},{6,10},{5,9},{7,11},{8,12},{10,14},{... | collective-permute-start | bytes 983048 | tf_op jit(solution)/shard_map/ppermute | solution.py:47
  46.6 1.7 %collective-permute-start.11 = (bf16[80,2048]{1,0:T(8,128)(2,1)S(1)}, bf16[80,2048]{1,0:T(8,128)(2,1)S(1)}, u32[]{:S(2)}, u32[]{:S(2)}) collective-permute-start(bf16[80,2048]{1,0:T(8,128)(2,1)S(1)} %slice.7), channel_id=1, source_target_pairs={{0,12},{2,14},{1,13},{3,15},{4,0},{6,2},{5,1},{7,3},{8,4},{10,6},{... | collective-permute-start | bytes 983048 | tf_op jit(solution)/shard_map/ppermute | solution.py:47
  48.3 1.1 %collective-permute-done.9.other = bf16[256,4096]{1,0:T(8,128)(2,1)S(1)} collective-permute-done((bf16[256,4096]{1,0:T(8,128)(2,1)S(1)}, bf16[256,4096]{1,0:T(8,128)(2,1)S(1)}, u32[]{:S(2)}, u32[]{:S(2)}) %collective-permute-start.9) | collective-permute-done | bytes 2097184 | tf_op jit(solution)/shard_map/ppermute | solution.py:47
  49.4 0.0 copy-done.6
  49.4 0.0 copy-done.7
  49.4 0.0 copy-done.1
  49.4 0.0 copy-start.2
  49.4 1.3 %copy-done.2 = bf16[256,4096]{1,0:T(8,128)(2,1)} copy-done((bf16[256,4096]{1,0:T(8,128)(2,1)}, bf16[256,4096]{1,0:T(8,128)(2,1)S(1)}, u32[]{:S(2)}) %copy-start.2) | copy-done | bytes 2097176
  50.7 8.6 %project_first.1.total_ref = f32[512,640]{1,0:T(8,128)} custom-call(s32[18]{0:T(128)} %stack.75.at_ref, f32[1,640]{1,0:T(1,128)} %reshape.28.bias_ref, bf16[256,4096]{1,0:T(8,128)(2,1)} %copy-done.1, bf16[256,4096]{1,0:T(8,128)(2,1)} %copy-done.2, bf16[80,4096]{1,0:T(8,128)(2,1)} %bitcast.22, bf16[80,4096]{1,0:T(8,128)(2,1)} %collective-permute-done.2.refs_1_, ...), custom_call_target="tpu_custom_call" | custom-call | flops 2684354560 | bytes 9437184 | tf_op jit(solution)/shard_map/project_first/pallas_call | solution.py:126
  59.4 0.0 copy-done.8
  59.4 0.0 collective-permute-done.10.refs_0_
  59.4 0.0 copy-start.4
  59.4 0.0 collective-permute-done.11.refs_1_
  59.4 0.0 copy-done.3
  59.4 0.7 copy-done.4
  60.1 0.0 copy-start.5
  60.1 0.7 copy-done.5
  60.9 6.3 %project_last.1 = bf16[8,64,640]{2,1,0:T(8,128)(2,1)} custom-call(s32[18]{0:T(128)} %stack.75.at_ref, f32[512,640]{1,0:T(8,128)} %project_first.1.total_ref, bf16[256,4096]{1,0:T(8,128)(2,1)} %copy-done.1, bf16[256,4096]{1,0:T(8,128)(2,1)} %copy-done.2, bf16[80,2048]{1,0:T(8,128)(2,1)} %copy-done.4, bf16[80,2048]{1,0:T(8,128)(2,1)} %copy-done.5, ...), custom_call_target="tpu_custom_call" | custom-call | flops 1073741824 | bytes 6291456 | tf_op jit(solution)/shard_map/project_last/pallas_call | solution.py:126
  67.1 15.3 %all_to_all.5.qkv = bf16[8,64,640]{2,1,0:T(8,128)(2,1)} all-to-all(bf16[8,64,640]{2,1,0:T(8,128)(2,1)} %project_last.1), channel_id=1, replica_groups=mesh['tp'=2,'z'=4,'y'=4,'xl'=2,'xh'=2] {'tp','z'}, dimensions={0} | all-to-all | bytes 1310720 | tf_op jit(solution)/shard_map/all_to_all | solution.py:299
  82.5 9.8 %attend.1 = bf16[64,4096]{1,0:T(8,128)(2,1)} custom-call(s32[4]{0:T(128)} %copy-done.8, f32[64,128]{1,0:T(8,128)} %get-tuple-element.24.cos_ref, f32[64,128]{1,0:T(8,128)} %get-tuple-element.25.sin_ref, bf16[8,64,640]{2,1,0:T(8,128)(2,1)} %all_to_all.5.qkv, bf16[4,1024,1024]{2,1,0:T(8,128)(2,1)} %cache_ref.1), custom_call_target="tpu_custom_call" | custom-call | tf_op jit(solution)/shard_map/attend/pallas_call | solution.py:211
  (8 shorter events, 0.1 us)
Async XLA Ops:
  0.0 8.6 %copy-start = (s32[256]{0:T(256)S(1)}, s32[256]{0:T(256)}, u32[]{:S(2)}) copy-start(s32[256]{0:T(256)} %param.13) | copy-start | bytes 3076
  0.0 16.5 %collective-permute-start.3 = (bf16[64,4096]{1,0:T(8,128)(2,1)}, bf16[64,4096]{1,0:T(8,128)(2,1)S(1)}, u32[]{:S(2)}, u32[]{:S(2)}) collective-permute-start(bf16[64,4096]{1,0:T(8,128)(2,1)} %param.8), channel_id=1, source_target_pairs={{0,16},{2,18},{1,17},{3,19},{4,20},{6,22},{5,21},{7,23},{8,24},{10... | collective-permute-start | bytes 1572872 | tf_op jit(solution)/shard_map/ppermute | solution.py:47
  2.5 14.1 %collective-permute-start.4 = (bf16[64,4096]{1,0:T(8,128)(2,1)}, bf16[64,4096]{1,0:T(8,128)(2,1)S(1)}, u32[]{:S(2)}, u32[]{:S(2)}) collective-permute-start(bf16[64,4096]{1,0:T(8,128)(2,1)} %param.8), channel_id=1, source_target_pairs={{0,48},{2,50},{1,49},{3,51},{4,52},{6,54},{5,53},{7,55},{8,56},{10... | collective-permute-start | bytes 1572872 | tf_op jit(solution)/shard_map/ppermute | solution.py:47
  4.7 16.8 %collective-permute-start.2 = (bf16[80,4096]{1,0:T(8,128)(2,1)}, bf16[80,4096]{1,0:T(8,128)(2,1)}, u32[]{:S(2)}, u32[]{:S(2)}) collective-permute-start(bf16[80,4096]{1,0:T(8,128)(2,1)} %bitcast.19), channel_id=1, source_target_pairs={{0,2},{2,1},{1,3},{3,0},{4,6},{6,5},{5,7},{7,4},{8,10},{10,9},{9,1... | collective-permute-start | bytes 1966088 | tf_op jit(solution)/shard_map/ppermute | solution.py:47
  5.9 15.8 %collective-permute-start.1 = (bf16[80,4096]{1,0:T(8,128)(2,1)}, bf16[80,4096]{1,0:T(8,128)(2,1)S(1)}, u32[]{:S(2)}, u32[]{:S(2)}) collective-permute-start(bf16[80,4096]{1,0:T(8,128)(2,1)} %bitcast.20), channel_id=1, source_target_pairs={{0,12},{2,14},{1,13},{3,15},{4,0},{6,2},{5,1},{7,3},{8,4},{10,6},{... | collective-permute-start | bytes 1966088 | tf_op jit(solution)/shard_map/ppermute | solution.py:47
  8.6 16.1 %collective-permute-start = (bf16[80,4096]{1,0:T(8,128)(2,1)}, bf16[80,4096]{1,0:T(8,128)(2,1)S(1)}, u32[]{:S(2)}, u32[]{:S(2)}) collective-permute-start(bf16[80,4096]{1,0:T(8,128)(2,1)} %bitcast.21), channel_id=1, source_target_pairs={{0,4},{2,6},{1,5},{3,7},{4,8},{6,10},{5,9},{7,11},{8,12},{10,14},{... | collective-permute-start | bytes 1966088 | tf_op jit(solution)/shard_map/ppermute | solution.py:47
  10.6 48.7 %copy-start.8 = (s32[4]{0:T(128)}, s32[4]{0:T(128)S(1)}, u32[]{:S(2)}) copy-start(s32[4]{0:T(128)S(1)} %and_select_fusion.length_ref) | copy-start | bytes 52
  21.7 27.7 %copy-start.6 = (bf16[80,4096]{1,0:T(8,128)(2,1)}, bf16[80,4096]{1,0:T(8,128)(2,1)S(1)}, u32[]{:S(2)}) copy-start(bf16[80,4096]{1,0:T(8,128)(2,1)S(1)} %collective-permute-done.1.refs_4_) | copy-start | bytes 1966084
  24.7 24.7 %copy-start.7 = (bf16[80,4096]{1,0:T(8,128)(2,1)}, bf16[80,4096]{1,0:T(8,128)(2,1)S(1)}, u32[]{:S(2)}) copy-start(bf16[80,4096]{1,0:T(8,128)(2,1)S(1)} %collective-permute-done.refs_2_) | copy-start | bytes 1966084
  24.7 12.7 %collective-permute-start.5 = (bf16[64,4096]{1,0:T(8,128)(2,1)}, bf16[64,4096]{1,0:T(8,128)(2,1)S(1)}, u32[]{:S(2)}, u32[]{:S(2)}) collective-permute-start(bf16[64,4096]{1,0:T(8,128)(2,1)} %param.8), channel_id=1, source_target_pairs={{0,32},{2,34},{1,33},{3,35},{4,36},{6,38},{5,37},{7,39},{8,40},{10... | collective-permute-start | bytes 1572872 | tf_op jit(solution)/shard_map/ppermute | solution.py:47
  25.7 14.9 %collective-permute-start.8 = (bf16[80,4096]{1,0:T(8,128)(2,1)}, bf16[80,4096]{1,0:T(8,128)(2,1)S(1)}, u32[]{:S(2)}, u32[]{:S(2)}) collective-permute-start(bf16[80,4096]{1,0:T(8,128)(2,1)} %collective-permute-done.2.refs_1_), channel_id=1, source_target_pairs={{0,8},{2,10},{1,9},{3,11},{4,12},{6,14},{5,13},{7,15},{8,0},{10,2}... | collective-permute-start | bytes 1966088 | tf_op jit(solution)/shard_map/ppermute | solution.py:47
  25.7 14.9 %collective-permute-start.6 = (bf16[80,4096]{1,0:T(8,128)(2,1)S(1)}, bf16[80,4096]{1,0:T(8,128)(2,1)S(1)}, u32[]{:S(2)}, u32[]{:S(2)}) collective-permute-start(bf16[80,4096]{1,0:T(8,128)(2,1)S(1)} %collective-permute-done.refs_2_), channel_id=1, source_target_pairs={{0,3},{2,0},{1,2},{3,1},{4,7},{6,4},{5,6},{7,5},{8,11},{10,8},{9,1... | collective-permute-start | bytes 1966088 | tf_op jit(solution)/shard_map/ppermute | solution.py:47
  27.2 14.4 %collective-permute-start.7 = (bf16[80,4096]{1,0:T(8,128)(2,1)S(1)}, bf16[80,4096]{1,0:T(8,128)(2,1)}, u32[]{:S(2)}, u32[]{:S(2)}) collective-permute-start(bf16[80,4096]{1,0:T(8,128)(2,1)S(1)} %collective-permute-done.1.refs_4_), channel_id=1, source_target_pairs={{0,2},{2,1},{1,3},{3,0},{4,6},{6,5},{5,7},{7,4},{8,10},{10,9},{9,1... | collective-permute-start | bytes 1966088 | tf_op jit(solution)/shard_map/ppermute | solution.py:47
  38.7 10.7 %copy-start.1 = (bf16[256,4096]{1,0:T(8,128)(2,1)}, bf16[256,4096]{1,0:T(8,128)(2,1)S(1)}, u32[]{:S(2)}) copy-start(bf16[256,4096]{1,0:T(8,128)(2,1)S(1)} %pad_maximum_fusion.near) | copy-start | bytes 6291460
  40.6 18.8 %copy-start.3 = (bf16[80,4096]{1,0:T(8,128)(2,1)}, bf16[80,4096]{1,0:T(8,128)(2,1)S(1)}, u32[]{:S(2)}) copy-start(bf16[80,4096]{1,0:T(8,128)(2,1)S(1)} %collective-permute-done.8.refs_2_) | copy-start | bytes 1966084
  40.6 0.9 copy-start.9
  41.5 7.9 %collective-permute-start.9 = (bf16[256,4096]{1,0:T(8,128)(2,1)S(1)}, bf16[256,4096]{1,0:T(8,128)(2,1)S(1)}, u32[]{:S(2)}, u32[]{:S(2)}) collective-permute-start(bf16[256,4096]{1,0:T(8,128)(2,1)S(1)} %pad_maximum_fusion.near), channel_id=1, source_target_pairs={{0,64},{2,66},{1,65},{3,67},{4,68},{6,70},{5,69},{7,71},{8,72},{10... | collective-permute-start | bytes 6291464 | tf_op jit(solution)/shard_map/ppermute | solution.py:47
  45.6 13.8 %collective-permute-start.10 = (bf16[80,2048]{1,0:T(8,128)(2,1)S(1)}, bf16[80,2048]{1,0:T(8,128)(2,1)S(1)}, u32[]{:S(2)}, u32[]{:S(2)}) collective-permute-start(bf16[80,2048]{1,0:T(8,128)(2,1)S(1)} %slice.6), channel_id=1, source_target_pairs={{0,4},{2,6},{1,5},{3,7},{4,8},{6,10},{5,9},{7,11},{8,12},{10,14},{... | collective-permute-start | bytes 983048 | tf_op jit(solution)/shard_map/ppermute | solution.py:47
  46.6 12.8 %collective-permute-start.11 = (bf16[80,2048]{1,0:T(8,128)(2,1)S(1)}, bf16[80,2048]{1,0:T(8,128)(2,1)S(1)}, u32[]{:S(2)}, u32[]{:S(2)}) collective-permute-start(bf16[80,2048]{1,0:T(8,128)(2,1)S(1)} %slice.7), channel_id=1, source_target_pairs={{0,12},{2,14},{1,13},{3,15},{4,0},{6,2},{5,1},{7,3},{8,4},{10,6},{... | collective-permute-start | bytes 983048 | tf_op jit(solution)/shard_map/ppermute | solution.py:47
  49.4 1.3 %copy-start.2 = (bf16[256,4096]{1,0:T(8,128)(2,1)}, bf16[256,4096]{1,0:T(8,128)(2,1)S(1)}, u32[]{:S(2)}) copy-start(bf16[256,4096]{1,0:T(8,128)(2,1)S(1)} %collective-permute-done.9.other) | copy-start | bytes 6291460
  59.4 0.7 copy-start.4
  60.1 0.7 copy-start.5

commit v4 on v3

v4 whole, which is shorter than its diff:
```python
import functools

import jax
import jax.numpy as jnp
from jax import lax
from jax.experimental import pallas as pl
from jax.experimental.pallas import tpu as pltpu
from jax.sharding import Mesh, PartitionSpec as P

D = 4096
HD = 128
HQ = 32
KVH = 4
STRETCH = 16
CAP = 1024
GROUP = 8
SLOTS = 4
ROWS = SLOTS * STRETCH
COLS = 80
SHARDS = 8
WIDE = COLS * SHARDS
HEADS = WIDE // HD
HALF = D // 2
ROPE_THETA = 1000000.0
LOG2E = 1.4426950408889634
AXES = ("tp", "z", "y", "xl", "xh")
NEAR = 4 * ROWS
WINDOW = 256
CHUNK = 256
PROJECT_VMEM = 20 * 1024 * 1024
ATTEND_VMEM = 16 * 1024 * 1024
NT = (((1,), (1,)), ((), ()))


def device_index(t, z, y, x):
    x = x % 4
    return ((((t % 2) * 4 + z % 4) * 4 + y % 4) * 2 + x % 2) * 2 + x // 2


def shift(array, dt=0, dz=0, dy=0, dx=0):
    pairs = [
        (device_index(t, z, y, x), device_index(t + dt, z + dz, y + dy, x + dx))
        for t in range(2)
        for z in range(4)
        for y in range(4)
        for x in range(4)
    ]
    return lax.ppermute(array, AXES, pairs)


def gather(pieces, where, at_ref, weights):
    for piece, (place, low) in zip(pieces, where):
        start = pl.multiple_of(at_ref[place], 16)
        weights[pl.ds(start, COLS), low : low + piece.shape[1]] = piece[...]


def multiply(near, other, weights):
    return [
        lax.dot_general(rows[...], weights[...], NT, preferred_element_type=jnp.float32)
        for rows in (near, other)
    ]


def project_first_kernel(where, at_ref, bias_ref, near, other, *refs):
    pieces = refs[:-2]
    out, weights = refs[-2:]
    start = pl.multiple_of(at_ref[16], 16)
    weights[pl.ds(start, 2 * COLS), :] = jnp.zeros((2 * COLS, D), jnp.bfloat16)
    gather(pieces, where, at_ref, weights)
    first, second = multiply(near, other, weights)
    out[:NEAR] = first + bias_ref[...]
    out[NEAR:] = second + bias_ref[...]


def project_last_kernel(where, at_ref, total_ref, near, other, *refs):
    pieces = refs[:-2]
    out, weights = refs[-2:]
    shift_by = at_ref[17]
    for k in range(4):

        @pl.when(shift_by == 2 * k * STRETCH)
        def _():
            low, high = 2 * k * STRETCH, 2 * k * STRETCH + 2 * COLS
            if low:
                weights[:low, :] = jnp.zeros((low, D), jnp.bfloat16)
            if high < WINDOW:
                weights[high:, :] = jnp.zeros((WINDOW - high, D), jnp.bfloat16)

    gather(pieces, where, at_ref, weights)
    total = multiply(near, other, weights)
    for k in range(4):

        @pl.when(shift_by == 2 * k * STRETCH)
        def _():
            low, high = k * HD, k * HD + WINDOW
            for block in range(8):
                rows = slice(block * ROWS, (block + 1) * ROWS)
                here = slice(block % 4 * ROWS, (block % 4 + 1) * ROWS)
                done = total_ref[rows, low:high] + total[block // 4][here]
                home = at_ref[8 + block]
                out[home, :, low:high] = done.astype(jnp.bfloat16)
                if low:
                    out[home, :, :low] = total_ref[rows, :low].astype(jnp.bfloat16)
                if high < WIDE:
                    out[home, :, high:] = total_ref[rows, high:].astype(jnp.bfloat16)


def project(kernel, width, out_shape, places, whole, near, other, pieces, where):
    return pl.pallas_call(
        functools.partial(kernel, where),
        in_specs=[pl.BlockSpec(memory_space=pltpu.SMEM)]
        + [pl.BlockSpec(memory_space=pltpu.VMEM)] * (len(pieces) + 3),
        out_specs=pl.BlockSpec(memory_space=pltpu.VMEM),
        out_shape=out_shape,
        scratch_shapes=[pltpu.VMEM((width, D), jnp.bfloat16)],
        compiler_params=pltpu.CompilerParams(vmem_limit_bytes=PROJECT_VMEM),
        cost_estimate=pl.CostEstimate(
            flops=4 * NEAR * width * D,
            bytes_accessed=2 * D * (2 * NEAR + width),
            transcendentals=0,
        ),
        name=kernel.__name__.removesuffix("_kernel"),
    )(places, whole, near, other, *pieces)


def attend_kernel(length_ref, cos_ref, sin_ref, qkv, cache, out_ref, scores):
    scale = HD ** (-0.5) * LOG2E
    key_at = lax.broadcasted_iota(jnp.int32, (1, CAP), 1)
    token = lax.broadcasted_iota(jnp.int32, (GROUP * STRETCH, STRETCH), 0) % STRETCH
    causal = lax.broadcasted_iota(jnp.int32, (GROUP * STRETCH, STRETCH), 1) <= token

    def head(slot, h):
        low = (h % HEADS) * HD
        rows = slice(slot * STRETCH, (slot + 1) * STRETCH)
        return qkv[h // HEADS, rows, low : low + HD]

    def rotated(slot, h):
        rows = slice(slot * STRETCH, (slot + 1) * STRETCH)
        u = head(slot, h).astype(jnp.float32)
        turned = pltpu.roll(u, HD // 2, 1) * sin_ref[rows, :]
        return (u * cos_ref[rows, :] + turned).astype(jnp.bfloat16)

    def score(slot, k):
        hidden = jnp.where(key_at < length_ref[slot], 0.0, -jnp.inf)
        queries = [rotated(slot, k * GROUP + g) for g in range(GROUP)]
        queries = jnp.concatenate(queries, axis=0)
        new = lax.dot_general(
            queries, rotated(slot, HQ + k), NT, preferred_element_type=jnp.float32
        )
        new = jnp.where(causal, new, -jnp.inf)
        highest = None
        for low in range(0, CAP, CHUNK):
            keys = cache[slot, low : low + CHUNK, k * HD : (k + 1) * HD]
            part = lax.dot_general(
                queries, keys, NT, preferred_element_type=jnp.float32
            )
            part = part + hidden[:, low : low + CHUNK]
            scores[k % 2, :, low : low + CHUNK] = part
            part = jnp.maximum(part[:, :HD], part[:, HD:])
            highest = part if highest is None else jnp.maximum(highest, part)
        top = jnp.maximum(
            jnp.max(highest, axis=1, keepdims=True), jnp.max(new, axis=1, keepdims=True)
        )
        return top * scale, new

    def mix(slot, k, base, new):
        new = jnp.exp2(new * scale - base)
        mixed = jnp.dot(
            new.astype(jnp.bfloat16),
            head(slot, HQ + KVH + k),
            preferred_element_type=jnp.float32,
        )
        total = None
        for low in range(0, CAP, CHUNK):
            part = jnp.exp2(scores[k % 2, :, low : low + CHUNK] * scale - base)
            values = cache[slot, low : low + CHUNK, (KVH + k) * HD : (KVH + k + 1) * HD]
            mixed = mixed + jnp.dot(
                part.astype(jnp.bfloat16), values, preferred_element_type=jnp.float32
            )
            part = part[:, :HD] + part[:, HD:]
            total = part if total is None else total + part
        total = jnp.sum(total, axis=1, keepdims=True) + jnp.sum(
            new, axis=1, keepdims=True
        )
        mixed = (mixed / total).astype(jnp.bfloat16)
        for g in range(GROUP):
            low = (k * GROUP + g) * HD
            out_ref[slot * STRETCH : (slot + 1) * STRETCH, low : low + HD] = mixed[
                g * STRETCH : (g + 1) * STRETCH
            ]

    pairs = [(slot, k) for slot in range(SLOTS) for k in range(KVH)]
    ahead = None
    for pair in pairs:
        state = score(*pair)
        if ahead is not None:
            mix(*ahead)
        ahead = (*pair, *state)
    mix(*ahead)


def attend(lengths, cosine, sine, qkv, cache):
    return pl.pallas_call(
        attend_kernel,
        in_specs=[pl.BlockSpec(memory_space=pltpu.SMEM)]
        + [pl.BlockSpec(memory_space=pltpu.VMEM)] * 4,
        out_specs=pl.BlockSpec(memory_space=pltpu.VMEM),
        out_shape=jax.ShapeDtypeStruct((ROWS, HQ * HD), jnp.bfloat16),
        scratch_shapes=[pltpu.VMEM((2, GROUP * STRETCH, CAP), jnp.float32)],
        compiler_params=pltpu.CompilerParams(vmem_limit_bytes=ATTEND_VMEM),
        name="attend",
    )(lengths, cosine, sine, qkv, cache)


def on_device(tokens, weight, bias, cache, lengths, slot_stream):
    t = lax.axis_index("tp")
    z = lax.axis_index("z")
    y = lax.axis_index("y")
    xl = lax.axis_index("xl")
    group = t * 4 + z
    index = (group * 4 + y) * 2 + xl

    far_y = (y + 2) % 4
    places = []
    for dy in range(4):
        base = far_y * 2 * STRETCH if dy == 2 else (y - dy) % 4 * 2 * COLS
        places += [base + xl * COLS, base + (1 - xl) * COLS]
    for core in (t, 1 - t):
        places += [core * 4 + (z - dz) % 4 for dz in (0, 1, 3, 2)]
    places += [far_y * 2 * COLS, far_y * 2 * STRETCH]
    places = jnp.stack(places).astype(jnp.int32)
    bias_cols = lax.dynamic_slice_in_dim(bias, group * WIDE, WIDE, 0)
    bias_cols = bias_cols.astype(jnp.float32)[None, :]

    my_slots = index * SLOTS + jnp.arange(SLOTS, dtype=jnp.int32)
    my_lengths = jnp.take(lengths, jnp.take(slot_stream, my_slots)).astype(jnp.int32)
    positions = (my_lengths[:, None] + jnp.arange(STRETCH, dtype=jnp.int32)).reshape(-1)
    frequency = ROPE_THETA ** (
        -(jnp.arange(HD // 2, dtype=jnp.float32) * 2.0) / HD
    )
    angles = positions.astype(jnp.float32)[:, None] * frequency[None, :]
    cosine, sine = jnp.cos(angles), jnp.sin(angles)
    cosine = jnp.concatenate([cosine, cosine], axis=1)
    sine = jnp.concatenate([-sine, sine], axis=1)

    own = weight.T
    one, three, own_side = shift(own, dy=1), shift(own, dy=3), shift(own, dx=1)
    up, down = shift(tokens, dz=1), shift(tokens, dz=3)
    one, three, own_side, up, down, tokens, small = lax.optimization_barrier(
        (one, three, own_side, up, down, tokens, (places, bias_cols, my_lengths, cosine, sine))
    )
    places, bias_cols, my_lengths, cosine, sine = small
    two_side = shift(own_side, dy=2)
    one_side, three_side = shift(one, dx=3), shift(three, dx=1)
    far = shift(tokens, dz=2)
    near = jnp.concatenate([tokens, up, down, far])
    low, high = one[:, :HALF], three[:, HALF:]
    near, one_side, three_side, two_side, low, high = lax.optimization_barrier(
        (near, one_side, three_side, two_side, low, high)
    )
    two_low, two_high = shift(low, dy=1), shift(high, dy=3)
    other = shift(near, dt=1)

    total = project(
        project_first_kernel,
        WIDE,
        jax.ShapeDtypeStruct((2 * NEAR, WIDE), jnp.float32),
        places,
        bias_cols,
        near,
        other,
        [own, own_side, one, one_side, three, three_side],
        tuple((place, 0) for place in (0, 1, 2, 3, 6, 7)),
    )
    parts = project(
        project_last_kernel,
        WINDOW,
        jax.ShapeDtypeStruct((8, ROWS, WIDE), jnp.bfloat16),
        places,
        total,
        near,
        other,
        [two_low, two_high, two_side],
        ((4, 0), (4, HALF), (5, 0)),
    )
    qkv = lax.all_to_all(parts, ("tp", "z"), split_axis=0, concat_axis=0, tiled=True)
    return attend(my_lengths, cosine, sine, qkv, cache)


def solution(mesh):
    fine = Mesh(mesh.devices.reshape(2, 4, 4, 2, 2), AXES)
    part = ("xh", "tp", "z", "y", "xl")
    in_specs = (
        P(part, None),
        P(None, ("tp", "z", "y", "xl")),
        P(),
        P(part, None, None),
        P("xh"),
        P("xh"),
    )
    return jax.shard_map(
        on_device,
        mesh=fine,
        in_specs=in_specs,
        out_specs=P(part, None),
        check_vma=False,
    )
```

time: 92.6 us -> 79.5 us (0.86)
  Pallas kernels: 24.7 us -> 12.6 us
  local copies, waits for them, and re-layouts: 6.99 us -> 2.21 us
  waiting for transfers between devices: 24.1 us -> 28.8 us
    pallas_call x2, Pallas kernels: 14.9 us -> 6.43 us  [project(): pl.pallas_call(functools.partial(kernel, where), in_specs=[pl.BlockSpec(m...]
    ppermute x12, waiting for transfers between devices: 24.1 us -> 28.8 us  [shift(): return lax.ppermute(array, AXES, pairs)]
    unnamed x20 -> x8, local copies, waits for them, and re-layouts: 3.63 us -> 0.02 us
    pallas_call x1, Pallas kernels: 9.77 us -> 6.22 us  [attend(): pl.pallas_call(attend_kernel, in_specs=[pl.BlockSpec(memory_space=pltpu.S...]
  transfers between devices with their start and end apart: 12 -> 12, of which waited for: 7 -> 9; matrix products, arithmetic and copies ran while one was open for 7% -> 6% of each run, Pallas kernels for 9% -> 5%
where the time goes in v4:
time: 79.5 us; the launch traced here: 79.3 us
  waiting for transfers between devices  28.8 us (36%)
  starting transfers between devices  17.9 us (23%)
  blocking collectives  14.9 us (19%)
  Pallas kernels  12.6 us (16%)
  other arithmetic  2.66 us (3%)
  local copies, waits for them, and re-layouts  2.21 us (3%)
    ppermute x12, waiting for transfers between devices, shift(): return lax.ppermute(array, AXES, pairs)  28.8 us
    ppermute x12, starting transfers between devices, shift(): return lax.ppermute(array, AXES, pairs)  17.9 us
    all_to_all x1, blocking collectives, on_device(): lax.all_to_all(parts, ('tp', 'z'), split_axis=0, concat_axis=0, tiled=True)  14.9 us
    pallas_call x2, Pallas kernels, project(): pl.pallas_call(functools.partial(kernel, where), in_specs=[pl.BlockSpec(m...  6.43 us
    pallas_call x1, Pallas kernels, attend(): pl.pallas_call(attend_kernel, in_specs=[pl.BlockSpec(memory_space=pltpu.S...  6.22 us
  transfers between devices with their start and end apart: 12, of which 9 were waited for; matrix products, arithmetic and copies ran while one was open for 6% of the time, Pallas kernels for 5%

profile of v4, /device:TPU:1, one launch (start us, length us, event | category | flops | bytes accessed | tf_op | source)
XLA Modules:
  0.0 79.3 jit_solution(11952426847262226803)
XLA Ops:
  0.0 0.0 copy-start
  0.0 0.0 copy-start.1
  0.0 2.5 %collective-permute-start.3 = (bf16[64,4096]{1,0:T(8,128)(2,1)}, bf16[64,4096]{1,0:T(8,128)(2,1)S(1)}, u32[]{:S(2)}, u32[]{:S(2)}) collective-permute-start(bf16[64,4096]{1,0:T(8,128)(2,1)} %param.8), channel_id=1, source_target_pairs={{0,16},{2,18},{1,17},{3,19},{4,20},{6,22},{5,21},{7,23},{8,24},{10... | collective-permute-start | bytes 1572872 | tf_op jit(solution)/shard_map/ppermute | solution.py:48
  2.5 2.2 %collective-permute-start.4 = (bf16[64,4096]{1,0:T(8,128)(2,1)}, bf16[64,4096]{1,0:T(8,128)(2,1)}, u32[]{:S(2)}, u32[]{:S(2)}) collective-permute-start(bf16[64,4096]{1,0:T(8,128)(2,1)} %param.8), channel_id=1, source_target_pairs={{0,48},{2,50},{1,49},{3,51},{4,52},{6,54},{5,53},{7,55},{8,56},{10... | collective-permute-start | bytes 1572872 | tf_op jit(solution)/shard_map/ppermute | solution.py:48
  4.7 1.2 %collective-permute-start.2 = (bf16[80,4096]{1,0:T(8,128)(2,1)}, bf16[80,4096]{1,0:T(8,128)(2,1)S(1)}, u32[]{:S(2)}, u32[]{:S(2)}) collective-permute-start(bf16[80,4096]{1,0:T(8,128)(2,1)} %bitcast.21), channel_id=1, source_target_pairs={{0,2},{2,1},{1,3},{3,0},{4,6},{6,5},{5,7},{7,4},{8,10},{10,9},{9,1... | collective-permute-start | bytes 1966088 | tf_op jit(solution)/shard_map/ppermute | solution.py:48
  5.9 2.7 %collective-permute-start.1 = (bf16[80,4096]{1,0:T(8,128)(2,1)}, bf16[80,4096]{1,0:T(8,128)(2,1)S(1)}, u32[]{:S(2)}, u32[]{:S(2)}) collective-permute-start(bf16[80,4096]{1,0:T(8,128)(2,1)} %bitcast.22), channel_id=1, source_target_pairs={{0,12},{2,14},{1,13},{3,15},{4,0},{6,2},{5,1},{7,3},{8,4},{10,6},{... | collective-permute-start | bytes 1966088 | tf_op jit(solution)/shard_map/ppermute | solution.py:48
  8.6 0.0 collective-permute-start
  8.6 0.0 copy-done
  8.6 0.6 gather_fusion
  9.3 1.3 %gather_fusion.1 = s32[4]{0:T(128)S(1)} fusion(s32[256]{0:T(256)} %param.12, s32[1024]{0:T(1024)S(1)} %pad_clamp_fusion), kind=kCustom, calls=%fused_computation.1.clone | custom fusion | bytes 48 | tf_op jit(solution)/shard_map/jit(_take)/gather | solution.py:236
  10.6 0.1 add_convert_fusion
  10.8 0.1 convert_element_type.12
  10.9 0.8 dynamic-slice_convert_fusion
  11.6 0.1 stack.75.at_ref
  11.8 0.2 fusion
  12.0 0.1 pad_maximum_fusion.1
  12.1 4.4 %collective-permute-done.3 = bf16[64,4096]{1,0:T(8,128)(2,1)S(1)} collective-permute-done((bf16[64,4096]{1,0:T(8,128)(2,1)}, bf16[64,4096]{1,0:T(8,128)(2,1)S(1)}, u32[]{:S(2)}, u32[]{:S(2)}) %collective-permute-start.3) | collective-permute-done | bytes 524320 | tf_op jit(solution)/shard_map/ppermute | solution.py:48
  16.5 0.0 collective-permute-done.4
  16.5 4.9 %collective-permute-done.2.refs_1_ = bf16[80,4096]{1,0:T(8,128)(2,1)S(1)} collective-permute-done((bf16[80,4096]{1,0:T(8,128)(2,1)}, bf16[80,4096]{1,0:T(8,128)(2,1)S(1)}, u32[]{:S(2)}, u32[]{:S(2)}) %collective-permute-start.2) | collective-permute-done | bytes 655392 | tf_op jit(solution)/shard_map/ppermute | solution.py:48
  21.4 0.3 collective-permute-done.1.refs_4_
  21.7 3.0 %collective-permute-done.refs_2_ = bf16[80,4096]{1,0:T(8,128)(2,1)S(1)} collective-permute-done((bf16[80,4096]{1,0:T(8,128)(2,1)}, bf16[80,4096]{1,0:T(8,128)(2,1)S(1)}, u32[]{:S(2)}, u32[]{:S(2)}) %collective-permute-start) | collective-permute-done | bytes 655392 | tf_op jit(solution)/shard_map/ppermute | solution.py:48
  24.7 0.9 %collective-permute-start.5 = (bf16[64,4096]{1,0:T(8,128)(2,1)}, bf16[64,4096]{1,0:T(8,128)(2,1)S(1)}, u32[]{:S(2)}, u32[]{:S(2)}) collective-permute-start(bf16[64,4096]{1,0:T(8,128)(2,1)} %param.8), channel_id=1, source_target_pairs={{0,32},{2,34},{1,33},{3,35},{4,36},{6,38},{5,37},{7,39},{8,40},{10... | collective-permute-start | bytes 1572872 | tf_op jit(solution)/shard_map/ppermute | solution.py:48
  25.7 0.0 collective-permute-start.8
  25.7 1.5 %collective-permute-start.6 = (bf16[80,4096]{1,0:T(8,128)(2,1)S(1)}, bf16[80,4096]{1,0:T(8,128)(2,1)S(1)}, u32[]{:S(2)}, u32[]{:S(2)}) collective-permute-start(bf16[80,4096]{1,0:T(8,128)(2,1)S(1)} %collective-permute-done.refs_2_), channel_id=1, source_target_pairs={{0,3},{2,0},{1,2},{3,1},{4,7},{6,4},{5,6},{7,5},{8,11},{10,8},{9,1... | collective-permute-start | bytes 1966088 | tf_op jit(solution)/shard_map/ppermute | solution.py:48
  27.2 0.0 collective-permute-start.7
  27.2 10.2 %collective-permute-done.5 = bf16[64,4096]{1,0:T(8,128)(2,1)S(1)} collective-permute-done((bf16[64,4096]{1,0:T(8,128)(2,1)}, bf16[64,4096]{1,0:T(8,128)(2,1)S(1)}, u32[]{:S(2)}, u32[]{:S(2)}) %collective-permute-start.5) | collective-permute-done | bytes 524320 | tf_op jit(solution)/shard_map/ppermute | solution.py:48
  37.4 0.0 slice-start
  37.4 1.5 %pad_maximum_fusion.near = bf16[256,4096]{1,0:T(8,128)(2,1)S(1)} fusion(bf16[64,4096]{1,0:T(8,128)(2,1)S(1)} %collective-permute-done.5, bf16[64,4096]{1,0:T(8,128)(2,1)} %collective-permute-done.4, bf16[64,4096]{1,0:T(8,128)(2,1)S(1)} %collective-permute-done.3, bf16[64,4096]{1,0:T(8,128)(2,1)} %param.8), kind=kLoop, calls=%fused_computation.2 | loop fusion | flops 8388608 | bytes 4194304 | tf_op jit(solution)/shard_map/concatenate | solution.py:256
  38.9 0.0 slice-start.1
  38.9 1.5 %collective-permute-done.8.refs_2_ = bf16[80,4096]{1,0:T(8,128)(2,1)S(1)} collective-permute-done((bf16[80,4096]{1,0:T(8,128)(2,1)S(1)}, bf16[80,4096]{1,0:T(8,128)(2,1)S(1)}, u32[]{:S(2)}, u32[]{:S(2)}) %collective-permute-start.8) | collective-permute-done | bytes 655392 | tf_op jit(solution)/shard_map/ppermute | solution.py:48
  40.4 0.0 collective-permute-done.6.refs_3_
  40.4 0.9 %collective-permute-done.7.refs_5_ = bf16[80,4096]{1,0:T(8,128)(2,1)S(1)} collective-permute-done((bf16[80,4096]{1,0:T(8,128)(2,1)S(1)}, bf16[80,4096]{1,0:T(8,128)(2,1)S(1)}, u32[]{:S(2)}, u32[]{:S(2)}) %collective-permute-start.7) | collective-permute-done | bytes 655392 | tf_op jit(solution)/shard_map/ppermute | solution.py:48
  41.3 4.2 %collective-permute-start.9 = (bf16[256,4096]{1,0:T(8,128)(2,1)S(1)}, bf16[256,4096]{1,0:T(8,128)(2,1)S(1)}, u32[]{:S(2)}, u32[]{:S(2)}) collective-permute-start(bf16[256,4096]{1,0:T(8,128)(2,1)S(1)} %pad_maximum_fusion.near), channel_id=1, source_target_pairs={{0,64},{2,66},{1,65},{3,67},{4,68},{6,70},{5,69},{7,71},{8,72},{10... | collective-permute-start | bytes 6291464 | tf_op jit(solution)/shard_map/ppermute | solution.py:48
  45.5 0.9 %collective-permute-start.10 = (bf16[80,2048]{1,0:T(8,128)(2,1)S(1)}, bf16[80,2048]{1,0:T(8,128)(2,1)S(1)}, u32[]{:S(2)}, u32[]{:S(2)}) collective-permute-start(bf16[80,2048]{1,0:T(8,128)(2,1)S(1)} %slice.6), channel_id=1, source_target_pairs={{0,4},{2,6},{1,5},{3,7},{4,8},{6,10},{5,9},{7,11},{8,12},{10,14},{... | collective-permute-start | bytes 983048 | tf_op jit(solution)/shard_map/ppermute | solution.py:48
  46.4 1.8 %collective-permute-start.11 = (bf16[80,2048]{1,0:T(8,128)(2,1)S(1)}, bf16[80,2048]{1,0:T(8,128)(2,1)S(1)}, u32[]{:S(2)}, u32[]{:S(2)}) collective-permute-start(bf16[80,2048]{1,0:T(8,128)(2,1)S(1)} %slice.7), channel_id=1, source_target_pairs={{0,12},{2,14},{1,13},{3,15},{4,0},{6,2},{5,1},{7,3},{8,4},{10,6},{... | collective-permute-start | bytes 983048 | tf_op jit(solution)/shard_map/ppermute | solution.py:48
  48.2 1.1 %collective-permute-done.9.other = bf16[256,4096]{1,0:T(8,128)(2,1)S(1)} collective-permute-done((bf16[256,4096]{1,0:T(8,128)(2,1)S(1)}, bf16[256,4096]{1,0:T(8,128)(2,1)S(1)}, u32[]{:S(2)}, u32[]{:S(2)}) %collective-permute-start.9) | collective-permute-done | bytes 2097184 | tf_op jit(solution)/shard_map/ppermute | solution.py:48
  49.3 0.0 copy-done.1
  49.3 4.3 %project_first.1.total_ref = f32[512,640]{1,0:T(8,128)S(1)} custom-call(s32[18]{0:T(128)S(1)} %stack.75.at_ref, f32[1,640]{1,0:T(1,128)S(1)} %reshape.28.bias_ref, bf16[256,4096]{1,0:T(8,128)(2,1)S(1)} %pad_maximum_fusion.near, bf16[256,4096]{1,0:T(8,128)(2,1)S(1)} %collective-permute-done.9.other, bf16[80,4096]{1,0:T(8,128)(2,1)S(1)} %bitcast.24, ...), custom_call_target="tpu_custom_call" | custom-call | flops 2684354560 | bytes 9437184 | tf_op jit(solution)/shard_map/project_first/pallas_call | solution.py:109
  53.7 2.4 %collective-permute-done.10.refs_0_ = bf16[80,2048]{1,0:T(8,128)(2,1)S(1)} collective-permute-done((bf16[80,2048]{1,0:T(8,128)(2,1)S(1)}, bf16[80,2048]{1,0:T(8,128)(2,1)S(1)}, u32[]{:S(2)}, u32[]{:S(2)}) %collective-permute-start.10) | collective-permute-done | bytes 327712 | tf_op jit(solution)/shard_map/ppermute | solution.py:48
  56.1 0.0 collective-permute-done.11.refs_1_
  56.1 2.1 %project_last.1 = bf16[8,64,640]{2,1,0:T(8,128)(2,1)S(1)} custom-call(s32[18]{0:T(128)S(1)} %stack.75.at_ref, f32[512,640]{1,0:T(8,128)S(1)} %project_first.1.total_ref, bf16[256,4096]{1,0:T(8,128)(2,1)S(1)} %pad_maximum_fusion.near, bf16[256,4096]{1,0:T(8,128)(2,1)S(1)} %collective-permute-done.9.other, ...), custom_call_target="tpu_custom_call" | custom-call | flops 1073741824 | bytes 6291456 | tf_op jit(solution)/shard_map/project_last/pallas_call | solution.py:109
  58.2 14.9 %all_to_all.5.qkv = bf16[8,64,640]{2,1,0:T(8,128)(2,1)S(1)} all-to-all(bf16[8,64,640]{2,1,0:T(8,128)(2,1)S(1)} %project_last.1), channel_id=1, replica_groups=mesh['tp'=2,'z'=4,'y'=4,'xl'=2,'xh'=2] {'tp','z'}, dimensions={0} | all-to-all | bytes 1310720 | tf_op jit(solution)/shard_map/all_to_all | solution.py:286
  73.1 0.0 slice-done
  73.1 0.0 slice-done.1
  73.1 6.2 %attend.1 = bf16[64,4096]{1,0:T(8,128)(2,1)} custom-call(s32[4]{0:T(128)S(1)} %and_select_fusion.length_ref, f32[64,128]{1,0:T(8,128)S(1)} %get-tuple-element.24.cos_ref, f32[64,128]{1,0:T(8,128)S(1)} %get-tuple-element.25.sin_ref, bf16[8,64,640]{2,1,0:T(8,128)(2,1)S(1)} %all_to_all.5.qkv, bf16[4,1024,1024]{2,1,0:T(8,128)(2,1)S(1)} %bitcast.20), custom_call_target="tpu_custom_call" | custom-call | tf_op jit(solution)/shard_map/attend/pallas_call | solution.py:203
  (10 shorter events, 0.1 us)
Async XLA Ops:
  0.0 8.6 %copy-start = (s32[256]{0:T(256)S(1)}, s32[256]{0:T(256)}, u32[]{:S(2)}) copy-start(s32[256]{0:T(256)} %param.13) | copy-start | bytes 3076
  0.0 49.3 %copy-start.1 = (bf16[4096,80]{0,1:T(8,128)(2,1)S(1)}, bf16[4096,80]{0,1:T(8,128)(2,1)}, u32[]{:S(2)}) copy-start(bf16[4096,80]{0,1:T(8,128)(2,1)} %param.9) | copy-start | bytes 1966084
  0.0 16.4 %collective-permute-start.3 = (bf16[64,4096]{1,0:T(8,128)(2,1)}, bf16[64,4096]{1,0:T(8,128)(2,1)S(1)}, u32[]{:S(2)}, u32[]{:S(2)}) collective-permute-start(bf16[64,4096]{1,0:T(8,128)(2,1)} %param.8), channel_id=1, source_target_pairs={{0,16},{2,18},{1,17},{3,19},{4,20},{6,22},{5,21},{7,23},{8,24},{10... | collective-permute-start | bytes 1572872 | tf_op jit(solution)/shard_map/ppermute | solution.py:48
  2.5 14.0 %collective-permute-start.4 = (bf16[64,4096]{1,0:T(8,128)(2,1)}, bf16[64,4096]{1,0:T(8,128)(2,1)}, u32[]{:S(2)}, u32[]{:S(2)}) collective-permute-start(bf16[64,4096]{1,0:T(8,128)(2,1)} %param.8), channel_id=1, source_target_pairs={{0,48},{2,50},{1,49},{3,51},{4,52},{6,54},{5,53},{7,55},{8,56},{10... | collective-permute-start | bytes 1572872 | tf_op jit(solution)/shard_map/ppermute | solution.py:48
  4.7 16.7 %collective-permute-start.2 = (bf16[80,4096]{1,0:T(8,128)(2,1)}, bf16[80,4096]{1,0:T(8,128)(2,1)S(1)}, u32[]{:S(2)}, u32[]{:S(2)}) collective-permute-start(bf16[80,4096]{1,0:T(8,128)(2,1)} %bitcast.21), channel_id=1, source_target_pairs={{0,2},{2,1},{1,3},{3,0},{4,6},{6,5},{5,7},{7,4},{8,10},{10,9},{9,1... | collective-permute-start | bytes 1966088 | tf_op jit(solution)/shard_map/ppermute | solution.py:48
  5.9 15.8 %collective-permute-start.1 = (bf16[80,4096]{1,0:T(8,128)(2,1)}, bf16[80,4096]{1,0:T(8,128)(2,1)S(1)}, u32[]{:S(2)}, u32[]{:S(2)}) collective-permute-start(bf16[80,4096]{1,0:T(8,128)(2,1)} %bitcast.22), channel_id=1, source_target_pairs={{0,12},{2,14},{1,13},{3,15},{4,0},{6,2},{5,1},{7,3},{8,4},{10,6},{... | collective-permute-start | bytes 1966088 | tf_op jit(solution)/shard_map/ppermute | solution.py:48
  8.6 16.1 %collective-permute-start = (bf16[80,4096]{1,0:T(8,128)(2,1)}, bf16[80,4096]{1,0:T(8,128)(2,1)S(1)}, u32[]{:S(2)}, u32[]{:S(2)}) collective-permute-start(bf16[80,4096]{1,0:T(8,128)(2,1)} %bitcast.23), channel_id=1, source_target_pairs={{0,4},{2,6},{1,5},{3,7},{4,8},{6,10},{5,9},{7,11},{8,12},{10,14},{... | collective-permute-start | bytes 1966088 | tf_op jit(solution)/shard_map/ppermute | solution.py:48
  24.7 12.7 %collective-permute-start.5 = (bf16[64,4096]{1,0:T(8,128)(2,1)}, bf16[64,4096]{1,0:T(8,128)(2,1)S(1)}, u32[]{:S(2)}, u32[]{:S(2)}) collective-permute-start(bf16[64,4096]{1,0:T(8,128)(2,1)} %param.8), channel_id=1, source_target_pairs={{0,32},{2,34},{1,33},{3,35},{4,36},{6,38},{5,37},{7,39},{8,40},{10... | collective-permute-start | bytes 1572872 | tf_op jit(solution)/shard_map/ppermute | solution.py:48
  25.7 14.7 %collective-permute-start.8 = (bf16[80,4096]{1,0:T(8,128)(2,1)S(1)}, bf16[80,4096]{1,0:T(8,128)(2,1)S(1)}, u32[]{:S(2)}, u32[]{:S(2)}) collective-permute-start(bf16[80,4096]{1,0:T(8,128)(2,1)S(1)} %collective-permute-done.2.refs_1_), channel_id=1, source_target_pairs={{0,8},{2,10},{1,9},{3,11},{4,12},{6,14},{5,13},{7,15},{8,0},{10,2}... | collective-permute-start | bytes 1966088 | tf_op jit(solution)/shard_map/ppermute | solution.py:48
  25.7 14.7 %collective-permute-start.6 = (bf16[80,4096]{1,0:T(8,128)(2,1)S(1)}, bf16[80,4096]{1,0:T(8,128)(2,1)S(1)}, u32[]{:S(2)}, u32[]{:S(2)}) collective-permute-start(bf16[80,4096]{1,0:T(8,128)(2,1)S(1)} %collective-permute-done.refs_2_), channel_id=1, source_target_pairs={{0,3},{2,0},{1,2},{3,1},{4,7},{6,4},{5,6},{7,5},{8,11},{10,8},{9,1... | collective-permute-start | bytes 1966088 | tf_op jit(solution)/shard_map/ppermute | solution.py:48
  27.2 14.2 %collective-permute-start.7 = (bf16[80,4096]{1,0:T(8,128)(2,1)S(1)}, bf16[80,4096]{1,0:T(8,128)(2,1)S(1)}, u32[]{:S(2)}, u32[]{:S(2)}) collective-permute-start(bf16[80,4096]{1,0:T(8,128)(2,1)S(1)} %collective-permute-done.1.refs_4_), channel_id=1, source_target_pairs={{0,2},{2,1},{1,3},{3,0},{4,6},{6,5},{5,7},{7,4},{8,10},{10,9},{9,1... | collective-permute-start | bytes 1966088 | tf_op jit(solution)/shard_map/ppermute | solution.py:48
  37.4 35.7 %slice-start = ((s8[8388608]{0:T(1024)(128)(4,1)}), s8[4194304]{0:T(1024)(128)(4,1)S(1)}, s32[]{:S(2)}) async-start(s8[8388608]{0:T(1024)(128)(4,1)} %bitcast.19), calls=%async_computation.1 | async-start | bytes 8388608
  38.9 34.2 %slice-start.1 = ((s8[8388608]{0:T(1024)(128)(4,1)}), s8[4194304]{0:T(1024)(128)(4,1)S(1)}, s32[]{:S(2)}) async-start(s8[8388608]{0:T(1024)(128)(4,1)} %bitcast.19), calls=%async_computation.2 | async-start | bytes 8388608
  41.3 8.0 %collective-permute-start.9 = (bf16[256,4096]{1,0:T(8,128)(2,1)S(1)}, bf16[256,4096]{1,0:T(8,128)(2,1)S(1)}, u32[]{:S(2)}, u32[]{:S(2)}) collective-permute-start(bf16[256,4096]{1,0:T(8,128)(2,1)S(1)} %pad_maximum_fusion.near), channel_id=1, source_target_pairs={{0,64},{2,66},{1,65},{3,67},{4,68},{6,70},{5,69},{7,71},{8,72},{10... | collective-permute-start | bytes 6291464 | tf_op jit(solution)/shard_map/ppermute | solution.py:48
  45.5 10.6 %collective-permute-start.10 = (bf16[80,2048]{1,0:T(8,128)(2,1)S(1)}, bf16[80,2048]{1,0:T(8,128)(2,1)S(1)}, u32[]{:S(2)}, u32[]{:S(2)}) collective-permute-start(bf16[80,2048]{1,0:T(8,128)(2,1)S(1)} %slice.6), channel_id=1, source_target_pairs={{0,4},{2,6},{1,5},{3,7},{4,8},{6,10},{5,9},{7,11},{8,12},{10,14},{... | collective-permute-start | bytes 983048 | tf_op jit(solution)/shard_map/ppermute | solution.py:48
  46.4 9.7 %collective-permute-start.11 = (bf16[80,2048]{1,0:T(8,128)(2,1)S(1)}, bf16[80,2048]{1,0:T(8,128)(2,1)S(1)}, u32[]{:S(2)}, u32[]{:S(2)}) collective-permute-start(bf16[80,2048]{1,0:T(8,128)(2,1)S(1)} %slice.7), channel_id=1, source_target_pairs={{0,12},{2,14},{1,13},{3,15},{4,0},{6,2},{5,1},{7,3},{8,4},{10,6},{... | collective-permute-start | bytes 983048 | tf_op jit(solution)/shard_map/ppermute | solution.py:48

commit v5 on v4

--- a/solution.py
+++ b/solution.py
@@ -27,9 +27,10 @@
 NEAR = 4 * ROWS
 WINDOW = 256
 CHUNK = 256
-PROJECT_VMEM = 20 * 1024 * 1024
-ATTEND_VMEM = 16 * 1024 * 1024
+PROJECT_VMEM = 14 * 1024 * 1024
+ATTEND_VMEM = 8 * 1024 * 1024
 NT = (((1,), (1,)), ((), ()))
+HOME = [(0, 2), (1, 2), (0, 1), (1, 1), (0, 3), (1, 3), (1, 0), (0, 0)]
 
 
 def device_index(t, z, y, x):
@@ -48,34 +49,61 @@
     return lax.ppermute(array, AXES, pairs)
 
 
+def copy_rows_kernel(rows, early, out, sem):
+    copy = pltpu.make_async_copy(rows, out, sem)
+    copy.start()
+    copy.wait()
+
+
+def copy_rows(rows, early):
+    return pl.pallas_call(
+        copy_rows_kernel,
+        in_specs=[pl.BlockSpec(memory_space=pltpu.HBM), pl.BlockSpec(memory_space=pl.ANY)],
+        out_specs=pl.BlockSpec(memory_space=pltpu.VMEM),
+        out_shape=jax.ShapeDtypeStruct((ROWS, D), jnp.bfloat16),
+        scratch_shapes=[pltpu.SemaphoreType.DMA],
+        compiler_params=pltpu.CompilerParams(vmem_limit_bytes=8 * 1024 * 1024),
+        name="copy_rows",
+    )(rows, early)
+
+
 def gather(pieces, where, at_ref, weights):
     for piece, (place, low) in zip(pieces, where):
         start = pl.multiple_of(at_ref[place], 16)
         weights[pl.ds(start, COLS), low : low + piece.shape[1]] = piece[...]
 
 
-def multiply(near, other, weights):
+def multiply(rows, weights):
     return [
-        lax.dot_general(rows[...], weights[...], NT, preferred_element_type=jnp.float32)
-        for rows in (near, other)
+        lax.dot_general(
+            rows[low : low + NEAR, :],
+            weights[...],
+            NT,
+            preferred_element_type=jnp.float32,
+        )
+        for low in (0, NEAR)
     ]
 
 
-def project_first_kernel(where, at_ref, bias_ref, near, other, *refs):
-    pieces = refs[:-2]
-    out, weights = refs[-2:]
-    start = pl.multiple_of(at_ref[16], 16)
+def project_first_kernel(where, at_ref, bias_ref, *refs):
+    pieces, blocks = refs[:-7], refs[-7:-3]
+    out, rows, weights = refs[-3:]
+    start = pl.multiple_of(at_ref[8], 16)
     weights[pl.ds(start, 2 * COLS), :] = jnp.zeros((2 * COLS, D), jnp.bfloat16)
     gather(pieces, where, at_ref, weights)
-    first, second = multiply(near, other, weights)
+    low = 0
+    for block in blocks:
+        rows[low : low + block.shape[0], :] = block[...]
+        low += block.shape[0]
+    first, second = multiply(rows, weights)
     out[:NEAR] = first + bias_ref[...]
     out[NEAR:] = second + bias_ref[...]
 
 
-def project_last_kernel(where, at_ref, total_ref, near, other, *refs):
-    pieces = refs[:-2]
-    out, weights = refs[-2:]
-    shift_by = at_ref[17]
+def project_last_kernel(where, at_ref, total_ref, *refs):
+    pieces, rows = refs[:-10], refs[-10]
+    outs, weights = refs[-9:-1], refs[-1]
+    shift_by = at_ref[9]
     for k in range(4):
 
         @pl.when(shift_by == 2 * k * STRETCH)
@@ -87,30 +115,30 @@
                 weights[high:, :] = jnp.zeros((WINDOW - high, D), jnp.bfloat16)
 
     gather(pieces, where, at_ref, weights)
-    total = multiply(near, other, weights)
+    total = multiply(rows, weights)
     for k in range(4):
 
         @pl.when(shift_by == 2 * k * STRETCH)
         def _():
             low, high = k * HD, k * HD + WINDOW
             for block in range(8):
-                rows = slice(block * ROWS, (block + 1) * ROWS)
+                span = slice(block * ROWS, (block + 1) * ROWS)
                 here = slice(block % 4 * ROWS, (block % 4 + 1) * ROWS)
-                done = total_ref[rows, low:high] + total[block // 4][here]
-                home = at_ref[8 + block]
-                out[home, :, low:high] = done.astype(jnp.bfloat16)
+                done = total_ref[span, low:high] + total[block // 4][here]
+                out = outs[HOME.index((block // 4, (0, 1, 3, 2)[block % 4]))]
+                out[:, low:high] = done.astype(jnp.bfloat16)
                 if low:
-                    out[home, :, :low] = total_ref[rows, :low].astype(jnp.bfloat16)
+                    out[:, :low] = total_ref[span, :low].astype(jnp.bfloat16)
                 if high < WIDE:
-                    out[home, :, high:] = total_ref[rows, high:].astype(jnp.bfloat16)
-
-
-def project(kernel, width, out_shape, places, whole, near, other, pieces, where):
+                    out[:, high:] = total_ref[span, high:].astype(jnp.bfloat16)
+
+
+def project(kernel, width, out_shape, places, whole, operands, where):
+    vmem = pl.BlockSpec(memory_space=pltpu.VMEM)
     return pl.pallas_call(
         functools.partial(kernel, where),
-        in_specs=[pl.BlockSpec(memory_space=pltpu.SMEM)]
-        + [pl.BlockSpec(memory_space=pltpu.VMEM)] * (len(pieces) + 3),
-        out_specs=pl.BlockSpec(memory_space=pltpu.VMEM),
+        in_specs=[pl.BlockSpec(memory_space=pltpu.SMEM)] + [vmem] * (len(operands) + 1),
+        out_specs=jax.tree.map(lambda _: vmem, out_shape),
         out_shape=out_shape,
         scratch_shapes=[pltpu.VMEM((width, D), jnp.bfloat16)],
         compiler_params=pltpu.CompilerParams(vmem_limit_bytes=PROJECT_VMEM),
@@ -120,10 +148,13 @@
             transcendentals=0,
         ),
         name=kernel.__name__.removesuffix("_kernel"),
-    )(places, whole, near, other, *pieces)
-
-
-def attend_kernel(length_ref, cos_ref, sin_ref, qkv, cache, out_ref, scores):
+    )(places, whole, *operands)
+
+
+def attend_kernel(group_ref, length_ref, cos_ref, sin_ref, cache, *refs):
+    blocks, out_ref, qkv, scores = refs[:8], *refs[8:]
+    for i, block in enumerate(blocks):
+        qkv[group_ref[i]] = block[...]
     scale = HD ** (-0.5) * LOG2E
     key_at = lax.broadcasted_iota(jnp.int32, (1, CAP), 1)
     token = lax.broadcasted_iota(jnp.int32, (GROUP * STRETCH, STRETCH), 0) % STRETCH
@@ -199,17 +230,20 @@
     mix(*ahead)
 
 
-def attend(lengths, cosine, sine, qkv, cache):
+def attend(groups, lengths, cosine, sine, cache, blocks):
     return pl.pallas_call(
         attend_kernel,
-        in_specs=[pl.BlockSpec(memory_space=pltpu.SMEM)]
-        + [pl.BlockSpec(memory_space=pltpu.VMEM)] * 4,
+        in_specs=[pl.BlockSpec(memory_space=pltpu.SMEM)] * 2
+        + [pl.BlockSpec(memory_space=pltpu.VMEM)] * 11,
         out_specs=pl.BlockSpec(memory_space=pltpu.VMEM),
         out_shape=jax.ShapeDtypeStruct((ROWS, HQ * HD), jnp.bfloat16),
-        scratch_shapes=[pltpu.VMEM((2, GROUP * STRETCH, CAP), jnp.float32)],
+        scratch_shapes=[
+            pltpu.VMEM((8, ROWS, WIDE), jnp.bfloat16),
+            pltpu.VMEM((2, GROUP * STRETCH, CAP), jnp.float32),
+        ],
         compiler_params=pltpu.CompilerParams(vmem_limit_bytes=ATTEND_VMEM),
         name="attend",
-    )(lengths, cosine, sine, qkv, cache)
+    )(groups, lengths, cosine, sine, cache, *blocks)
 
 
 def on_device(tokens, weight, bias, cache, lengths, slot_stream):
@@ -220,15 +254,23 @@
     group = t * 4 + z
     index = (group * 4 + y) * 2 + xl
 
+    own = weight.T
+    own_side, three, one = shift(own, dx=1), shift(own, dy=3), shift(own, dy=1)
+    early = shift(jnp.zeros((16, HD), jnp.bfloat16), dt=1)
+    late = copy_rows(tokens, early)
+    late, bias, lengths, slot_stream = lax.optimization_barrier(
+        (late, bias, lengths, slot_stream)
+    )
+
     far_y = (y + 2) % 4
     places = []
     for dy in range(4):
         base = far_y * 2 * STRETCH if dy == 2 else (y - dy) % 4 * 2 * COLS
         places += [base + xl * COLS, base + (1 - xl) * COLS]
-    for core in (t, 1 - t):
-        places += [core * 4 + (z - dz) % 4 for dz in (0, 1, 3, 2)]
     places += [far_y * 2 * COLS, far_y * 2 * STRETCH]
     places = jnp.stack(places).astype(jnp.int32)
+    groups = [(t + dt) % 2 * 4 + (z + dz) % 4 for dt, dz in HOME]
+    groups = jnp.stack(groups).astype(jnp.int32)
     bias_cols = lax.dynamic_slice_in_dim(bias, group * WIDE, WIDE, 0)
     bias_cols = bias_cols.astype(jnp.float32)[None, :]
 
@@ -243,48 +285,49 @@
     cosine = jnp.concatenate([cosine, cosine], axis=1)
     sine = jnp.concatenate([-sine, sine], axis=1)
 
-    own = weight.T
-    one, three, own_side = shift(own, dy=1), shift(own, dy=3), shift(own, dx=1)
-    up, down = shift(tokens, dz=1), shift(tokens, dz=3)
-    one, three, own_side, up, down, tokens, small = lax.optimization_barrier(
-        (one, three, own_side, up, down, tokens, (places, bias_cols, my_lengths, cosine, sine))
-    )
-    places, bias_cols, my_lengths, cosine, sine = small
+    up, down = shift(late, dz=1), shift(late, dz=3)
+    own_side, three, one, tokens, late, small = lax.optimization_barrier(
+        (own_side, three, one, tokens, late, (places, groups, bias_cols, my_lengths, cosine, sine))
+    )
+    places, groups, bias_cols, my_lengths, cosine, sine = small
+    far = shift(late, dz=2)
+    one_side, three_side = shift(one, dx=3), shift(three, dx=1)
     two_side = shift(own_side, dy=2)
-    one_side, three_side = shift(one, dx=3), shift(three, dx=1)
-    far = shift(tokens, dz=2)
-    near = jnp.concatenate([tokens, up, down, far])
+    near = jnp.concatenate([tokens, up, down])
     low, high = one[:, :HALF], three[:, HALF:]
-    near, one_side, three_side, two_side, low, high = lax.optimization_barrier(
-        (near, one_side, three_side, two_side, low, high)
+    two_side, one_side, three_side, far, near, low, high = lax.optimization_barrier(
+        (two_side, one_side, three_side, far, near, low, high)
     )
     two_low, two_high = shift(low, dy=1), shift(high, dy=3)
     other = shift(near, dt=1)
-
-    total = project(
+    other_far = shift(far, dt=1)
+
+    total, rows = project(
         project_first_kernel,
         WIDE,
-        jax.ShapeDtypeStruct((2 * NEAR, WIDE), jnp.float32),
+        [
+            jax.ShapeDtypeStruct((2 * NEAR, WIDE), jnp.float32),
+            jax.ShapeDtypeStruct((2 * NEAR, D), jnp.bfloat16),
+        ],
         places,
         bias_cols,
-        near,
-        other,
-        [own, own_side, one, one_side, three, three_side],
+        [own, own_side, one, one_side, three, three_side, near, far, other, other_far],
         tuple((place, 0) for place in (0, 1, 2, 3, 6, 7)),
     )
     parts = project(
         project_last_kernel,
         WINDOW,
-        jax.ShapeDtypeStruct((8, ROWS, WIDE), jnp.bfloat16),
+        [jax.ShapeDtypeStruct((ROWS, WIDE), jnp.bfloat16)] * 8,
         places,
         total,
-        near,
-        other,
-        [two_low, two_high, two_side],
+        [two_low, two_high, two_side, rows],
         ((4, 0), (4, HALF), (5, 0)),
     )
-    qkv = lax.all_to_all(parts, ("tp", "z"), split_axis=0, concat_axis=0, tiled=True)
-    return attend(my_lengths, cosine, sine, qkv, cache)
+    blocks = [
+        shift(part, dt=-dt, dz=-dz) if dt or dz else part
+        for part, (dt, dz) in zip(parts, HOME)
+    ]
+    return attend(groups, my_lengths, cosine, sine, cache, blocks)
 
 
 def solution(mesh):

time: 79.5 us -> 75.6 us (0.951)
  blocking collectives: 14.9 us -> 0 us
  starting transfers between devices: 17.9 us -> 29.8 us
  waiting for transfers between devices: 28.8 us -> 19.9 us
  local copies, waits for them, and re-layouts: 2.21 us -> 6.43 us
  other arithmetic: 2.66 us -> 6.07 us
    all_to_all x1 -> x0, blocking collectives: 14.9 us -> none  [on_device(): lax.all_to_all(parts, ('tp', 'z'), split_axis=0, concat_axis=0, tiled=True)]
    ppermute x12 -> x21, starting transfers between devices: 17.9 us -> 29.8 us  [shift(): return lax.ppermute(array, AXES, pairs)]
    ppermute x12 -> x21, waiting for transfers between devices: 28.8 us -> 19.9 us  [shift(): return lax.ppermute(array, AXES, pairs)]
    unnamed x8 -> x14, local copies, waits for them, and re-layouts: 0.02 us -> 1.64 us
    convert_element_type x1, local copies, waits for them, and re-layouts: 0.08 us -> 1.3 us  [on_device(): angles = positions.astype(jnp.float32)[:, None] * frequency[None, :]]
  transfers between devices with their start and end apart: 12 -> 21, of which waited for: 9 -> 9; matrix products, arithmetic and copies ran while one was open for 6% -> 14% of each run, Pallas kernels for 5% -> 7%
where the time goes in v5:
time: 75.6 us; the launch traced here: 75.3 us
  starting transfers between devices  29.8 us (39%)
  waiting for transfers between devices  19.9 us (26%)
  Pallas kernels  12.9 us (17%)
  local copies, waits for them, and re-layouts  6.43 us (9%)
  other arithmetic  6.07 us (8%)
    ppermute x21, starting transfers between devices, shift(): return lax.ppermute(array, AXES, pairs)  29.8 us
    ppermute x21, waiting for transfers between devices, shift(): return lax.ppermute(array, AXES, pairs)  19.9 us
    pallas_call x2, Pallas kernels, project(): pl.pallas_call(functools.partial(kernel, where), in_specs=[pl.BlockSpec(m...  7.03 us
    pallas_call x1, Pallas kernels, attend(): pl.pallas_call(attend_kernel, in_specs=[pl.BlockSpec(memory_space=pltpu.S...  5.87 us
    gather x1, local copies, waits for them, and re-layouts, on_device(): jnp.take(lengths, jnp.take(slot_stream, my_slots)).astype(jnp.int32)  1.82 us
    unnamed x14, local copies, waits for them, and re-layouts  1.64 us
  transfers between devices with their start and end apart: 21, of which 9 were waited for; matrix products, arithmetic and copies ran while one was open for 14% of the time, Pallas kernels for 7%

profile of v5, /device:TPU:1, one launch (start us, length us, event | category | flops | bytes accessed | tf_op | source)
XLA Modules:
  0.0 75.3 jit_solution(5760079840055267953)
XLA Ops:
  0.0 2.1 %collective-permute-start.2 = (bf16[80,4096]{1,0:T(8,128)(2,1)}, bf16[80,4096]{1,0:T(8,128)(2,1)S(1)}, u32[]{:S(2)}, u32[]{:S(2)}) collective-permute-start(bf16[80,4096]{1,0:T(8,128)(2,1)} %bitcast.21), channel_id=1, source_target_pairs={{0,4},{2,6},{1,5},{3,7},{4,8},{6,10},{5,9},{7,11},{8,12},{10,14},{... | collective-permute-start | bytes 1966088 | tf_op jit(solution)/shard_map/ppermute | solution.py:49
  2.1 1.5 %collective-permute-start.1 = (bf16[80,4096]{1,0:T(8,128)(2,1)}, bf16[80,4096]{1,0:T(8,128)(2,1)S(1)}, u32[]{:S(2)}, u32[]{:S(2)}) collective-permute-start(bf16[80,4096]{1,0:T(8,128)(2,1)} %bitcast.22), channel_id=1, source_target_pairs={{0,12},{2,14},{1,13},{3,15},{4,0},{6,2},{5,1},{7,3},{8,4},{10,6},{... | collective-permute-start | bytes 1966088 | tf_op jit(solution)/shard_map/ppermute | solution.py:49
  3.6 1.2 %collective-permute-start = (bf16[80,4096]{1,0:T(8,128)(2,1)}, bf16[80,4096]{1,0:T(8,128)(2,1)}, u32[]{:S(2)}, u32[]{:S(2)}) collective-permute-start(bf16[80,4096]{1,0:T(8,128)(2,1)} %bitcast.23), channel_id=1, source_target_pairs={{0,2},{2,1},{1,3},{3,0},{4,6},{6,5},{5,7},{7,4},{8,10},{10,9},{9,1... | collective-permute-start | bytes 1966088 | tf_op jit(solution)/shard_map/ppermute | solution.py:49
  4.9 1.4 %collective-permute-start.3 = (bf16[16,128]{1,0:T(8,128)(2,1)S(1)}, bf16[16,128]{1,0:T(8,128)(2,1)S(1)}, u32[]{:S(2)}, u32[]{:S(2)}) collective-permute-start(bf16[16,128]{1,0:T(8,128)(2,1)S(1)} %broadcast_in_dim.16), channel_id=1, source_target_pairs={{0,64},{2,66},{1,65},{3,67},{4,68},{6,70},{5,69},{7,71},{8,72},{10... | collective-permute-start | bytes 12296 | tf_op jit(solution)/shard_map/ppermute | solution.py:49
  6.2 0.5 multiply_power_fusion
  6.7 0.6 pad_clamp_fusion.1
  7.3 0.1 stack.79.group_ref
  7.4 0.1 stack.70.at_ref
  7.5 0.0 collective-permute-done.3.early
  7.5 0.0 copy-start.1
  7.5 1.0 %copy-done.1 = bf16[64,4096]{1,0:T(8,128)(2,1)S(1)} copy-done((bf16[64,4096]{1,0:T(8,128)(2,1)S(1)}, bf16[64,4096]{1,0:T(8,128)(2,1)}, u32[]{:S(2)}) %copy-start.1) | copy-done | bytes 524312
  8.6 0.0 copy-start.3
  8.6 3.8 %collective-permute-start.9 = (bf16[64,4096]{1,0:T(8,128)(2,1)S(1)}, bf16[64,4096]{1,0:T(8,128)(2,1)S(1)}, u32[]{:S(2)}, u32[]{:S(2)}) collective-permute-start(bf16[64,4096]{1,0:T(8,128)(2,1)S(1)} %copy_rows.1), channel_id=1, source_target_pairs={{0,48},{2,50},{1,49},{3,51},{4,52},{6,54},{5,53},{7,55},{8,56},{10... | collective-permute-start | bytes 1572872 | tf_op jit(solution)/shard_map/ppermute | solution.py:49
  12.5 0.0 collective-permute-start.8
  12.5 0.8 %gather_fusion = s32[4]{0:T(128)S(1)} fusion(s32[256]{0:T(256)S(1)} %copy-done, s32[1024]{0:T(1024)} %pad_clamp_fusion.1), kind=kCustom, calls=%fused_computation.clone | custom fusion | bytes 48 | tf_op jit(solution)/shard_map/jit(_take)/gather | solution.py:278
  13.2 0.6 copy-done.4
  13.8 1.8 %gather_fusion.1 = s32[4]{0:T(128)} fusion(s32[256]{0:T(256)} %param.12, s32[1024]{0:T(1024)S(1)} %pad_clamp_fusion), kind=kCustom, calls=%fused_computation.1.clone | custom fusion | bytes 48 | tf_op jit(solution)/shard_map/jit(_take)/gather | solution.py:278
  15.6 0.7 and_select_fusion.length_ref
  16.3 0.7 add_convert_fusion
  17.0 1.4 %dynamic-slice_convert_fusion = f32[640]{0:T(1024)} fusion(bf16[5120]{0:T(1024)(128)(2,1)} %param.10, s32[]{:T(128)S(6)} %select_n.83), kind=kLoop, calls=%fused_computation.13 | loop fusion | flops 640 | bytes 3844 | tf_op jit(solution)/shard_map/broadcast_in_dim | solution.py:275
  18.4 1.3 %convert_element_type.12 = f32[64]{0:T(128)} reshape(f32[4,16]{1,0:T(4,128)} %add_convert_fusion) | data formatting | bytes 512 | tf_op jit(solution)/shard_map/convert_element_type | solution.py:283
  19.7 0.7 reshape.28.bias_ref
  20.3 0.8 %fusion = (f32[64,64]{1,0:T(8,128)S(1)}, f32[64,64]{1,0:T(8,128)S(1)}, f32[64,64]{1,0:T(8,128)S(1)}) fusion(f32[64]{0:T(128)} %multiply_power_fusion, f32[64]{0:T(128)} %convert_element_type.12), kind=kLoop, calls=%fused_computation.7 | loop fusion | flops 8192 | bytes 49664 | tf_op jit(solution)/shard_map/neg | solution.py:286
  21.2 0.1 pad_maximum_fusion.1
  21.3 0.0 collective-permute-done.2.refs_2_
  21.3 0.0 collective-permute-done.1.refs_4_
  21.3 0.0 collective-permute-done.refs_1_
  21.3 1.8 %collective-permute-start.4 = (bf16[80,4096]{1,0:T(8,128)(2,1)}, bf16[80,4096]{1,0:T(8,128)(2,1)S(1)}, u32[]{:S(2)}, u32[]{:S(2)}) collective-permute-start(bf16[80,4096]{1,0:T(8,128)(2,1)} %collective-permute-done.refs_1_), channel_id=1, source_target_pairs={{0,8},{2,10},{1,9},{3,11},{4,12},{6,14},{5,13},{7,15},{8,0},{10,2}... | collective-permute-start | bytes 1966088 | tf_op jit(solution)/shard_map/ppermute | solution.py:49
  23.1 1.5 %collective-permute-start.5 = (bf16[80,4096]{1,0:T(8,128)(2,1)S(1)}, bf16[80,4096]{1,0:T(8,128)(2,1)S(1)}, u32[]{:S(2)}, u32[]{:S(2)}) collective-permute-start(bf16[80,4096]{1,0:T(8,128)(2,1)S(1)} %collective-permute-done.2.refs_2_), channel_id=1, source_target_pairs={{0,3},{2,0},{1,2},{3,1},{4,7},{6,4},{5,6},{7,5},{8,11},{10,8},{9,1... | collective-permute-start | bytes 1966088 | tf_op jit(solution)/shard_map/ppermute | solution.py:49
  24.5 0.0 collective-permute-start.6
  24.5 0.0 collective-permute-done.9
  24.6 2.2 %collective-permute-start.7 = (bf16[64,4096]{1,0:T(8,128)(2,1)S(1)}, bf16[64,4096]{1,0:T(8,128)(2,1)S(1)}, u32[]{:S(2)}, u32[]{:S(2)}) collective-permute-start(bf16[64,4096]{1,0:T(8,128)(2,1)S(1)} %copy_rows.1), channel_id=1, source_target_pairs={{0,32},{2,34},{1,33},{3,35},{4,36},{6,38},{5,37},{7,39},{8,40},{10... | collective-permute-start | bytes 1572872 | tf_op jit(solution)/shard_map/ppermute | solution.py:49
  26.9 0.2 collective-permute-done.8
  27.0 1.3 %pad_maximum_fusion.refs_6_ = bf16[192,4096]{1,0:T(8,128)(2,1)S(1)} fusion(bf16[64,4096]{1,0:T(8,128)(2,1)S(1)} %collective-permute-done.9, bf16[64,4096]{1,0:T(8,128)(2,1)} %collective-permute-done.8, bf16[64,4096]{1,0:T(8,128)(2,1)S(1)} %copy-done.2), kind=kLoop, calls=%fused_computation.2 | loop fusion | flops 4718592 | bytes 3145728 | tf_op jit(solution)/shard_map/concatenate | solution.py:296
  28.4 0.0 slice-start.1
  28.4 9.1 %collective-permute-done.7.refs_7_ = bf16[64,4096]{1,0:T(8,128)(2,1)S(1)} collective-permute-done((bf16[64,4096]{1,0:T(8,128)(2,1)S(1)}, bf16[64,4096]{1,0:T(8,128)(2,1)S(1)}, u32[]{:S(2)}, u32[]{:S(2)}) %collective-permute-start.7) | collective-permute-done | bytes 524320 | tf_op jit(solution)/shard_map/ppermute | solution.py:49
  37.5 0.9 %collective-permute-done.4.refs_2_ = bf16[80,4096]{1,0:T(8,128)(2,1)S(1)} collective-permute-done((bf16[80,4096]{1,0:T(8,128)(2,1)}, bf16[80,4096]{1,0:T(8,128)(2,1)S(1)}, u32[]{:S(2)}, u32[]{:S(2)}) %collective-permute-start.4) | collective-permute-done | bytes 655392 | tf_op jit(solution)/shard_map/ppermute | solution.py:49
  38.4 0.0 collective-permute-done.5.refs_3_
  38.4 2.4 %collective-permute-done.6.refs_5_ = bf16[80,4096]{1,0:T(8,128)(2,1)S(1)} collective-permute-done((bf16[80,4096]{1,0:T(8,128)(2,1)S(1)}, bf16[80,4096]{1,0:T(8,128)(2,1)S(1)}, u32[]{:S(2)}, u32[]{:S(2)}) %collective-permute-start.6) | collective-permute-done | bytes 655392 | tf_op jit(solution)/shard_map/ppermute | solution.py:49
  40.8 2.1 %collective-permute-start.10 = (bf16[192,4096]{1,0:T(8,128)(2,1)S(1)}, bf16[192,4096]{1,0:T(8,128)(2,1)S(1)}, u32[]{:S(2)}, u32[]{:S(2)}) collective-permute-start(bf16[192,4096]{1,0:T(8,128)(2,1)S(1)} %pad_maximum_fusion.refs_6_), channel_id=1, source_target_pairs={{0,64},{2,66},{1,65},{3,67},{4,68},{6,70},{5,69},{7,71},{8,72},{10... | collective-permute-start | bytes 4718600 | tf_op jit(solution)/shard_map/ppermute | solution.py:49
  42.9 0.0 collective-permute-start.11
  42.9 0.4 collective-permute-start.12
  43.3 2.3 %collective-permute-start.13 = (bf16[80,2048]{1,0:T(8,128)(2,1)S(1)}, bf16[80,2048]{1,0:T(8,128)(2,1)S(1)}, u32[]{:S(2)}, u32[]{:S(2)}) collective-permute-start(bf16[80,2048]{1,0:T(8,128)(2,1)S(1)} %slice.7), channel_id=1, source_target_pairs={{0,12},{2,14},{1,13},{3,15},{4,0},{6,2},{5,1},{7,3},{8,4},{10,6},{... | collective-permute-start | bytes 983048 | tf_op jit(solution)/shard_map/ppermute | solution.py:49
  45.6 1.1 %collective-permute-done.11.refs_9_ = bf16[64,4096]{1,0:T(8,128)(2,1)S(1)} collective-permute-done((bf16[64,4096]{1,0:T(8,128)(2,1)S(1)}, bf16[64,4096]{1,0:T(8,128)(2,1)S(1)}, u32[]{:S(2)}, u32[]{:S(2)}) %collective-permute-start.11) | collective-permute-done | bytes 524320 | tf_op jit(solution)/shard_map/ppermute | solution.py:49
  46.7 0.0 collective-permute-done.10.refs_8_
  46.7 4.9 %project_first.1 = (f32[512,640]{1,0:T(8,128)S(1)}, bf16[512,4096]{1,0:T(8,128)(2,1)S(1)}) custom-call(s32[10]{0:T(128)S(1)} %stack.70.at_ref, f32[1,640]{1,0:T(1,128)S(1)} %reshape.28.bias_ref, bf16[80,4096]{1,0:T(8,128)(2,1)S(1)} %bitcast.24, bf16[80,4096]{1,0:T(8,128)(2,1)} %collective-permute-done.refs_1_, ...), custom_call_target="tpu_custom_call" | custom-call | flops 2684354560 | bytes 9437184 | tf_op jit(solution)/shard_map/project_first/pallas_call | solution.py:138
  51.6 1.2 %collective-permute-done.12.refs_0_ = bf16[80,2048]{1,0:T(8,128)(2,1)S(1)} collective-permute-done((bf16[80,2048]{1,0:T(8,128)(2,1)S(1)}, bf16[80,2048]{1,0:T(8,128)(2,1)S(1)}, u32[]{:S(2)}, u32[]{:S(2)}) %collective-permute-start.12) | collective-permute-done | bytes 327712 | tf_op jit(solution)/shard_map/ppermute | solution.py:49
  52.9 0.0 collective-permute-done.13.refs_1_
  52.9 2.1 %project_last.1 = (bf16[64,640]{1,0:T(8,128)(2,1)S(1)}, bf16[64,640]{1,0:T(8,128)(2,1)S(1)}, bf16[64,640]{1,0:T(8,128)(2,1)S(1)}, bf16[64,640]{1,0:T(8,128)(2,1)...) custom-call(s32[10]{0:T(128)S(1)} %stack.70.at_ref, ...), custom_call_target="tpu_custom_call" | custom-call | flops 1073741824 | bytes 6291456 | tf_op jit(solution)/shard_map/project_last/pallas_call | solution.py:138
  55.0 2.1 %collective-permute-start.14 = (bf16[64,640]{1,0:T(8,128)(2,1)S(1)}, bf16[64,640]{1,0:T(8,128)(2,1)S(1)}, u32[]{:S(2)}, u32[]{:S(2)}) collective-permute-start(bf16[64,640]{1,0:T(8,128)(2,1)S(1)} %get-tuple-element.62), channel_id=1, source_target_pairs={{0,32},{2,34},{1,33},{3,35},{4,36},{6,38},{5,37},{7,39},{8,40},{10... | collective-permute-start | bytes 245768 | tf_op jit(solution)/shard_map/ppermute | solution.py:49
  57.1 2.5 %collective-permute-start.15 = (bf16[64,640]{1,0:T(8,128)(2,1)S(1)}, bf16[64,640]{1,0:T(8,128)(2,1)S(1)}, u32[]{:S(2)}, u32[]{:S(2)}) collective-permute-start(bf16[64,640]{1,0:T(8,128)(2,1)S(1)} %get-tuple-element.63), channel_id=1, source_target_pairs={{0,96},{2,98},{1,97},{3,99},{4,100},{6,102},{5,101},{7,103},{8,104... | collective-permute-start | bytes 245768 | tf_op jit(solution)/shard_map/ppermute | solution.py:49
  59.6 2.7 %collective-permute-start.16 = (bf16[64,640]{1,0:T(8,128)(2,1)S(1)}, bf16[64,640]{1,0:T(8,128)(2,1)S(1)}, u32[]{:S(2)}, u32[]{:S(2)}) collective-permute-start(bf16[64,640]{1,0:T(8,128)(2,1)S(1)} %get-tuple-element.64), channel_id=1, source_target_pairs={{0,48},{2,50},{1,49},{3,51},{4,52},{6,54},{5,53},{7,55},{8,56},{10... | collective-permute-start | bytes 245768 | tf_op jit(solution)/shard_map/ppermute | solution.py:49
  62.2 0.0 collective-permute-start.17
  62.2 0.5 collective-permute-start.18
  62.7 0.0 collective-permute-done.14.refs_0_
  62.7 1.3 %collective-permute-start.19 = (bf16[64,640]{1,0:T(8,128)(2,1)S(1)}, bf16[64,640]{1,0:T(8,128)(2,1)S(1)}, u32[]{:S(2)}, u32[]{:S(2)}) collective-permute-start(bf16[64,640]{1,0:T(8,128)(2,1)S(1)} %get-tuple-element.67), channel_id=1, source_target_pairs={{0,80},{2,82},{1,81},{3,83},{4,84},{6,86},{5,85},{7,87},{8,88},{10... | collective-permute-start | bytes 245768 | tf_op jit(solution)/shard_map/ppermute | solution.py:49
  64.0 0.0 collective-permute-done.15.refs_1_
  64.0 0.4 collective-permute-start.20
  64.5 0.4 collective-permute-done.16.refs_2_
  64.9 1.9 %collective-permute-done.17.refs_3_ = bf16[64,640]{1,0:T(8,128)(2,1)S(1)} collective-permute-done((bf16[64,640]{1,0:T(8,128)(2,1)S(1)}, bf16[64,640]{1,0:T(8,128)(2,1)S(1)}, u32[]{:S(2)}, u32[]{:S(2)}) %collective-permute-start.17) | collective-permute-done | bytes 81952 | tf_op jit(solution)/shard_map/ppermute | solution.py:49
  66.8 0.0 collective-permute-done.18.refs_4_
  66.8 2.6 %collective-permute-done.19.refs_5_ = bf16[64,640]{1,0:T(8,128)(2,1)S(1)} collective-permute-done((bf16[64,640]{1,0:T(8,128)(2,1)S(1)}, bf16[64,640]{1,0:T(8,128)(2,1)S(1)}, u32[]{:S(2)}, u32[]{:S(2)}) %collective-permute-start.19) | collective-permute-done | bytes 81952 | tf_op jit(solution)/shard_map/ppermute | solution.py:49
  69.4 0.0 collective-permute-done.20.refs_6_
  69.4 5.9 %attend.1 = bf16[64,4096]{1,0:T(8,128)(2,1)} custom-call(s32[8]{0:T(128)S(1)} %stack.79.group_ref, s32[4]{0:T(128)S(1)} %and_select_fusion.length_ref, f32[64,128]{1,0:T(8,128)S(1)} %get-tuple-element.44.cos_ref, f32[64,128]{1,0:T(8,128)S(1)} %get-tuple-element.45.sin_ref, bf16[4,1024,1024]{2,1,0:T(8,128)(2,1)S(1)} %bitcast.20, ...), custom_call_target="tpu_custom_call" | custom-call | tf_op jit(solution)/shard_map/attend/pallas_call | solution.py:234
  (17 shorter events, 0.1 us)
Async XLA Ops:
  0.0 12.5 %copy-start = (s32[256]{0:T(256)S(1)}, s32[256]{0:T(256)}, u32[]{:S(2)}) copy-start(s32[256]{0:T(256)} %param.13) | copy-start | bytes 3076
  0.0 21.3 %collective-permute-start.2 = (bf16[80,4096]{1,0:T(8,128)(2,1)}, bf16[80,4096]{1,0:T(8,128)(2,1)S(1)}, u32[]{:S(2)}, u32[]{:S(2)}) collective-permute-start(bf16[80,4096]{1,0:T(8,128)(2,1)} %bitcast.21), channel_id=1, source_target_pairs={{0,4},{2,6},{1,5},{3,7},{4,8},{6,10},{5,9},{7,11},{8,12},{10,14},{... | collective-permute-start | bytes 1966088 | tf_op jit(solution)/shard_map/ppermute | solution.py:49
  2.1 19.1 %collective-permute-start.1 = (bf16[80,4096]{1,0:T(8,128)(2,1)}, bf16[80,4096]{1,0:T(8,128)(2,1)S(1)}, u32[]{:S(2)}, u32[]{:S(2)}) collective-permute-start(bf16[80,4096]{1,0:T(8,128)(2,1)} %bitcast.22), channel_id=1, source_target_pairs={{0,12},{2,14},{1,13},{3,15},{4,0},{6,2},{5,1},{7,3},{8,4},{10,6},{... | collective-permute-start | bytes 1966088 | tf_op jit(solution)/shard_map/ppermute | solution.py:49
  3.6 17.6 %collective-permute-start = (bf16[80,4096]{1,0:T(8,128)(2,1)}, bf16[80,4096]{1,0:T(8,128)(2,1)}, u32[]{:S(2)}, u32[]{:S(2)}) collective-permute-start(bf16[80,4096]{1,0:T(8,128)(2,1)} %bitcast.23), channel_id=1, source_target_pairs={{0,2},{2,1},{1,3},{3,0},{4,6},{6,5},{5,7},{7,4},{8,10},{10,9},{9,1... | collective-permute-start | bytes 1966088 | tf_op jit(solution)/shard_map/ppermute | solution.py:49
  4.9 2.7 %collective-permute-start.3 = (bf16[16,128]{1,0:T(8,128)(2,1)S(1)}, bf16[16,128]{1,0:T(8,128)(2,1)S(1)}, u32[]{:S(2)}, u32[]{:S(2)}) collective-permute-start(bf16[16,128]{1,0:T(8,128)(2,1)S(1)} %broadcast_in_dim.16), channel_id=1, source_target_pairs={{0,64},{2,66},{1,65},{3,67},{4,68},{6,70},{5,69},{7,71},{8,72},{10... | collective-permute-start | bytes 12296 | tf_op jit(solution)/shard_map/ppermute | solution.py:49
  7.5 1.0 %copy-start.1 = (bf16[64,4096]{1,0:T(8,128)(2,1)S(1)}, bf16[64,4096]{1,0:T(8,128)(2,1)}, u32[]{:S(2)}) copy-start(bf16[64,4096]{1,0:T(8,128)(2,1)} %rows.1) | copy-start | bytes 1572868
  8.6 18.4 %copy-start.2 = (bf16[64,4096]{1,0:T(8,128)(2,1)S(1)}, bf16[64,4096]{1,0:T(8,128)(2,1)}, u32[]{:S(2)}) copy-start(bf16[64,4096]{1,0:T(8,128)(2,1)} %rows.1) | copy-start | bytes 1572868
  8.6 38.1 %copy-start.3 = (bf16[4096,80]{0,1:T(8,128)(2,1)S(1)}, bf16[4096,80]{0,1:T(8,128)(2,1)}, u32[]{:S(2)}) copy-start(bf16[4096,80]{0,1:T(8,128)(2,1)} %param.9) | copy-start | bytes 1966084
  8.6 15.9 %collective-permute-start.9 = (bf16[64,4096]{1,0:T(8,128)(2,1)S(1)}, bf16[64,4096]{1,0:T(8,128)(2,1)S(1)}, u32[]{:S(2)}, u32[]{:S(2)}) collective-permute-start(bf16[64,4096]{1,0:T(8,128)(2,1)S(1)} %copy_rows.1), channel_id=1, source_target_pairs={{0,48},{2,50},{1,49},{3,51},{4,52},{6,54},{5,53},{7,55},{8,56},{10... | collective-permute-start | bytes 1572872 | tf_op jit(solution)/shard_map/ppermute | solution.py:49
  12.5 14.6 %collective-permute-start.8 = (bf16[64,4096]{1,0:T(8,128)(2,1)S(1)}, bf16[64,4096]{1,0:T(8,128)(2,1)}, u32[]{:S(2)}, u32[]{:S(2)}) collective-permute-start(bf16[64,4096]{1,0:T(8,128)(2,1)S(1)} %copy_rows.1), channel_id=1, source_target_pairs={{0,16},{2,18},{1,17},{3,19},{4,20},{6,22},{5,21},{7,23},{8,24},{10... | collective-permute-start | bytes 1572872 | tf_op jit(solution)/shard_map/ppermute | solution.py:49
  13.2 0.6 copy-start.4
  21.3 17.1 %collective-permute-start.4 = (bf16[80,4096]{1,0:T(8,128)(2,1)}, bf16[80,4096]{1,0:T(8,128)(2,1)S(1)}, u32[]{:S(2)}, u32[]{:S(2)}) collective-permute-start(bf16[80,4096]{1,0:T(8,128)(2,1)} %collective-permute-done.refs_1_), channel_id=1, source_target_pairs={{0,8},{2,10},{1,9},{3,11},{4,12},{6,14},{5,13},{7,15},{8,0},{10,2}... | collective-permute-start | bytes 1966088 | tf_op jit(solution)/shard_map/ppermute | solution.py:49
  23.1 15.3 %collective-permute-start.5 = (bf16[80,4096]{1,0:T(8,128)(2,1)S(1)}, bf16[80,4096]{1,0:T(8,128)(2,1)S(1)}, u32[]{:S(2)}, u32[]{:S(2)}) collective-permute-start(bf16[80,4096]{1,0:T(8,128)(2,1)S(1)} %collective-permute-done.2.refs_2_), channel_id=1, source_target_pairs={{0,3},{2,0},{1,2},{3,1},{4,7},{6,4},{5,6},{7,5},{8,11},{10,8},{9,1... | collective-permute-start | bytes 1966088 | tf_op jit(solution)/shard_map/ppermute | solution.py:49
  24.5 16.3 %collective-permute-start.6 = (bf16[80,4096]{1,0:T(8,128)(2,1)S(1)}, bf16[80,4096]{1,0:T(8,128)(2,1)S(1)}, u32[]{:S(2)}, u32[]{:S(2)}) collective-permute-start(bf16[80,4096]{1,0:T(8,128)(2,1)S(1)} %collective-permute-done.1.refs_4_), channel_id=1, source_target_pairs={{0,2},{2,1},{1,3},{3,0},{4,6},{6,5},{5,7},{7,4},{8,10},{10,9},{9,1... | collective-permute-start | bytes 1966088 | tf_op jit(solution)/shard_map/ppermute | solution.py:49
  24.6 12.9 %collective-permute-start.7 = (bf16[64,4096]{1,0:T(8,128)(2,1)S(1)}, bf16[64,4096]{1,0:T(8,128)(2,1)S(1)}, u32[]{:S(2)}, u32[]{:S(2)}) collective-permute-start(bf16[64,4096]{1,0:T(8,128)(2,1)S(1)} %copy_rows.1), channel_id=1, source_target_pairs={{0,32},{2,34},{1,33},{3,35},{4,36},{6,38},{5,37},{7,39},{8,40},{10... | collective-permute-start | bytes 1572872 | tf_op jit(solution)/shard_map/ppermute | solution.py:49
  27.0 42.4 %slice-start = ((s8[8388608]{0:T(1024)(128)(4,1)}), s8[4194304]{0:T(1024)(128)(4,1)S(1)}, s32[]{:S(2)}) async-start(s8[8388608]{0:T(1024)(128)(4,1)} %bitcast.19), calls=%async_computation | async-start | bytes 8388608
  28.4 41.0 %slice-start.1 = ((s8[8388608]{0:T(1024)(128)(4,1)}), s8[4194304]{0:T(1024)(128)(4,1)S(1)}, s32[]{:S(2)}) async-start(s8[8388608]{0:T(1024)(128)(4,1)} %bitcast.19), calls=%async_computation.1 | async-start | bytes 8388608
  40.8 5.9 %collective-permute-start.10 = (bf16[192,4096]{1,0:T(8,128)(2,1)S(1)}, bf16[192,4096]{1,0:T(8,128)(2,1)S(1)}, u32[]{:S(2)}, u32[]{:S(2)}) collective-permute-start(bf16[192,4096]{1,0:T(8,128)(2,1)S(1)} %pad_maximum_fusion.refs_6_), channel_id=1, source_target_pairs={{0,64},{2,66},{1,65},{3,67},{4,68},{6,70},{5,69},{7,71},{8,72},{10... | collective-permute-start | bytes 4718600 | tf_op jit(solution)/shard_map/ppermute | solution.py:49
  42.9 3.8 %collective-permute-start.11 = (bf16[64,4096]{1,0:T(8,128)(2,1)S(1)}, bf16[64,4096]{1,0:T(8,128)(2,1)S(1)}, u32[]{:S(2)}, u32[]{:S(2)}) collective-permute-start(bf16[64,4096]{1,0:T(8,128)(2,1)S(1)} %collective-permute-done.7.refs_7_), channel_id=1, source_target_pairs={{0,64},{2,66},{1,65},{3,67},{4,68},{6,70},{5,69},{7,71},{8,72},{10... | collective-permute-start | bytes 1572872 | tf_op jit(solution)/shard_map/ppermute | solution.py:49
  42.9 10.0 %collective-permute-start.12 = (bf16[80,2048]{1,0:T(8,128)(2,1)S(1)}, bf16[80,2048]{1,0:T(8,128)(2,1)S(1)}, u32[]{:S(2)}, u32[]{:S(2)}) collective-permute-start(bf16[80,2048]{1,0:T(8,128)(2,1)S(1)} %slice.6), channel_id=1, source_target_pairs={{0,4},{2,6},{1,5},{3,7},{4,8},{6,10},{5,9},{7,11},{8,12},{10,14},{... | collective-permute-start | bytes 983048 | tf_op jit(solution)/shard_map/ppermute | solution.py:49
  43.3 9.6 %collective-permute-start.13 = (bf16[80,2048]{1,0:T(8,128)(2,1)S(1)}, bf16[80,2048]{1,0:T(8,128)(2,1)S(1)}, u32[]{:S(2)}, u32[]{:S(2)}) collective-permute-start(bf16[80,2048]{1,0:T(8,128)(2,1)S(1)} %slice.7), channel_id=1, source_target_pairs={{0,12},{2,14},{1,13},{3,15},{4,0},{6,2},{5,1},{7,3},{8,4},{10,6},{... | collective-permute-start | bytes 983048 | tf_op jit(solution)/shard_map/ppermute | solution.py:49
  55.0 7.8 %collective-permute-start.14 = (bf16[64,640]{1,0:T(8,128)(2,1)S(1)}, bf16[64,640]{1,0:T(8,128)(2,1)S(1)}, u32[]{:S(2)}, u32[]{:S(2)}) collective-permute-start(bf16[64,640]{1,0:T(8,128)(2,1)S(1)} %get-tuple-element.62), channel_id=1, source_target_pairs={{0,32},{2,34},{1,33},{3,35},{4,36},{6,38},{5,37},{7,39},{8,40},{10... | collective-permute-start | bytes 245768 | tf_op jit(solution)/shard_map/ppermute | solution.py:49
  57.1 6.9 %collective-permute-start.15 = (bf16[64,640]{1,0:T(8,128)(2,1)S(1)}, bf16[64,640]{1,0:T(8,128)(2,1)S(1)}, u32[]{:S(2)}, u32[]{:S(2)}) collective-permute-start(bf16[64,640]{1,0:T(8,128)(2,1)S(1)} %get-tuple-element.63), channel_id=1, source_target_pairs={{0,96},{2,98},{1,97},{3,99},{4,100},{6,102},{5,101},{7,103},{8,104... | collective-permute-start | bytes 245768 | tf_op jit(solution)/shard_map/ppermute | solution.py:49
  59.6 5.3 %collective-permute-start.16 = (bf16[64,640]{1,0:T(8,128)(2,1)S(1)}, bf16[64,640]{1,0:T(8,128)(2,1)S(1)}, u32[]{:S(2)}, u32[]{:S(2)}) collective-permute-start(bf16[64,640]{1,0:T(8,128)(2,1)S(1)} %get-tuple-element.64), channel_id=1, source_target_pairs={{0,48},{2,50},{1,49},{3,51},{4,52},{6,54},{5,53},{7,55},{8,56},{10... | collective-permute-start | bytes 245768 | tf_op jit(solution)/shard_map/ppermute | solution.py:49
  62.2 4.5 %collective-permute-start.17 = (bf16[64,640]{1,0:T(8,128)(2,1)S(1)}, bf16[64,640]{1,0:T(8,128)(2,1)S(1)}, u32[]{:S(2)}, u32[]{:S(2)}) collective-permute-start(bf16[64,640]{1,0:T(8,128)(2,1)S(1)} %get-tuple-element.65), channel_id=1, source_target_pairs={{0,112},{2,114},{1,113},{3,115},{4,116},{6,118},{5,117},{7,119},{8... | collective-permute-start | bytes 245768 | tf_op jit(solution)/shard_map/ppermute | solution.py:49
  62.2 4.5 %collective-permute-start.18 = (bf16[64,640]{1,0:T(8,128)(2,1)S(1)}, bf16[64,640]{1,0:T(8,128)(2,1)S(1)}, u32[]{:S(2)}, u32[]{:S(2)}) collective-permute-start(bf16[64,640]{1,0:T(8,128)(2,1)S(1)} %get-tuple-element.66), channel_id=1, source_target_pairs={{0,16},{2,18},{1,17},{3,19},{4,20},{6,22},{5,21},{7,23},{8,24},{10... | collective-permute-start | bytes 245768 | tf_op jit(solution)/shard_map/ppermute | solution.py:49
  62.7 6.7 %collective-permute-start.19 = (bf16[64,640]{1,0:T(8,128)(2,1)S(1)}, bf16[64,640]{1,0:T(8,128)(2,1)S(1)}, u32[]{:S(2)}, u32[]{:S(2)}) collective-permute-start(bf16[64,640]{1,0:T(8,128)(2,1)S(1)} %get-tuple-element.67), channel_id=1, source_target_pairs={{0,80},{2,82},{1,81},{3,83},{4,84},{6,86},{5,85},{7,87},{8,88},{10... | collective-permute-start | bytes 245768 | tf_op jit(solution)/shard_map/ppermute | solution.py:49
  64.0 5.4 %collective-permute-start.20 = (bf16[64,640]{1,0:T(8,128)(2,1)S(1)}, bf16[64,640]{1,0:T(8,128)(2,1)S(1)}, u32[]{:S(2)}, u32[]{:S(2)}) collective-permute-start(bf16[64,640]{1,0:T(8,128)(2,1)S(1)} %get-tuple-element.68), channel_id=1, source_target_pairs={{0,64},{2,66},{1,65},{3,67},{4,68},{6,70},{5,69},{7,71},{8,72},{10... | collective-permute-start | bytes 245768 | tf_op jit(solution)/shard_map/ppermute | solution.py:49

commit v6 on v5

--- a/solution.py
+++ b/solution.py
@@ -142,11 +142,7 @@
         out_shape=out_shape,
         scratch_shapes=[pltpu.VMEM((width, D), jnp.bfloat16)],
         compiler_params=pltpu.CompilerParams(vmem_limit_bytes=PROJECT_VMEM),
-        cost_estimate=pl.CostEstimate(
-            flops=4 * NEAR * width * D,
-            bytes_accessed=2 * D * (2 * NEAR + width),
-            transcendentals=0,
-        ),
+        cost_estimate=pl.CostEstimate(flops=1, bytes_accessed=1, transcendentals=0),
         name=kernel.__name__.removesuffix("_kernel"),
     )(places, whole, *operands)
 
@@ -286,8 +282,8 @@
     sine = jnp.concatenate([-sine, sine], axis=1)
 
     up, down = shift(late, dz=1), shift(late, dz=3)
-    own_side, three, one, tokens, late, small = lax.optimization_barrier(
-        (own_side, three, one, tokens, late, (places, groups, bias_cols, my_lengths, cosine, sine))
+    own_side, tokens, late, small = lax.optimization_barrier(
+        (own_side, tokens, late, (places, groups, bias_cols, my_lengths, cosine, sine))
     )
     places, groups, bias_cols, my_lengths, cosine, sine = small
     far = shift(late, dz=2)
@@ -295,8 +291,8 @@
     two_side = shift(own_side, dy=2)
     near = jnp.concatenate([tokens, up, down])
     low, high = one[:, :HALF], three[:, HALF:]
-    two_side, one_side, three_side, far, near, low, high = lax.optimization_barrier(
-        (two_side, one_side, three_side, far, near, low, high)
+    two_side, one_side, three_side, far, near = lax.optimization_barrier(
+        (two_side, one_side, three_side, far, near)
     )
     two_low, two_high = shift(low, dy=1), shift(high, dy=3)
     other = shift(near, dt=1)

time: 75.6 us -> 74.9 us (level)
  starting transfers between devices: 29.8 us -> 34.1 us
  other arithmetic: 6.07 us -> 2.67 us
  local copies, waits for them, and re-layouts: 6.43 us -> 3.33 us
  waiting for transfers between devices: 19.9 us -> 21.6 us
    ppermute x21, starting transfers between devices: 29.8 us -> 34.1 us  [shift(): return lax.ppermute(array, AXES, pairs)]
    ppermute x21, waiting for transfers between devices: 19.9 us -> 21.6 us  [shift(): return lax.ppermute(array, AXES, pairs)]
    convert_element_type x1, local copies, waits for them, and re-layouts: 1.3 us -> 0.08 us  [on_device(): angles = positions.astype(jnp.float32)[:, None] * frequency[None, :]]
    unnamed x14 -> x10, local copies, waits for them, and re-layouts: 1.64 us -> 1.06 us
  transfers between devices with their start and end apart: 21 -> 21, of which waited for: 9 -> 11; matrix products, arithmetic and copies ran while one was open for 14% -> 7% of each run, Pallas kernels for 7% -> 6%
where the time goes in v6:
time: 74.9 us; the launch traced here: 74.7 us
  starting transfers between devices  34.1 us (46%)
  waiting for transfers between devices  21.6 us (29%)
  Pallas kernels  12.9 us (17%)
  local copies, waits for them, and re-layouts  3.33 us (4%)
  other arithmetic  2.67 us (4%)
    ppermute x21, starting transfers between devices, shift(): return lax.ppermute(array, AXES, pairs)  34.1 us
    ppermute x21, waiting for transfers between devices, shift(): return lax.ppermute(array, AXES, pairs)  21.6 us
    pallas_call x2, Pallas kernels, project(): pl.pallas_call(functools.partial(kernel, where), in_specs=[pl.BlockSpec(m...  6.54 us
    pallas_call x1, Pallas kernels, attend(): pl.pallas_call(attend_kernel, in_specs=[pl.BlockSpec(memory_space=pltpu.S...  6.29 us
    concatenate x1, other arithmetic, on_device(): near = jnp.concatenate([tokens, up, down])  1.5 us
  transfers between devices with their start and end apart: 21, of which 11 were waited for; matrix products, arithmetic and copies ran while one was open for 7% of the time, Pallas kernels for 6%

profile of v6, /device:TPU:1, one launch (start us, length us, event | category | flops | bytes accessed | tf_op | source)
XLA Modules:
  0.0 74.7 jit_solution(4134719900535882176)
XLA Ops:
  0.0 0.0 copy-start
  0.0 2.0 %collective-permute-start = (bf16[80,4096]{1,0:T(8,128)(2,1)}, bf16[80,4096]{1,0:T(8,128)(2,1)S(1)}, u32[]{:S(2)}, u32[]{:S(2)}) collective-permute-start(bf16[80,4096]{1,0:T(8,128)(2,1)} %bitcast.21), channel_id=1, source_target_pairs={{0,2},{2,1},{1,3},{3,0},{4,6},{6,5},{5,7},{7,4},{8,10},{10,9},{9,1... | collective-permute-start | bytes 1966088 | tf_op jit(solution)/shard_map/ppermute | solution.py:49
  2.0 1.3 %collective-permute-start.2 = (bf16[80,4096]{1,0:T(8,128)(2,1)}, bf16[80,4096]{1,0:T(8,128)(2,1)S(1)}, u32[]{:S(2)}, u32[]{:S(2)}) collective-permute-start(bf16[80,4096]{1,0:T(8,128)(2,1)} %bitcast.22), channel_id=1, source_target_pairs={{0,4},{2,6},{1,5},{3,7},{4,8},{6,10},{5,9},{7,11},{8,12},{10,14},{... | collective-permute-start | bytes 1966088 | tf_op jit(solution)/shard_map/ppermute | solution.py:49
  3.3 1.4 %collective-permute-start.5 = (bf16[80,4096]{1,0:T(8,128)(2,1)}, bf16[80,4096]{1,0:T(8,128)(2,1)S(1)}, u32[]{:S(2)}, u32[]{:S(2)}) collective-permute-start(bf16[80,4096]{1,0:T(8,128)(2,1)} %bitcast.23), channel_id=1, source_target_pairs={{0,12},{2,14},{1,13},{3,15},{4,0},{6,2},{5,1},{7,3},{8,4},{10,6},{... | collective-permute-start | bytes 1966088 | tf_op jit(solution)/shard_map/ppermute | solution.py:49
  4.8 1.5 %collective-permute-start.1 = (bf16[16,128]{1,0:T(8,128)(2,1)S(1)}, bf16[16,128]{1,0:T(8,128)(2,1)S(1)}, u32[]{:S(2)}, u32[]{:S(2)}) collective-permute-start(bf16[16,128]{1,0:T(8,128)(2,1)S(1)} %broadcast_in_dim.16), channel_id=1, source_target_pairs={{0,64},{2,66},{1,65},{3,67},{4,68},{6,70},{5,69},{7,71},{8,72},{10... | collective-permute-start | bytes 12296 | tf_op jit(solution)/shard_map/ppermute | solution.py:49
  6.3 0.1 stack.79.group_ref
  6.4 0.1 stack.70.at_ref
  6.5 0.6 collective-permute-done.1.early
  7.1 0.0 copy-start.1
  7.1 1.0 %copy-done.1 = bf16[64,4096]{1,0:T(8,128)(2,1)S(1)} copy-done((bf16[64,4096]{1,0:T(8,128)(2,1)S(1)}, bf16[64,4096]{1,0:T(8,128)(2,1)}, u32[]{:S(2)}) %copy-start.1) | copy-done | bytes 524312
  8.2 0.0 copy-start.2
  8.2 3.8 %collective-permute-start.9 = (bf16[64,4096]{1,0:T(8,128)(2,1)S(1)}, bf16[64,4096]{1,0:T(8,128)(2,1)}, u32[]{:S(2)}, u32[]{:S(2)}) collective-permute-start(bf16[64,4096]{1,0:T(8,128)(2,1)S(1)} %copy_rows.1), channel_id=1, source_target_pairs={{0,48},{2,50},{1,49},{3,51},{4,52},{6,54},{5,53},{7,55},{8,56},{10... | collective-permute-start | bytes 1572872 | tf_op jit(solution)/shard_map/ppermute | solution.py:49
  12.0 0.0 collective-permute-start.8
  12.0 0.0 copy-done
  12.0 0.6 gather_fusion
  12.7 1.3 %gather_fusion.1 = s32[4]{0:T(128)S(1)} fusion(s32[256]{0:T(256)} %param.12, s32[1024]{0:T(1024)S(1)} %pad_clamp_fusion), kind=kCustom, calls=%fused_computation.1.clone | custom fusion | bytes 48 | tf_op jit(solution)/shard_map/jit(_take)/gather | solution.py:274
  14.0 0.1 add_convert_fusion
  14.1 0.8 %dynamic-slice_convert_fusion = f32[640]{0:T(1024)S(1)} fusion(bf16[5120]{0:T(1024)(128)(2,1)} %param.10, s32[]{:T(128)S(6)} %select_n.83), kind=kLoop, calls=%fused_computation.13 | loop fusion | flops 640 | bytes 3844 | tf_op jit(solution)/shard_map/broadcast_in_dim | solution.py:271
  14.8 0.1 convert_element_type.12
  14.9 0.2 fusion
  15.1 0.1 pad_maximum_fusion.1
  15.2 2.4 %collective-permute-done.refs_1_ = bf16[80,4096]{1,0:T(8,128)(2,1)S(1)} collective-permute-done((bf16[80,4096]{1,0:T(8,128)(2,1)}, bf16[80,4096]{1,0:T(8,128)(2,1)S(1)}, u32[]{:S(2)}, u32[]{:S(2)}) %collective-permute-start) | collective-permute-done | bytes 655392 | tf_op jit(solution)/shard_map/ppermute | solution.py:49
  17.6 3.2 %collective-permute-start.3 = (bf16[80,4096]{1,0:T(8,128)(2,1)S(1)}, bf16[80,4096]{1,0:T(8,128)(2,1)S(1)}, u32[]{:S(2)}, u32[]{:S(2)}) collective-permute-start(bf16[80,4096]{1,0:T(8,128)(2,1)S(1)} %collective-permute-done.refs_1_), channel_id=1, source_target_pairs={{0,8},{2,10},{1,9},{3,11},{4,12},{6,14},{5,13},{7,15},{8,0},{10,2}... | collective-permute-start | bytes 1966088 | tf_op jit(solution)/shard_map/ppermute | solution.py:49
  20.9 0.0 collective-permute-done.2.refs_2_
  20.9 1.3 %collective-permute-start.4 = (bf16[80,4096]{1,0:T(8,128)(2,1)S(1)}, bf16[80,4096]{1,0:T(8,128)(2,1)S(1)}, u32[]{:S(2)}, u32[]{:S(2)}) collective-permute-start(bf16[80,4096]{1,0:T(8,128)(2,1)S(1)} %collective-permute-done.2.refs_2_), channel_id=1, source_target_pairs={{0,3},{2,0},{1,2},{3,1},{4,7},{6,4},{5,6},{7,5},{8,11},{10,8},{9,1... | collective-permute-start | bytes 1966088 | tf_op jit(solution)/shard_map/ppermute | solution.py:49
  22.1 0.0 collective-permute-done.5.refs_4_
  22.2 0.2 collective-permute-start.6
  22.3 0.6 collective-permute-done.9
  23.0 2.9 %collective-permute-start.7 = (bf16[64,4096]{1,0:T(8,128)(2,1)S(1)}, bf16[64,4096]{1,0:T(8,128)(2,1)S(1)}, u32[]{:S(2)}, u32[]{:S(2)}) collective-permute-start(bf16[64,4096]{1,0:T(8,128)(2,1)S(1)} %copy_rows.1), channel_id=1, source_target_pairs={{0,32},{2,34},{1,33},{3,35},{4,36},{6,38},{5,37},{7,39},{8,40},{10... | collective-permute-start | bytes 1572872 | tf_op jit(solution)/shard_map/ppermute | solution.py:49
  25.8 0.3 collective-permute-done.8
  26.2 1.5 %pad_maximum_fusion.refs_6_ = bf16[192,4096]{1,0:T(8,128)(2,1)S(1)} fusion(bf16[64,4096]{1,0:T(8,128)(2,1)} %collective-permute-done.9, bf16[64,4096]{1,0:T(8,128)(2,1)} %collective-permute-done.8, bf16[64,4096]{1,0:T(8,128)(2,1)} %rows.1), kind=kLoop, calls=%fused_computation.2 | loop fusion | flops 4718592 | bytes 3145728 | tf_op jit(solution)/shard_map/concatenate | solution.py:292
  27.7 8.2 %collective-permute-done.7.refs_7_ = bf16[64,4096]{1,0:T(8,128)(2,1)S(1)} collective-permute-done((bf16[64,4096]{1,0:T(8,128)(2,1)S(1)}, bf16[64,4096]{1,0:T(8,128)(2,1)S(1)}, u32[]{:S(2)}, u32[]{:S(2)}) %collective-permute-start.7) | collective-permute-done | bytes 524320 | tf_op jit(solution)/shard_map/ppermute | solution.py:49
  35.9 0.0 collective-permute-done.3.refs_2_
  35.9 0.0 collective-permute-done.4.refs_3_
  35.9 1.7 %collective-permute-done.6.refs_5_ = bf16[80,4096]{1,0:T(8,128)(2,1)S(1)} collective-permute-done((bf16[80,4096]{1,0:T(8,128)(2,1)S(1)}, bf16[80,4096]{1,0:T(8,128)(2,1)S(1)}, u32[]{:S(2)}, u32[]{:S(2)}) %collective-permute-start.6) | collective-permute-done | bytes 655392 | tf_op jit(solution)/shard_map/ppermute | solution.py:49
  37.6 2.9 %collective-permute-start.10 = (bf16[192,4096]{1,0:T(8,128)(2,1)S(1)}, bf16[192,4096]{1,0:T(8,128)(2,1)S(1)}, u32[]{:S(2)}, u32[]{:S(2)}) collective-permute-start(bf16[192,4096]{1,0:T(8,128)(2,1)S(1)} %pad_maximum_fusion.refs_6_), channel_id=1, source_target_pairs={{0,64},{2,66},{1,65},{3,67},{4,68},{6,70},{5,69},{7,71},{8,72},{10... | collective-permute-start | bytes 4718600 | tf_op jit(solution)/shard_map/ppermute | solution.py:49
  40.5 0.0 collective-permute-start.11
  40.5 0.5 collective-permute-start.12
  41.0 0.0 slice-start.1
  41.0 2.3 %collective-permute-start.13 = (bf16[80,2048]{1,0:T(8,128)(2,1)S(1)}, bf16[80,2048]{1,0:T(8,128)(2,1)S(1)}, u32[]{:S(2)}, u32[]{:S(2)}) collective-permute-start(bf16[80,2048]{1,0:T(8,128)(2,1)S(1)} %slice.13), channel_id=1, source_target_pairs={{0,12},{2,14},{1,13},{3,15},{4,0},{6,2},{5,1},{7,3},{8,4},{10,6},{... | collective-permute-start | bytes 983048 | tf_op jit(solution)/shard_map/ppermute | solution.py:49
  43.4 0.9 %collective-permute-done.11.refs_9_ = bf16[64,4096]{1,0:T(8,128)(2,1)S(1)} collective-permute-done((bf16[64,4096]{1,0:T(8,128)(2,1)S(1)}, bf16[64,4096]{1,0:T(8,128)(2,1)S(1)}, u32[]{:S(2)}, u32[]{:S(2)}) %collective-permute-start.11) | collective-permute-done | bytes 524320 | tf_op jit(solution)/shard_map/ppermute | solution.py:49
  44.3 0.0 collective-permute-done.10.refs_8_
  44.3 0.0 copy-done.2
  44.3 4.4 %project_first.1 = (f32[512,640]{1,0:T(8,128)S(1)}, bf16[512,4096]{1,0:T(8,128)(2,1)S(1)}) custom-call(s32[10]{0:T(128)S(1)} %stack.70.at_ref, f32[1,640]{1,0:T(1,128)S(1)} %reshape.28.bias_ref, bf16[80,4096]{1,0:T(8,128)(2,1)S(1)} %bitcast.24, bf16[80,4096]{1,0:T(8,128)(2,1)S(1)} %collective-permute-done.refs_1_, ...), custom_call_target="tpu_custom_call" | custom-call | flops 1 | bytes 1 | tf_op jit(solution)/shard_map/project_first/pallas_call | solution.py:138
  48.8 1.8 %collective-permute-done.12.refs_0_ = bf16[80,2048]{1,0:T(8,128)(2,1)S(1)} collective-permute-done((bf16[80,2048]{1,0:T(8,128)(2,1)S(1)}, bf16[80,2048]{1,0:T(8,128)(2,1)S(1)}, u32[]{:S(2)}, u32[]{:S(2)}) %collective-permute-start.12) | collective-permute-done | bytes 327712 | tf_op jit(solution)/shard_map/ppermute | solution.py:49
  50.6 0.0 collective-permute-done.13.refs_1_
  50.6 2.1 %project_last.1 = (bf16[64,640]{1,0:T(8,128)(2,1)S(1)}, bf16[64,640]{1,0:T(8,128)(2,1)S(1)}, bf16[64,640]{1,0:T(8,128)(2,1)S(1)}, bf16[64,640]{1,0:T(8,128)(2,1)...) custom-call(s32[10]{0:T(128)S(1)} %stack.70.at_ref, ...), custom_call_target="tpu_custom_call" | custom-call | flops 1 | bytes 1 | tf_op jit(solution)/shard_map/project_last/pallas_call | solution.py:138
  52.7 3.7 %collective-permute-start.14 = (bf16[64,640]{1,0:T(8,128)(2,1)S(1)}, bf16[64,640]{1,0:T(8,128)(2,1)S(1)}, u32[]{:S(2)}, u32[]{:S(2)}) collective-permute-start(bf16[64,640]{1,0:T(8,128)(2,1)S(1)} %get-tuple-element.54), channel_id=1, source_target_pairs={{0,32},{2,34},{1,33},{3,35},{4,36},{6,38},{5,37},{7,39},{8,40},{10... | collective-permute-start | bytes 245768 | tf_op jit(solution)/shard_map/ppermute | solution.py:49
  56.4 1.3 %collective-permute-start.15 = (bf16[64,640]{1,0:T(8,128)(2,1)S(1)}, bf16[64,640]{1,0:T(8,128)(2,1)S(1)}, u32[]{:S(2)}, u32[]{:S(2)}) collective-permute-start(bf16[64,640]{1,0:T(8,128)(2,1)S(1)} %get-tuple-element.55), channel_id=1, source_target_pairs={{0,96},{2,98},{1,97},{3,99},{4,100},{6,102},{5,101},{7,103},{8,104... | collective-permute-start | bytes 245768 | tf_op jit(solution)/shard_map/ppermute | solution.py:49
  57.7 3.3 %collective-permute-start.16 = (bf16[64,640]{1,0:T(8,128)(2,1)S(1)}, bf16[64,640]{1,0:T(8,128)(2,1)S(1)}, u32[]{:S(2)}, u32[]{:S(2)}) collective-permute-start(bf16[64,640]{1,0:T(8,128)(2,1)S(1)} %get-tuple-element.56), channel_id=1, source_target_pairs={{0,48},{2,50},{1,49},{3,51},{4,52},{6,54},{5,53},{7,55},{8,56},{10... | collective-permute-start | bytes 245768 | tf_op jit(solution)/shard_map/ppermute | solution.py:49
  61.0 0.0 collective-permute-start.17
  61.0 0.5 collective-permute-start.18
  61.5 0.0 collective-permute-done.14.refs_0_
  61.5 1.3 %collective-permute-start.19 = (bf16[64,640]{1,0:T(8,128)(2,1)S(1)}, bf16[64,640]{1,0:T(8,128)(2,1)S(1)}, u32[]{:S(2)}, u32[]{:S(2)}) collective-permute-start(bf16[64,640]{1,0:T(8,128)(2,1)S(1)} %get-tuple-element.59), channel_id=1, source_target_pairs={{0,80},{2,82},{1,81},{3,83},{4,84},{6,86},{5,85},{7,87},{8,88},{10... | collective-permute-start | bytes 245768 | tf_op jit(solution)/shard_map/ppermute | solution.py:49
  62.8 0.0 collective-permute-done.15.refs_1_
  62.8 0.6 collective-permute-start.20
  63.4 0.3 collective-permute-done.16.refs_2_
  63.7 2.6 %collective-permute-done.17.refs_3_ = bf16[64,640]{1,0:T(8,128)(2,1)S(1)} collective-permute-done((bf16[64,640]{1,0:T(8,128)(2,1)S(1)}, bf16[64,640]{1,0:T(8,128)(2,1)S(1)}, u32[]{:S(2)}, u32[]{:S(2)}) %collective-permute-start.17) | collective-permute-done | bytes 81952 | tf_op jit(solution)/shard_map/ppermute | solution.py:49
  66.3 0.0 collective-permute-done.18.refs_4_
  66.3 2.1 %collective-permute-done.19.refs_5_ = bf16[64,640]{1,0:T(8,128)(2,1)S(1)} collective-permute-done((bf16[64,640]{1,0:T(8,128)(2,1)S(1)}, bf16[64,640]{1,0:T(8,128)(2,1)S(1)}, u32[]{:S(2)}, u32[]{:S(2)}) %collective-permute-start.19) | collective-permute-done | bytes 81952 | tf_op jit(solution)/shard_map/ppermute | solution.py:49
  68.4 0.0 collective-permute-done.20.refs_6_
  68.4 0.0 slice-done
  68.4 0.0 slice-done.1
  68.4 6.3 %attend.1 = bf16[64,4096]{1,0:T(8,128)(2,1)} custom-call(s32[8]{0:T(128)S(1)} %stack.79.group_ref, s32[4]{0:T(128)S(1)} %and_select_fusion.length_ref, f32[64,128]{1,0:T(8,128)S(1)} %get-tuple-element.40.cos_ref, f32[64,128]{1,0:T(8,128)S(1)} %get-tuple-element.41.sin_ref, bf16[4,1024,1024]{2,1,0:T(8,128)(2,1)S(1)} %bitcast.20, ...), custom_call_target="tpu_custom_call" | custom-call | tf_op jit(solution)/shard_map/attend/pallas_call | solution.py:230
  (13 shorter events, 0.2 us)
Async XLA Ops:
  0.0 12.0 %copy-start = (s32[256]{0:T(256)S(1)}, s32[256]{0:T(256)}, u32[]{:S(2)}) copy-start(s32[256]{0:T(256)} %param.13) | copy-start | bytes 3076
  0.0 17.6 %collective-permute-start = (bf16[80,4096]{1,0:T(8,128)(2,1)}, bf16[80,4096]{1,0:T(8,128)(2,1)S(1)}, u32[]{:S(2)}, u32[]{:S(2)}) collective-permute-start(bf16[80,4096]{1,0:T(8,128)(2,1)} %bitcast.21), channel_id=1, source_target_pairs={{0,2},{2,1},{1,3},{3,0},{4,6},{6,5},{5,7},{7,4},{8,10},{10,9},{9,1... | collective-permute-start | bytes 1966088 | tf_op jit(solution)/shard_map/ppermute | solution.py:49
  2.0 18.8 %collective-permute-start.2 = (bf16[80,4096]{1,0:T(8,128)(2,1)}, bf16[80,4096]{1,0:T(8,128)(2,1)S(1)}, u32[]{:S(2)}, u32[]{:S(2)}) collective-permute-start(bf16[80,4096]{1,0:T(8,128)(2,1)} %bitcast.22), channel_id=1, source_target_pairs={{0,4},{2,6},{1,5},{3,7},{4,8},{6,10},{5,9},{7,11},{8,12},{10,14},{... | collective-permute-start | bytes 1966088 | tf_op jit(solution)/shard_map/ppermute | solution.py:49
  3.3 18.8 %collective-permute-start.5 = (bf16[80,4096]{1,0:T(8,128)(2,1)}, bf16[80,4096]{1,0:T(8,128)(2,1)S(1)}, u32[]{:S(2)}, u32[]{:S(2)}) collective-permute-start(bf16[80,4096]{1,0:T(8,128)(2,1)} %bitcast.23), channel_id=1, source_target_pairs={{0,12},{2,14},{1,13},{3,15},{4,0},{6,2},{5,1},{7,3},{8,4},{10,6},{... | collective-permute-start | bytes 1966088 | tf_op jit(solution)/shard_map/ppermute | solution.py:49
  4.8 2.3 %collective-permute-start.1 = (bf16[16,128]{1,0:T(8,128)(2,1)S(1)}, bf16[16,128]{1,0:T(8,128)(2,1)S(1)}, u32[]{:S(2)}, u32[]{:S(2)}) collective-permute-start(bf16[16,128]{1,0:T(8,128)(2,1)S(1)} %broadcast_in_dim.16), channel_id=1, source_target_pairs={{0,64},{2,66},{1,65},{3,67},{4,68},{6,70},{5,69},{7,71},{8,72},{10... | collective-permute-start | bytes 12296 | tf_op jit(solution)/shard_map/ppermute | solution.py:49
  7.1 1.0 %copy-start.1 = (bf16[64,4096]{1,0:T(8,128)(2,1)S(1)}, bf16[64,4096]{1,0:T(8,128)(2,1)}, u32[]{:S(2)}) copy-start(bf16[64,4096]{1,0:T(8,128)(2,1)} %rows.1) | copy-start | bytes 1572868
  8.2 36.1 %copy-start.2 = (bf16[4096,80]{0,1:T(8,128)(2,1)S(1)}, bf16[4096,80]{0,1:T(8,128)(2,1)}, u32[]{:S(2)}) copy-start(bf16[4096,80]{0,1:T(8,128)(2,1)} %param.9) | copy-start | bytes 1966084
  8.2 14.8 %collective-permute-start.9 = (bf16[64,4096]{1,0:T(8,128)(2,1)S(1)}, bf16[64,4096]{1,0:T(8,128)(2,1)}, u32[]{:S(2)}, u32[]{:S(2)}) collective-permute-start(bf16[64,4096]{1,0:T(8,128)(2,1)S(1)} %copy_rows.1), channel_id=1, source_target_pairs={{0,48},{2,50},{1,49},{3,51},{4,52},{6,54},{5,53},{7,55},{8,56},{10... | collective-permute-start | bytes 1572872 | tf_op jit(solution)/shard_map/ppermute | solution.py:49
  12.0 14.2 %collective-permute-start.8 = (bf16[64,4096]{1,0:T(8,128)(2,1)S(1)}, bf16[64,4096]{1,0:T(8,128)(2,1)}, u32[]{:S(2)}, u32[]{:S(2)}) collective-permute-start(bf16[64,4096]{1,0:T(8,128)(2,1)S(1)} %copy_rows.1), channel_id=1, source_target_pairs={{0,16},{2,18},{1,17},{3,19},{4,20},{6,22},{5,21},{7,23},{8,24},{10... | collective-permute-start | bytes 1572872 | tf_op jit(solution)/shard_map/ppermute | solution.py:49
  17.6 18.2 %collective-permute-start.3 = (bf16[80,4096]{1,0:T(8,128)(2,1)S(1)}, bf16[80,4096]{1,0:T(8,128)(2,1)S(1)}, u32[]{:S(2)}, u32[]{:S(2)}) collective-permute-start(bf16[80,4096]{1,0:T(8,128)(2,1)S(1)} %collective-permute-done.refs_1_), channel_id=1, source_target_pairs={{0,8},{2,10},{1,9},{3,11},{4,12},{6,14},{5,13},{7,15},{8,0},{10,2}... | collective-permute-start | bytes 1966088 | tf_op jit(solution)/shard_map/ppermute | solution.py:49
  20.9 15.0 %collective-permute-start.4 = (bf16[80,4096]{1,0:T(8,128)(2,1)S(1)}, bf16[80,4096]{1,0:T(8,128)(2,1)S(1)}, u32[]{:S(2)}, u32[]{:S(2)}) collective-permute-start(bf16[80,4096]{1,0:T(8,128)(2,1)S(1)} %collective-permute-done.2.refs_2_), channel_id=1, source_target_pairs={{0,3},{2,0},{1,2},{3,1},{4,7},{6,4},{5,6},{7,5},{8,11},{10,8},{9,1... | collective-permute-start | bytes 1966088 | tf_op jit(solution)/shard_map/ppermute | solution.py:49
  22.2 15.4 %collective-permute-start.6 = (bf16[80,4096]{1,0:T(8,128)(2,1)S(1)}, bf16[80,4096]{1,0:T(8,128)(2,1)S(1)}, u32[]{:S(2)}, u32[]{:S(2)}) collective-permute-start(bf16[80,4096]{1,0:T(8,128)(2,1)S(1)} %collective-permute-done.5.refs_4_), channel_id=1, source_target_pairs={{0,2},{2,1},{1,3},{3,0},{4,6},{6,5},{5,7},{7,4},{8,10},{10,9},{9,1... | collective-permute-start | bytes 1966088 | tf_op jit(solution)/shard_map/ppermute | solution.py:49
  23.0 12.9 %collective-permute-start.7 = (bf16[64,4096]{1,0:T(8,128)(2,1)S(1)}, bf16[64,4096]{1,0:T(8,128)(2,1)S(1)}, u32[]{:S(2)}, u32[]{:S(2)}) collective-permute-start(bf16[64,4096]{1,0:T(8,128)(2,1)S(1)} %copy_rows.1), channel_id=1, source_target_pairs={{0,32},{2,34},{1,33},{3,35},{4,36},{6,38},{5,37},{7,39},{8,40},{10... | collective-permute-start | bytes 1572872 | tf_op jit(solution)/shard_map/ppermute | solution.py:49
  37.6 6.7 %collective-permute-start.10 = (bf16[192,4096]{1,0:T(8,128)(2,1)S(1)}, bf16[192,4096]{1,0:T(8,128)(2,1)S(1)}, u32[]{:S(2)}, u32[]{:S(2)}) collective-permute-start(bf16[192,4096]{1,0:T(8,128)(2,1)S(1)} %pad_maximum_fusion.refs_6_), channel_id=1, source_target_pairs={{0,64},{2,66},{1,65},{3,67},{4,68},{6,70},{5,69},{7,71},{8,72},{10... | collective-permute-start | bytes 4718600 | tf_op jit(solution)/shard_map/ppermute | solution.py:49
  40.5 3.8 %collective-permute-start.11 = (bf16[64,4096]{1,0:T(8,128)(2,1)S(1)}, bf16[64,4096]{1,0:T(8,128)(2,1)S(1)}, u32[]{:S(2)}, u32[]{:S(2)}) collective-permute-start(bf16[64,4096]{1,0:T(8,128)(2,1)S(1)} %collective-permute-done.7.refs_7_), channel_id=1, source_target_pairs={{0,64},{2,66},{1,65},{3,67},{4,68},{6,70},{5,69},{7,71},{8,72},{10... | collective-permute-start | bytes 1572872 | tf_op jit(solution)/shard_map/ppermute | solution.py:49
  40.5 10.0 %collective-permute-start.12 = (bf16[80,2048]{1,0:T(8,128)(2,1)S(1)}, bf16[80,2048]{1,0:T(8,128)(2,1)S(1)}, u32[]{:S(2)}, u32[]{:S(2)}) collective-permute-start(bf16[80,2048]{1,0:T(8,128)(2,1)S(1)} %slice.12), channel_id=1, source_target_pairs={{0,4},{2,6},{1,5},{3,7},{4,8},{6,10},{5,9},{7,11},{8,12},{10,14},{... | collective-permute-start | bytes 983048 | tf_op jit(solution)/shard_map/ppermute | solution.py:49
  41.0 27.4 %slice-start = ((s8[8388608]{0:T(1024)(128)(4,1)}), s8[4194304]{0:T(1024)(128)(4,1)S(1)}, s32[]{:S(2)}) async-start(s8[8388608]{0:T(1024)(128)(4,1)} %bitcast.19), calls=%async_computation | async-start | bytes 8388608
  41.0 27.3 %slice-start.1 = ((s8[8388608]{0:T(1024)(128)(4,1)}), s8[4194304]{0:T(1024)(128)(4,1)S(1)}, s32[]{:S(2)}) async-start(s8[8388608]{0:T(1024)(128)(4,1)} %bitcast.19), calls=%async_computation.1 | async-start | bytes 8388608
  41.0 9.5 %collective-permute-start.13 = (bf16[80,2048]{1,0:T(8,128)(2,1)S(1)}, bf16[80,2048]{1,0:T(8,128)(2,1)S(1)}, u32[]{:S(2)}, u32[]{:S(2)}) collective-permute-start(bf16[80,2048]{1,0:T(8,128)(2,1)S(1)} %slice.13), channel_id=1, source_target_pairs={{0,12},{2,14},{1,13},{3,15},{4,0},{6,2},{5,1},{7,3},{8,4},{10,6},{... | collective-permute-start | bytes 983048 | tf_op jit(solution)/shard_map/ppermute | solution.py:49
  52.7 8.8 %collective-permute-start.14 = (bf16[64,640]{1,0:T(8,128)(2,1)S(1)}, bf16[64,640]{1,0:T(8,128)(2,1)S(1)}, u32[]{:S(2)}, u32[]{:S(2)}) collective-permute-start(bf16[64,640]{1,0:T(8,128)(2,1)S(1)} %get-tuple-element.54), channel_id=1, source_target_pairs={{0,32},{2,34},{1,33},{3,35},{4,36},{6,38},{5,37},{7,39},{8,40},{10... | collective-permute-start | bytes 245768 | tf_op jit(solution)/shard_map/ppermute | solution.py:49
  56.4 6.4 %collective-permute-start.15 = (bf16[64,640]{1,0:T(8,128)(2,1)S(1)}, bf16[64,640]{1,0:T(8,128)(2,1)S(1)}, u32[]{:S(2)}, u32[]{:S(2)}) collective-permute-start(bf16[64,640]{1,0:T(8,128)(2,1)S(1)} %get-tuple-element.55), channel_id=1, source_target_pairs={{0,96},{2,98},{1,97},{3,99},{4,100},{6,102},{5,101},{7,103},{8,104... | collective-permute-start | bytes 245768 | tf_op jit(solution)/shard_map/ppermute | solution.py:49
  57.7 6.0 %collective-permute-start.16 = (bf16[64,640]{1,0:T(8,128)(2,1)S(1)}, bf16[64,640]{1,0:T(8,128)(2,1)S(1)}, u32[]{:S(2)}, u32[]{:S(2)}) collective-permute-start(bf16[64,640]{1,0:T(8,128)(2,1)S(1)} %get-tuple-element.56), channel_id=1, source_target_pairs={{0,48},{2,50},{1,49},{3,51},{4,52},{6,54},{5,53},{7,55},{8,56},{10... | collective-permute-start | bytes 245768 | tf_op jit(solution)/shard_map/ppermute | solution.py:49
  61.0 5.3 %collective-permute-start.17 = (bf16[64,640]{1,0:T(8,128)(2,1)S(1)}, bf16[64,640]{1,0:T(8,128)(2,1)S(1)}, u32[]{:S(2)}, u32[]{:S(2)}) collective-permute-start(bf16[64,640]{1,0:T(8,128)(2,1)S(1)} %get-tuple-element.57), channel_id=1, source_target_pairs={{0,112},{2,114},{1,113},{3,115},{4,116},{6,118},{5,117},{7,119},{8... | collective-permute-start | bytes 245768 | tf_op jit(solution)/shard_map/ppermute | solution.py:49
  61.0 5.3 %collective-permute-start.18 = (bf16[64,640]{1,0:T(8,128)(2,1)S(1)}, bf16[64,640]{1,0:T(8,128)(2,1)S(1)}, u32[]{:S(2)}, u32[]{:S(2)}) collective-permute-start(bf16[64,640]{1,0:T(8,128)(2,1)S(1)} %get-tuple-element.58), channel_id=1, source_target_pairs={{0,16},{2,18},{1,17},{3,19},{4,20},{6,22},{5,21},{7,23},{8,24},{10... | collective-permute-start | bytes 245768 | tf_op jit(solution)/shard_map/ppermute | solution.py:49
  61.5 6.8 %collective-permute-start.19 = (bf16[64,640]{1,0:T(8,128)(2,1)S(1)}, bf16[64,640]{1,0:T(8,128)(2,1)S(1)}, u32[]{:S(2)}, u32[]{:S(2)}) collective-permute-start(bf16[64,640]{1,0:T(8,128)(2,1)S(1)} %get-tuple-element.59), channel_id=1, source_target_pairs={{0,80},{2,82},{1,81},{3,83},{4,84},{6,86},{5,85},{7,87},{8,88},{10... | collective-permute-start | bytes 245768 | tf_op jit(solution)/shard_map/ppermute | solution.py:49
  62.8 5.5 %collective-permute-start.20 = (bf16[64,640]{1,0:T(8,128)(2,1)S(1)}, bf16[64,640]{1,0:T(8,128)(2,1)S(1)}, u32[]{:S(2)}, u32[]{:S(2)}) collective-permute-start(bf16[64,640]{1,0:T(8,128)(2,1)S(1)} %get-tuple-element.60), channel_id=1, source_target_pairs={{0,64},{2,66},{1,65},{3,67},{4,68},{6,70},{5,69},{7,71},{8,72},{10... | collective-permute-start | bytes 245768 | tf_op jit(solution)/shard_map/ppermute | solution.py:49

commit v7 on v6

--- a/solution.py
+++ b/solution.py
@@ -188,10 +188,10 @@
         top = jnp.maximum(
             jnp.max(highest, axis=1, keepdims=True), jnp.max(new, axis=1, keepdims=True)
         )
-        return top * scale, new
-
-    def mix(slot, k, base, new):
-        new = jnp.exp2(new * scale - base)
+        return top, new
+
+    def mix(slot, k, top, new):
+        new = jnp.exp2((new - top) * scale)
         mixed = jnp.dot(
             new.astype(jnp.bfloat16),
             head(slot, HQ + KVH + k),
@@ -199,7 +199,7 @@
         )
         total = None
         for low in range(0, CAP, CHUNK):
-            part = jnp.exp2(scores[k % 2, :, low : low + CHUNK] * scale - base)
+            part = jnp.exp2((scores[k % 2, :, low : low + CHUNK] - top) * scale)
             values = cache[slot, low : low + CHUNK, (KVH + k) * HD : (KVH + k + 1) * HD]
             mixed = mixed + jnp.dot(
                 part.astype(jnp.bfloat16), values, preferred_element_type=jnp.float32

time: 74.9 us -> 74.9 us (level)
  no operation moved by 1% of the time
where the time goes in v7:
time: 74.9 us; the launch traced here: 74.7 us
  starting transfers between devices  34.1 us (46%)
  waiting for transfers between devices  21.6 us (29%)
  Pallas kernels  12.9 us (17%)
  local copies, waits for them, and re-layouts  3.33 us (4%)
  other arithmetic  2.67 us (4%)
    ppermute x21, starting transfers between devices, shift(): return lax.ppermute(array, AXES, pairs)  34.1 us
    ppermute x21, waiting for transfers between devices, shift(): return lax.ppermute(array, AXES, pairs)  21.6 us
    pallas_call x2, Pallas kernels, project(): pl.pallas_call(functools.partial(kernel, where), in_specs=[pl.BlockSpec(m...  6.54 us
    pallas_call x1, Pallas kernels, attend(): pl.pallas_call(attend_kernel, in_specs=[pl.BlockSpec(memory_space=pltpu.S...  6.29 us
    concatenate x1, other arithmetic, on_device(): near = jnp.concatenate([tokens, up, down])  1.5 us
  transfers between devices with their start and end apart: 21, of which 11 were waited for; matrix products, arithmetic and copies ran while one was open for 7% of the time, Pallas kernels for 6%

profile of v7, /device:TPU:1, one launch (start us, length us, event | category | flops | bytes accessed | tf_op | source)
XLA Modules:
  0.0 74.7 jit_solution(16765898581226152739)
XLA Ops:
  0.0 0.0 copy-start
  0.0 2.0 %collective-permute-start = (bf16[80,4096]{1,0:T(8,128)(2,1)}, bf16[80,4096]{1,0:T(8,128)(2,1)S(1)}, u32[]{:S(2)}, u32[]{:S(2)}) collective-permute-start(bf16[80,4096]{1,0:T(8,128)(2,1)} %bitcast.21), channel_id=1, source_target_pairs={{0,2},{2,1},{1,3},{3,0},{4,6},{6,5},{5,7},{7,4},{8,10},{10,9},{9,1... | collective-permute-start | bytes 1966088 | tf_op jit(solution)/shard_map/ppermute | solution.py:49
  2.0 1.3 %collective-permute-start.2 = (bf16[80,4096]{1,0:T(8,128)(2,1)}, bf16[80,4096]{1,0:T(8,128)(2,1)S(1)}, u32[]{:S(2)}, u32[]{:S(2)}) collective-permute-start(bf16[80,4096]{1,0:T(8,128)(2,1)} %bitcast.22), channel_id=1, source_target_pairs={{0,4},{2,6},{1,5},{3,7},{4,8},{6,10},{5,9},{7,11},{8,12},{10,14},{... | collective-permute-start | bytes 1966088 | tf_op jit(solution)/shard_map/ppermute | solution.py:49
  3.3 1.4 %collective-permute-start.5 = (bf16[80,4096]{1,0:T(8,128)(2,1)}, bf16[80,4096]{1,0:T(8,128)(2,1)S(1)}, u32[]{:S(2)}, u32[]{:S(2)}) collective-permute-start(bf16[80,4096]{1,0:T(8,128)(2,1)} %bitcast.23), channel_id=1, source_target_pairs={{0,12},{2,14},{1,13},{3,15},{4,0},{6,2},{5,1},{7,3},{8,4},{10,6},{... | collective-permute-start | bytes 1966088 | tf_op jit(solution)/shard_map/ppermute | solution.py:49
  4.8 1.5 %collective-permute-start.1 = (bf16[16,128]{1,0:T(8,128)(2,1)S(1)}, bf16[16,128]{1,0:T(8,128)(2,1)S(1)}, u32[]{:S(2)}, u32[]{:S(2)}) collective-permute-start(bf16[16,128]{1,0:T(8,128)(2,1)S(1)} %broadcast_in_dim.16), channel_id=1, source_target_pairs={{0,64},{2,66},{1,65},{3,67},{4,68},{6,70},{5,69},{7,71},{8,72},{10... | collective-permute-start | bytes 12296 | tf_op jit(solution)/shard_map/ppermute | solution.py:49
  6.3 0.1 stack.79.group_ref
  6.4 0.1 stack.70.at_ref
  6.5 0.6 collective-permute-done.1.early
  7.1 0.0 copy-start.1
  7.1 1.0 %copy-done.1 = bf16[64,4096]{1,0:T(8,128)(2,1)S(1)} copy-done((bf16[64,4096]{1,0:T(8,128)(2,1)S(1)}, bf16[64,4096]{1,0:T(8,128)(2,1)}, u32[]{:S(2)}) %copy-start.1) | copy-done | bytes 524312
  8.2 0.0 copy-start.2
  8.2 3.8 %collective-permute-start.9 = (bf16[64,4096]{1,0:T(8,128)(2,1)S(1)}, bf16[64,4096]{1,0:T(8,128)(2,1)}, u32[]{:S(2)}, u32[]{:S(2)}) collective-permute-start(bf16[64,4096]{1,0:T(8,128)(2,1)S(1)} %copy_rows.1), channel_id=1, source_target_pairs={{0,48},{2,50},{1,49},{3,51},{4,52},{6,54},{5,53},{7,55},{8,56},{10... | collective-permute-start | bytes 1572872 | tf_op jit(solution)/shard_map/ppermute | solution.py:49
  12.0 0.0 collective-permute-start.8
  12.0 0.0 copy-done
  12.0 0.6 gather_fusion
  12.7 1.3 %gather_fusion.1 = s32[4]{0:T(128)S(1)} fusion(s32[256]{0:T(256)} %param.12, s32[1024]{0:T(1024)S(1)} %pad_clamp_fusion), kind=kCustom, calls=%fused_computation.1.clone | custom fusion | bytes 48 | tf_op jit(solution)/shard_map/jit(_take)/gather | solution.py:274
  14.0 0.1 add_convert_fusion
  14.1 0.8 %dynamic-slice_convert_fusion = f32[640]{0:T(1024)S(1)} fusion(bf16[5120]{0:T(1024)(128)(2,1)} %param.10, s32[]{:T(128)S(6)} %select_n.83), kind=kLoop, calls=%fused_computation.13 | loop fusion | flops 640 | bytes 3844 | tf_op jit(solution)/shard_map/broadcast_in_dim | solution.py:271
  14.8 0.1 convert_element_type.12
  14.9 0.2 fusion
  15.1 0.1 pad_maximum_fusion.1
  15.2 2.4 %collective-permute-done.refs_1_ = bf16[80,4096]{1,0:T(8,128)(2,1)S(1)} collective-permute-done((bf16[80,4096]{1,0:T(8,128)(2,1)}, bf16[80,4096]{1,0:T(8,128)(2,1)S(1)}, u32[]{:S(2)}, u32[]{:S(2)}) %collective-permute-start) | collective-permute-done | bytes 655392 | tf_op jit(solution)/shard_map/ppermute | solution.py:49
  17.6 3.2 %collective-permute-start.3 = (bf16[80,4096]{1,0:T(8,128)(2,1)S(1)}, bf16[80,4096]{1,0:T(8,128)(2,1)S(1)}, u32[]{:S(2)}, u32[]{:S(2)}) collective-permute-start(bf16[80,4096]{1,0:T(8,128)(2,1)S(1)} %collective-permute-done.refs_1_), channel_id=1, source_target_pairs={{0,8},{2,10},{1,9},{3,11},{4,12},{6,14},{5,13},{7,15},{8,0},{10,2}... | collective-permute-start | bytes 1966088 | tf_op jit(solution)/shard_map/ppermute | solution.py:49
  20.9 0.0 collective-permute-done.2.refs_2_
  20.9 1.3 %collective-permute-start.4 = (bf16[80,4096]{1,0:T(8,128)(2,1)S(1)}, bf16[80,4096]{1,0:T(8,128)(2,1)S(1)}, u32[]{:S(2)}, u32[]{:S(2)}) collective-permute-start(bf16[80,4096]{1,0:T(8,128)(2,1)S(1)} %collective-permute-done.2.refs_2_), channel_id=1, source_target_pairs={{0,3},{2,0},{1,2},{3,1},{4,7},{6,4},{5,6},{7,5},{8,11},{10,8},{9,1... | collective-permute-start | bytes 1966088 | tf_op jit(solution)/shard_map/ppermute | solution.py:49
  22.1 0.0 collective-permute-done.5.refs_4_
  22.2 0.2 collective-permute-start.6
  22.3 0.6 collective-permute-done.9
  23.0 2.9 %collective-permute-start.7 = (bf16[64,4096]{1,0:T(8,128)(2,1)S(1)}, bf16[64,4096]{1,0:T(8,128)(2,1)S(1)}, u32[]{:S(2)}, u32[]{:S(2)}) collective-permute-start(bf16[64,4096]{1,0:T(8,128)(2,1)S(1)} %copy_rows.1), channel_id=1, source_target_pairs={{0,32},{2,34},{1,33},{3,35},{4,36},{6,38},{5,37},{7,39},{8,40},{10... | collective-permute-start | bytes 1572872 | tf_op jit(solution)/shard_map/ppermute | solution.py:49
  25.8 0.3 collective-permute-done.8
  26.2 1.5 %pad_maximum_fusion.refs_6_ = bf16[192,4096]{1,0:T(8,128)(2,1)S(1)} fusion(bf16[64,4096]{1,0:T(8,128)(2,1)} %collective-permute-done.9, bf16[64,4096]{1,0:T(8,128)(2,1)} %collective-permute-done.8, bf16[64,4096]{1,0:T(8,128)(2,1)} %rows.1), kind=kLoop, calls=%fused_computation.2 | loop fusion | flops 4718592 | bytes 3145728 | tf_op jit(solution)/shard_map/concatenate | solution.py:292
  27.7 8.2 %collective-permute-done.7.refs_7_ = bf16[64,4096]{1,0:T(8,128)(2,1)S(1)} collective-permute-done((bf16[64,4096]{1,0:T(8,128)(2,1)S(1)}, bf16[64,4096]{1,0:T(8,128)(2,1)S(1)}, u32[]{:S(2)}, u32[]{:S(2)}) %collective-permute-start.7) | collective-permute-done | bytes 524320 | tf_op jit(solution)/shard_map/ppermute | solution.py:49
  35.9 0.0 collective-permute-done.3.refs_2_
  35.9 0.0 collective-permute-done.4.refs_3_
  35.9 1.7 %collective-permute-done.6.refs_5_ = bf16[80,4096]{1,0:T(8,128)(2,1)S(1)} collective-permute-done((bf16[80,4096]{1,0:T(8,128)(2,1)S(1)}, bf16[80,4096]{1,0:T(8,128)(2,1)S(1)}, u32[]{:S(2)}, u32[]{:S(2)}) %collective-permute-start.6) | collective-permute-done | bytes 655392 | tf_op jit(solution)/shard_map/ppermute | solution.py:49
  37.6 2.9 %collective-permute-start.10 = (bf16[192,4096]{1,0:T(8,128)(2,1)S(1)}, bf16[192,4096]{1,0:T(8,128)(2,1)S(1)}, u32[]{:S(2)}, u32[]{:S(2)}) collective-permute-start(bf16[192,4096]{1,0:T(8,128)(2,1)S(1)} %pad_maximum_fusion.refs_6_), channel_id=1, source_target_pairs={{0,64},{2,66},{1,65},{3,67},{4,68},{6,70},{5,69},{7,71},{8,72},{10... | collective-permute-start | bytes 4718600 | tf_op jit(solution)/shard_map/ppermute | solution.py:49
  40.5 0.0 collective-permute-start.11
  40.5 0.5 collective-permute-start.12
  41.0 0.0 slice-start.1
  41.0 2.3 %collective-permute-start.13 = (bf16[80,2048]{1,0:T(8,128)(2,1)S(1)}, bf16[80,2048]{1,0:T(8,128)(2,1)S(1)}, u32[]{:S(2)}, u32[]{:S(2)}) collective-permute-start(bf16[80,2048]{1,0:T(8,128)(2,1)S(1)} %slice.13), channel_id=1, source_target_pairs={{0,12},{2,14},{1,13},{3,15},{4,0},{6,2},{5,1},{7,3},{8,4},{10,6},{... | collective-permute-start | bytes 983048 | tf_op jit(solution)/shard_map/ppermute | solution.py:49
  43.4 0.9 %collective-permute-done.11.refs_9_ = bf16[64,4096]{1,0:T(8,128)(2,1)S(1)} collective-permute-done((bf16[64,4096]{1,0:T(8,128)(2,1)S(1)}, bf16[64,4096]{1,0:T(8,128)(2,1)S(1)}, u32[]{:S(2)}, u32[]{:S(2)}) %collective-permute-start.11) | collective-permute-done | bytes 524320 | tf_op jit(solution)/shard_map/ppermute | solution.py:49
  44.3 0.0 collective-permute-done.10.refs_8_
  44.3 0.0 copy-done.2
  44.3 4.4 %project_first.1 = (f32[512,640]{1,0:T(8,128)S(1)}, bf16[512,4096]{1,0:T(8,128)(2,1)S(1)}) custom-call(s32[10]{0:T(128)S(1)} %stack.70.at_ref, f32[1,640]{1,0:T(1,128)S(1)} %reshape.28.bias_ref, bf16[80,4096]{1,0:T(8,128)(2,1)S(1)} %bitcast.24, bf16[80,4096]{1,0:T(8,128)(2,1)S(1)} %collective-permute-done.refs_1_, ...), custom_call_target="tpu_custom_call" | custom-call | flops 1 | bytes 1 | tf_op jit(solution)/shard_map/project_first/pallas_call | solution.py:138
  48.8 1.8 %collective-permute-done.12.refs_0_ = bf16[80,2048]{1,0:T(8,128)(2,1)S(1)} collective-permute-done((bf16[80,2048]{1,0:T(8,128)(2,1)S(1)}, bf16[80,2048]{1,0:T(8,128)(2,1)S(1)}, u32[]{:S(2)}, u32[]{:S(2)}) %collective-permute-start.12) | collective-permute-done | bytes 327712 | tf_op jit(solution)/shard_map/ppermute | solution.py:49
  50.6 0.0 collective-permute-done.13.refs_1_
  50.6 2.1 %project_last.1 = (bf16[64,640]{1,0:T(8,128)(2,1)S(1)}, bf16[64,640]{1,0:T(8,128)(2,1)S(1)}, bf16[64,640]{1,0:T(8,128)(2,1)S(1)}, bf16[64,640]{1,0:T(8,128)(2,1)...) custom-call(s32[10]{0:T(128)S(1)} %stack.70.at_ref, ...), custom_call_target="tpu_custom_call" | custom-call | flops 1 | bytes 1 | tf_op jit(solution)/shard_map/project_last/pallas_call | solution.py:138
  52.7 3.7 %collective-permute-start.14 = (bf16[64,640]{1,0:T(8,128)(2,1)S(1)}, bf16[64,640]{1,0:T(8,128)(2,1)S(1)}, u32[]{:S(2)}, u32[]{:S(2)}) collective-permute-start(bf16[64,640]{1,0:T(8,128)(2,1)S(1)} %get-tuple-element.54), channel_id=1, source_target_pairs={{0,32},{2,34},{1,33},{3,35},{4,36},{6,38},{5,37},{7,39},{8,40},{10... | collective-permute-start | bytes 245768 | tf_op jit(solution)/shard_map/ppermute | solution.py:49
  56.4 1.3 %collective-permute-start.15 = (bf16[64,640]{1,0:T(8,128)(2,1)S(1)}, bf16[64,640]{1,0:T(8,128)(2,1)S(1)}, u32[]{:S(2)}, u32[]{:S(2)}) collective-permute-start(bf16[64,640]{1,0:T(8,128)(2,1)S(1)} %get-tuple-element.55), channel_id=1, source_target_pairs={{0,96},{2,98},{1,97},{3,99},{4,100},{6,102},{5,101},{7,103},{8,104... | collective-permute-start | bytes 245768 | tf_op jit(solution)/shard_map/ppermute | solution.py:49
  57.7 3.3 %collective-permute-start.16 = (bf16[64,640]{1,0:T(8,128)(2,1)S(1)}, bf16[64,640]{1,0:T(8,128)(2,1)S(1)}, u32[]{:S(2)}, u32[]{:S(2)}) collective-permute-start(bf16[64,640]{1,0:T(8,128)(2,1)S(1)} %get-tuple-element.56), channel_id=1, source_target_pairs={{0,48},{2,50},{1,49},{3,51},{4,52},{6,54},{5,53},{7,55},{8,56},{10... | collective-permute-start | bytes 245768 | tf_op jit(solution)/shard_map/ppermute | solution.py:49
  61.0 0.0 collective-permute-start.17
  61.0 0.5 collective-permute-start.18
  61.5 0.0 collective-permute-done.14.refs_0_
  61.5 1.3 %collective-permute-start.19 = (bf16[64,640]{1,0:T(8,128)(2,1)S(1)}, bf16[64,640]{1,0:T(8,128)(2,1)S(1)}, u32[]{:S(2)}, u32[]{:S(2)}) collective-permute-start(bf16[64,640]{1,0:T(8,128)(2,1)S(1)} %get-tuple-element.59), channel_id=1, source_target_pairs={{0,80},{2,82},{1,81},{3,83},{4,84},{6,86},{5,85},{7,87},{8,88},{10... | collective-permute-start | bytes 245768 | tf_op jit(solution)/shard_map/ppermute | solution.py:49
  62.8 0.0 collective-permute-done.15.refs_1_
  62.8 0.6 collective-permute-start.20
  63.4 0.3 collective-permute-done.16.refs_2_
  63.7 2.6 %collective-permute-done.17.refs_3_ = bf16[64,640]{1,0:T(8,128)(2,1)S(1)} collective-permute-done((bf16[64,640]{1,0:T(8,128)(2,1)S(1)}, bf16[64,640]{1,0:T(8,128)(2,1)S(1)}, u32[]{:S(2)}, u32[]{:S(2)}) %collective-permute-start.17) | collective-permute-done | bytes 81952 | tf_op jit(solution)/shard_map/ppermute | solution.py:49
  66.3 0.0 collective-permute-done.18.refs_4_
  66.3 2.1 %collective-permute-done.19.refs_5_ = bf16[64,640]{1,0:T(8,128)(2,1)S(1)} collective-permute-done((bf16[64,640]{1,0:T(8,128)(2,1)S(1)}, bf16[64,640]{1,0:T(8,128)(2,1)S(1)}, u32[]{:S(2)}, u32[]{:S(2)}) %collective-permute-start.19) | collective-permute-done | bytes 81952 | tf_op jit(solution)/shard_map/ppermute | solution.py:49
  68.4 0.0 collective-permute-done.20.refs_6_
  68.4 0.0 slice-done
  68.4 0.0 slice-done.1
  68.4 6.3 %attend.1 = bf16[64,4096]{1,0:T(8,128)(2,1)} custom-call(s32[8]{0:T(128)S(1)} %stack.79.group_ref, s32[4]{0:T(128)S(1)} %and_select_fusion.length_ref, f32[64,128]{1,0:T(8,128)S(1)} %get-tuple-element.40.cos_ref, f32[64,128]{1,0:T(8,128)S(1)} %get-tuple-element.41.sin_ref, bf16[4,1024,1024]{2,1,0:T(8,128)(2,1)S(1)} %bitcast.20, ...), custom_call_target="tpu_custom_call" | custom-call | tf_op jit(solution)/shard_map/attend/pallas_call | solution.py:230
  (13 shorter events, 0.2 us)
Async XLA Ops:
  0.0 12.0 %copy-start = (s32[256]{0:T(256)S(1)}, s32[256]{0:T(256)}, u32[]{:S(2)}) copy-start(s32[256]{0:T(256)} %param.13) | copy-start | bytes 3076
  0.0 17.6 %collective-permute-start = (bf16[80,4096]{1,0:T(8,128)(2,1)}, bf16[80,4096]{1,0:T(8,128)(2,1)S(1)}, u32[]{:S(2)}, u32[]{:S(2)}) collective-permute-start(bf16[80,4096]{1,0:T(8,128)(2,1)} %bitcast.21), channel_id=1, source_target_pairs={{0,2},{2,1},{1,3},{3,0},{4,6},{6,5},{5,7},{7,4},{8,10},{10,9},{9,1... | collective-permute-start | bytes 1966088 | tf_op jit(solution)/shard_map/ppermute | solution.py:49
  2.0 18.8 %collective-permute-start.2 = (bf16[80,4096]{1,0:T(8,128)(2,1)}, bf16[80,4096]{1,0:T(8,128)(2,1)S(1)}, u32[]{:S(2)}, u32[]{:S(2)}) collective-permute-start(bf16[80,4096]{1,0:T(8,128)(2,1)} %bitcast.22), channel_id=1, source_target_pairs={{0,4},{2,6},{1,5},{3,7},{4,8},{6,10},{5,9},{7,11},{8,12},{10,14},{... | collective-permute-start | bytes 1966088 | tf_op jit(solution)/shard_map/ppermute | solution.py:49
  3.3 18.8 %collective-permute-start.5 = (bf16[80,4096]{1,0:T(8,128)(2,1)}, bf16[80,4096]{1,0:T(8,128)(2,1)S(1)}, u32[]{:S(2)}, u32[]{:S(2)}) collective-permute-start(bf16[80,4096]{1,0:T(8,128)(2,1)} %bitcast.23), channel_id=1, source_target_pairs={{0,12},{2,14},{1,13},{3,15},{4,0},{6,2},{5,1},{7,3},{8,4},{10,6},{... | collective-permute-start | bytes 1966088 | tf_op jit(solution)/shard_map/ppermute | solution.py:49
  4.8 2.3 %collective-permute-start.1 = (bf16[16,128]{1,0:T(8,128)(2,1)S(1)}, bf16[16,128]{1,0:T(8,128)(2,1)S(1)}, u32[]{:S(2)}, u32[]{:S(2)}) collective-permute-start(bf16[16,128]{1,0:T(8,128)(2,1)S(1)} %broadcast_in_dim.16), channel_id=1, source_target_pairs={{0,64},{2,66},{1,65},{3,67},{4,68},{6,70},{5,69},{7,71},{8,72},{10... | collective-permute-start | bytes 12296 | tf_op jit(solution)/shard_map/ppermute | solution.py:49
  7.1 1.0 %copy-start.1 = (bf16[64,4096]{1,0:T(8,128)(2,1)S(1)}, bf16[64,4096]{1,0:T(8,128)(2,1)}, u32[]{:S(2)}) copy-start(bf16[64,4096]{1,0:T(8,128)(2,1)} %rows.1) | copy-start | bytes 1572868
  8.2 36.1 %copy-start.2 = (bf16[4096,80]{0,1:T(8,128)(2,1)S(1)}, bf16[4096,80]{0,1:T(8,128)(2,1)}, u32[]{:S(2)}) copy-start(bf16[4096,80]{0,1:T(8,128)(2,1)} %param.9) | copy-start | bytes 1966084
  8.2 14.8 %collective-permute-start.9 = (bf16[64,4096]{1,0:T(8,128)(2,1)S(1)}, bf16[64,4096]{1,0:T(8,128)(2,1)}, u32[]{:S(2)}, u32[]{:S(2)}) collective-permute-start(bf16[64,4096]{1,0:T(8,128)(2,1)S(1)} %copy_rows.1), channel_id=1, source_target_pairs={{0,48},{2,50},{1,49},{3,51},{4,52},{6,54},{5,53},{7,55},{8,56},{10... | collective-permute-start | bytes 1572872 | tf_op jit(solution)/shard_map/ppermute | solution.py:49
  12.0 14.2 %collective-permute-start.8 = (bf16[64,4096]{1,0:T(8,128)(2,1)S(1)}, bf16[64,4096]{1,0:T(8,128)(2,1)}, u32[]{:S(2)}, u32[]{:S(2)}) collective-permute-start(bf16[64,4096]{1,0:T(8,128)(2,1)S(1)} %copy_rows.1), channel_id=1, source_target_pairs={{0,16},{2,18},{1,17},{3,19},{4,20},{6,22},{5,21},{7,23},{8,24},{10... | collective-permute-start | bytes 1572872 | tf_op jit(solution)/shard_map/ppermute | solution.py:49
  17.6 18.2 %collective-permute-start.3 = (bf16[80,4096]{1,0:T(8,128)(2,1)S(1)}, bf16[80,4096]{1,0:T(8,128)(2,1)S(1)}, u32[]{:S(2)}, u32[]{:S(2)}) collective-permute-start(bf16[80,4096]{1,0:T(8,128)(2,1)S(1)} %collective-permute-done.refs_1_), channel_id=1, source_target_pairs={{0,8},{2,10},{1,9},{3,11},{4,12},{6,14},{5,13},{7,15},{8,0},{10,2}... | collective-permute-start | bytes 1966088 | tf_op jit(solution)/shard_map/ppermute | solution.py:49
  20.9 15.0 %collective-permute-start.4 = (bf16[80,4096]{1,0:T(8,128)(2,1)S(1)}, bf16[80,4096]{1,0:T(8,128)(2,1)S(1)}, u32[]{:S(2)}, u32[]{:S(2)}) collective-permute-start(bf16[80,4096]{1,0:T(8,128)(2,1)S(1)} %collective-permute-done.2.refs_2_), channel_id=1, source_target_pairs={{0,3},{2,0},{1,2},{3,1},{4,7},{6,4},{5,6},{7,5},{8,11},{10,8},{9,1... | collective-permute-start | bytes 1966088 | tf_op jit(solution)/shard_map/ppermute | solution.py:49
  22.2 15.4 %collective-permute-start.6 = (bf16[80,4096]{1,0:T(8,128)(2,1)S(1)}, bf16[80,4096]{1,0:T(8,128)(2,1)S(1)}, u32[]{:S(2)}, u32[]{:S(2)}) collective-permute-start(bf16[80,4096]{1,0:T(8,128)(2,1)S(1)} %collective-permute-done.5.refs_4_), channel_id=1, source_target_pairs={{0,2},{2,1},{1,3},{3,0},{4,6},{6,5},{5,7},{7,4},{8,10},{10,9},{9,1... | collective-permute-start | bytes 1966088 | tf_op jit(solution)/shard_map/ppermute | solution.py:49
  23.0 12.9 %collective-permute-start.7 = (bf16[64,4096]{1,0:T(8,128)(2,1)S(1)}, bf16[64,4096]{1,0:T(8,128)(2,1)S(1)}, u32[]{:S(2)}, u32[]{:S(2)}) collective-permute-start(bf16[64,4096]{1,0:T(8,128)(2,1)S(1)} %copy_rows.1), channel_id=1, source_target_pairs={{0,32},{2,34},{1,33},{3,35},{4,36},{6,38},{5,37},{7,39},{8,40},{10... | collective-permute-start | bytes 1572872 | tf_op jit(solution)/shard_map/ppermute | solution.py:49
  37.6 6.7 %collective-permute-start.10 = (bf16[192,4096]{1,0:T(8,128)(2,1)S(1)}, bf16[192,4096]{1,0:T(8,128)(2,1)S(1)}, u32[]{:S(2)}, u32[]{:S(2)}) collective-permute-start(bf16[192,4096]{1,0:T(8,128)(2,1)S(1)} %pad_maximum_fusion.refs_6_), channel_id=1, source_target_pairs={{0,64},{2,66},{1,65},{3,67},{4,68},{6,70},{5,69},{7,71},{8,72},{10... | collective-permute-start | bytes 4718600 | tf_op jit(solution)/shard_map/ppermute | solution.py:49
  40.5 3.8 %collective-permute-start.11 = (bf16[64,4096]{1,0:T(8,128)(2,1)S(1)}, bf16[64,4096]{1,0:T(8,128)(2,1)S(1)}, u32[]{:S(2)}, u32[]{:S(2)}) collective-permute-start(bf16[64,4096]{1,0:T(8,128)(2,1)S(1)} %collective-permute-done.7.refs_7_), channel_id=1, source_target_pairs={{0,64},{2,66},{1,65},{3,67},{4,68},{6,70},{5,69},{7,71},{8,72},{10... | collective-permute-start | bytes 1572872 | tf_op jit(solution)/shard_map/ppermute | solution.py:49
  40.5 10.0 %collective-permute-start.12 = (bf16[80,2048]{1,0:T(8,128)(2,1)S(1)}, bf16[80,2048]{1,0:T(8,128)(2,1)S(1)}, u32[]{:S(2)}, u32[]{:S(2)}) collective-permute-start(bf16[80,2048]{1,0:T(8,128)(2,1)S(1)} %slice.12), channel_id=1, source_target_pairs={{0,4},{2,6},{1,5},{3,7},{4,8},{6,10},{5,9},{7,11},{8,12},{10,14},{... | collective-permute-start | bytes 983048 | tf_op jit(solution)/shard_map/ppermute | solution.py:49
  41.0 27.4 %slice-start = ((s8[8388608]{0:T(1024)(128)(4,1)}), s8[4194304]{0:T(1024)(128)(4,1)S(1)}, s32[]{:S(2)}) async-start(s8[8388608]{0:T(1024)(128)(4,1)} %bitcast.19), calls=%async_computation | async-start | bytes 8388608
  41.0 27.3 %slice-start.1 = ((s8[8388608]{0:T(1024)(128)(4,1)}), s8[4194304]{0:T(1024)(128)(4,1)S(1)}, s32[]{:S(2)}) async-start(s8[8388608]{0:T(1024)(128)(4,1)} %bitcast.19), calls=%async_computation.1 | async-start | bytes 8388608
  41.0 9.5 %collective-permute-start.13 = (bf16[80,2048]{1,0:T(8,128)(2,1)S(1)}, bf16[80,2048]{1,0:T(8,128)(2,1)S(1)}, u32[]{:S(2)}, u32[]{:S(2)}) collective-permute-start(bf16[80,2048]{1,0:T(8,128)(2,1)S(1)} %slice.13), channel_id=1, source_target_pairs={{0,12},{2,14},{1,13},{3,15},{4,0},{6,2},{5,1},{7,3},{8,4},{10,6},{... | collective-permute-start | bytes 983048 | tf_op jit(solution)/shard_map/ppermute | solution.py:49
  52.7 8.8 %collective-permute-start.14 = (bf16[64,640]{1,0:T(8,128)(2,1)S(1)}, bf16[64,640]{1,0:T(8,128)(2,1)S(1)}, u32[]{:S(2)}, u32[]{:S(2)}) collective-permute-start(bf16[64,640]{1,0:T(8,128)(2,1)S(1)} %get-tuple-element.54), channel_id=1, source_target_pairs={{0,32},{2,34},{1,33},{3,35},{4,36},{6,38},{5,37},{7,39},{8,40},{10... | collective-permute-start | bytes 245768 | tf_op jit(solution)/shard_map/ppermute | solution.py:49
  56.4 6.4 %collective-permute-start.15 = (bf16[64,640]{1,0:T(8,128)(2,1)S(1)}, bf16[64,640]{1,0:T(8,128)(2,1)S(1)}, u32[]{:S(2)}, u32[]{:S(2)}) collective-permute-start(bf16[64,640]{1,0:T(8,128)(2,1)S(1)} %get-tuple-element.55), channel_id=1, source_target_pairs={{0,96},{2,98},{1,97},{3,99},{4,100},{6,102},{5,101},{7,103},{8,104... | collective-permute-start | bytes 245768 | tf_op jit(solution)/shard_map/ppermute | solution.py:49
  57.7 6.0 %collective-permute-start.16 = (bf16[64,640]{1,0:T(8,128)(2,1)S(1)}, bf16[64,640]{1,0:T(8,128)(2,1)S(1)}, u32[]{:S(2)}, u32[]{:S(2)}) collective-permute-start(bf16[64,640]{1,0:T(8,128)(2,1)S(1)} %get-tuple-element.56), channel_id=1, source_target_pairs={{0,48},{2,50},{1,49},{3,51},{4,52},{6,54},{5,53},{7,55},{8,56},{10... | collective-permute-start | bytes 245768 | tf_op jit(solution)/shard_map/ppermute | solution.py:49
  61.0 5.3 %collective-permute-start.17 = (bf16[64,640]{1,0:T(8,128)(2,1)S(1)}, bf16[64,640]{1,0:T(8,128)(2,1)S(1)}, u32[]{:S(2)}, u32[]{:S(2)}) collective-permute-start(bf16[64,640]{1,0:T(8,128)(2,1)S(1)} %get-tuple-element.57), channel_id=1, source_target_pairs={{0,112},{2,114},{1,113},{3,115},{4,116},{6,118},{5,117},{7,119},{8... | collective-permute-start | bytes 245768 | tf_op jit(solution)/shard_map/ppermute | solution.py:49
  61.0 5.3 %collective-permute-start.18 = (bf16[64,640]{1,0:T(8,128)(2,1)S(1)}, bf16[64,640]{1,0:T(8,128)(2,1)S(1)}, u32[]{:S(2)}, u32[]{:S(2)}) collective-permute-start(bf16[64,640]{1,0:T(8,128)(2,1)S(1)} %get-tuple-element.58), channel_id=1, source_target_pairs={{0,16},{2,18},{1,17},{3,19},{4,20},{6,22},{5,21},{7,23},{8,24},{10... | collective-permute-start | bytes 245768 | tf_op jit(solution)/shard_map/ppermute | solution.py:49
  61.5 6.8 %collective-permute-start.19 = (bf16[64,640]{1,0:T(8,128)(2,1)S(1)}, bf16[64,640]{1,0:T(8,128)(2,1)S(1)}, u32[]{:S(2)}, u32[]{:S(2)}) collective-permute-start(bf16[64,640]{1,0:T(8,128)(2,1)S(1)} %get-tuple-element.59), channel_id=1, source_target_pairs={{0,80},{2,82},{1,81},{3,83},{4,84},{6,86},{5,85},{7,87},{8,88},{10... | collective-permute-start | bytes 245768 | tf_op jit(solution)/shard_map/ppermute | solution.py:49
  62.8 5.5 %collective-permute-start.20 = (bf16[64,640]{1,0:T(8,128)(2,1)S(1)}, bf16[64,640]{1,0:T(8,128)(2,1)S(1)}, u32[]{:S(2)}, u32[]{:S(2)}) collective-permute-start(bf16[64,640]{1,0:T(8,128)(2,1)S(1)} %get-tuple-element.60), channel_id=1, source_target_pairs={{0,64},{2,66},{1,65},{3,67},{4,68},{6,70},{5,69},{7,71},{8,72},{10... | collective-permute-start | bytes 245768 | tf_op jit(solution)/shard_map/ppermute | solution.py:49

commit v8 on v7

--- a/solution.py
+++ b/solution.py
@@ -282,8 +282,8 @@
     sine = jnp.concatenate([-sine, sine], axis=1)
 
     up, down = shift(late, dz=1), shift(late, dz=3)
-    own_side, tokens, late, small = lax.optimization_barrier(
-        (own_side, tokens, late, (places, groups, bias_cols, my_lengths, cosine, sine))
+    one, tokens, late, small = lax.optimization_barrier(
+        (one, tokens, late, (places, groups, bias_cols, my_lengths, cosine, sine))
     )
     places, groups, bias_cols, my_lengths, cosine, sine = small
     far = shift(late, dz=2)

time: 74.9 us -> 74.9 us (level)
  starting transfers between devices: 34.1 us -> 33.3 us
    ppermute x21, waiting for transfers between devices: 21.6 us -> 22.3 us  [shift(): return lax.ppermute(array, AXES, pairs)]
    ppermute x21, starting transfers between devices: 34.1 us -> 33.3 us  [shift(): return lax.ppermute(array, AXES, pairs)]
  transfers between devices with their start and end apart: 21 -> 21, of which waited for: 11 -> 12; matrix products, arithmetic and copies ran while one was open for 7% -> 7% of each run, Pallas kernels for 6% -> 6%
where the time goes in v8:
time: 74.9 us; the launch traced here: 74.7 us
  starting transfers between devices  33.3 us (44%)
  waiting for transfers between devices  22.3 us (30%)
  Pallas kernels  12.9 us (17%)
  local copies, waits for them, and re-layouts  3.33 us (4%)
  other arithmetic  2.67 us (4%)
    ppermute x21, starting transfers between devices, shift(): return lax.ppermute(array, AXES, pairs)  33.3 us
    ppermute x21, waiting for transfers between devices, shift(): return lax.ppermute(array, AXES, pairs)  22.3 us
    pallas_call x2, Pallas kernels, project(): pl.pallas_call(functools.partial(kernel, where), in_specs=[pl.BlockSpec(m...  6.54 us
    pallas_call x1, Pallas kernels, attend(): pl.pallas_call(attend_kernel, in_specs=[pl.BlockSpec(memory_space=pltpu.S...  6.29 us
    concatenate x1, other arithmetic, on_device(): near = jnp.concatenate([tokens, up, down])  1.5 us
  transfers between devices with their start and end apart: 21, of which 12 were waited for; matrix products, arithmetic and copies ran while one was open for 7% of the time, Pallas kernels for 6%

profile of v8, /device:TPU:1, one launch (start us, length us, event | category | flops | bytes accessed | tf_op | source)
XLA Modules:
  0.0 74.7 jit_solution(6753134945575504107)
XLA Ops:
  0.0 0.0 copy-start
  0.0 2.1 %collective-permute-start = (bf16[80,4096]{1,0:T(8,128)(2,1)}, bf16[80,4096]{1,0:T(8,128)(2,1)S(1)}, u32[]{:S(2)}, u32[]{:S(2)}) collective-permute-start(bf16[80,4096]{1,0:T(8,128)(2,1)} %bitcast.21), channel_id=1, source_target_pairs={{0,4},{2,6},{1,5},{3,7},{4,8},{6,10},{5,9},{7,11},{8,12},{10,14},{... | collective-permute-start | bytes 1966088 | tf_op jit(solution)/shard_map/ppermute | solution.py:49
  2.1 1.2 %collective-permute-start.2 = (bf16[80,4096]{1,0:T(8,128)(2,1)}, bf16[80,4096]{1,0:T(8,128)(2,1)S(1)}, u32[]{:S(2)}, u32[]{:S(2)}) collective-permute-start(bf16[80,4096]{1,0:T(8,128)(2,1)} %bitcast.22), channel_id=1, source_target_pairs={{0,2},{2,1},{1,3},{3,0},{4,6},{6,5},{5,7},{7,4},{8,10},{10,9},{9,1... | collective-permute-start | bytes 1966088 | tf_op jit(solution)/shard_map/ppermute | solution.py:49
  3.3 1.5 %collective-permute-start.5 = (bf16[80,4096]{1,0:T(8,128)(2,1)}, bf16[80,4096]{1,0:T(8,128)(2,1)S(1)}, u32[]{:S(2)}, u32[]{:S(2)}) collective-permute-start(bf16[80,4096]{1,0:T(8,128)(2,1)} %bitcast.23), channel_id=1, source_target_pairs={{0,12},{2,14},{1,13},{3,15},{4,0},{6,2},{5,1},{7,3},{8,4},{10,6},{... | collective-permute-start | bytes 1966088 | tf_op jit(solution)/shard_map/ppermute | solution.py:49
  4.9 1.4 %collective-permute-start.1 = (bf16[16,128]{1,0:T(8,128)(2,1)S(1)}, bf16[16,128]{1,0:T(8,128)(2,1)S(1)}, u32[]{:S(2)}, u32[]{:S(2)}) collective-permute-start(bf16[16,128]{1,0:T(8,128)(2,1)S(1)} %broadcast_in_dim.16), channel_id=1, source_target_pairs={{0,64},{2,66},{1,65},{3,67},{4,68},{6,70},{5,69},{7,71},{8,72},{10... | collective-permute-start | bytes 12296 | tf_op jit(solution)/shard_map/ppermute | solution.py:49
  6.3 0.1 stack.79.group_ref
  6.4 0.1 stack.70.at_ref
  6.5 0.6 collective-permute-done.1.early
  7.1 0.0 copy-start.1
  7.1 1.0 %copy-done.1 = bf16[64,4096]{1,0:T(8,128)(2,1)S(1)} copy-done((bf16[64,4096]{1,0:T(8,128)(2,1)S(1)}, bf16[64,4096]{1,0:T(8,128)(2,1)}, u32[]{:S(2)}) %copy-start.1) | copy-done | bytes 524312
  8.2 0.0 copy-start.2
  8.2 3.8 %collective-permute-start.9 = (bf16[64,4096]{1,0:T(8,128)(2,1)S(1)}, bf16[64,4096]{1,0:T(8,128)(2,1)}, u32[]{:S(2)}, u32[]{:S(2)}) collective-permute-start(bf16[64,4096]{1,0:T(8,128)(2,1)S(1)} %copy_rows.1), channel_id=1, source_target_pairs={{0,48},{2,50},{1,49},{3,51},{4,52},{6,54},{5,53},{7,55},{8,56},{10... | collective-permute-start | bytes 1572872 | tf_op jit(solution)/shard_map/ppermute | solution.py:49
  12.0 0.0 collective-permute-start.8
  12.0 0.0 copy-done
  12.0 0.6 gather_fusion
  12.7 1.3 %gather_fusion.1 = s32[4]{0:T(128)S(1)} fusion(s32[256]{0:T(256)} %param.12, s32[1024]{0:T(1024)S(1)} %pad_clamp_fusion), kind=kCustom, calls=%fused_computation.1.clone | custom fusion | bytes 48 | tf_op jit(solution)/shard_map/jit(_take)/gather | solution.py:274
  14.0 0.1 add_convert_fusion
  14.1 0.8 %dynamic-slice_convert_fusion = f32[640]{0:T(1024)S(1)} fusion(bf16[5120]{0:T(1024)(128)(2,1)} %param.10, s32[]{:T(128)S(6)} %select_n.83), kind=kLoop, calls=%fused_computation.13 | loop fusion | flops 640 | bytes 3844 | tf_op jit(solution)/shard_map/broadcast_in_dim | solution.py:271
  14.8 0.1 convert_element_type.12
  14.9 0.2 fusion
  15.1 0.1 pad_maximum_fusion.1
  15.2 3.0 %collective-permute-done.refs_2_ = bf16[80,4096]{1,0:T(8,128)(2,1)S(1)} collective-permute-done((bf16[80,4096]{1,0:T(8,128)(2,1)}, bf16[80,4096]{1,0:T(8,128)(2,1)S(1)}, u32[]{:S(2)}, u32[]{:S(2)}) %collective-permute-start) | collective-permute-done | bytes 655392 | tf_op jit(solution)/shard_map/ppermute | solution.py:49
  18.2 2.4 %collective-permute-start.4 = (bf16[80,4096]{1,0:T(8,128)(2,1)S(1)}, bf16[80,4096]{1,0:T(8,128)(2,1)S(1)}, u32[]{:S(2)}, u32[]{:S(2)}) collective-permute-start(bf16[80,4096]{1,0:T(8,128)(2,1)S(1)} %collective-permute-done.refs_2_), channel_id=1, source_target_pairs={{0,3},{2,0},{1,2},{3,1},{4,7},{6,4},{5,6},{7,5},{8,11},{10,8},{9,1... | collective-permute-start | bytes 1966088 | tf_op jit(solution)/shard_map/ppermute | solution.py:49
  20.6 0.0 collective-permute-done.2.refs_1_
  20.6 1.6 %collective-permute-start.3 = (bf16[80,4096]{1,0:T(8,128)(2,1)S(1)}, bf16[80,4096]{1,0:T(8,128)(2,1)S(1)}, u32[]{:S(2)}, u32[]{:S(2)}) collective-permute-start(bf16[80,4096]{1,0:T(8,128)(2,1)S(1)} %collective-permute-done.2.refs_1_), channel_id=1, source_target_pairs={{0,8},{2,10},{1,9},{3,11},{4,12},{6,14},{5,13},{7,15},{8,0},{10,2}... | collective-permute-start | bytes 1966088 | tf_op jit(solution)/shard_map/ppermute | solution.py:49
  22.1 0.0 collective-permute-done.5.refs_4_
  22.2 0.0 collective-permute-start.6
  22.2 0.8 %collective-permute-done.9 = bf16[64,4096]{1,0:T(8,128)(2,1)} collective-permute-done((bf16[64,4096]{1,0:T(8,128)(2,1)S(1)}, bf16[64,4096]{1,0:T(8,128)(2,1)}, u32[]{:S(2)}, u32[]{:S(2)}) %collective-permute-start.9) | collective-permute-done | bytes 524320 | tf_op jit(solution)/shard_map/ppermute | solution.py:49
  23.0 2.9 %collective-permute-start.7 = (bf16[64,4096]{1,0:T(8,128)(2,1)S(1)}, bf16[64,4096]{1,0:T(8,128)(2,1)S(1)}, u32[]{:S(2)}, u32[]{:S(2)}) collective-permute-start(bf16[64,4096]{1,0:T(8,128)(2,1)S(1)} %copy_rows.1), channel_id=1, source_target_pairs={{0,32},{2,34},{1,33},{3,35},{4,36},{6,38},{5,37},{7,39},{8,40},{10... | collective-permute-start | bytes 1572872 | tf_op jit(solution)/shard_map/ppermute | solution.py:49
  25.8 0.3 collective-permute-done.8
  26.2 1.5 %pad_maximum_fusion.refs_6_ = bf16[192,4096]{1,0:T(8,128)(2,1)S(1)} fusion(bf16[64,4096]{1,0:T(8,128)(2,1)} %collective-permute-done.9, bf16[64,4096]{1,0:T(8,128)(2,1)} %collective-permute-done.8, bf16[64,4096]{1,0:T(8,128)(2,1)} %rows.1), kind=kLoop, calls=%fused_computation.2 | loop fusion | flops 4718592 | bytes 3145728 | tf_op jit(solution)/shard_map/concatenate | solution.py:292
  27.7 8.6 %collective-permute-done.7.refs_7_ = bf16[64,4096]{1,0:T(8,128)(2,1)S(1)} collective-permute-done((bf16[64,4096]{1,0:T(8,128)(2,1)S(1)}, bf16[64,4096]{1,0:T(8,128)(2,1)S(1)}, u32[]{:S(2)}, u32[]{:S(2)}) %collective-permute-start.7) | collective-permute-done | bytes 524320 | tf_op jit(solution)/shard_map/ppermute | solution.py:49
  36.3 0.4 collective-permute-done.3.refs_2_
  36.7 0.0 collective-permute-done.4.refs_3_
  36.7 0.9 %collective-permute-done.6.refs_5_ = bf16[80,4096]{1,0:T(8,128)(2,1)S(1)} collective-permute-done((bf16[80,4096]{1,0:T(8,128)(2,1)S(1)}, bf16[80,4096]{1,0:T(8,128)(2,1)S(1)}, u32[]{:S(2)}, u32[]{:S(2)}) %collective-permute-start.6) | collective-permute-done | bytes 655392 | tf_op jit(solution)/shard_map/ppermute | solution.py:49
  37.6 2.9 %collective-permute-start.10 = (bf16[192,4096]{1,0:T(8,128)(2,1)S(1)}, bf16[192,4096]{1,0:T(8,128)(2,1)S(1)}, u32[]{:S(2)}, u32[]{:S(2)}) collective-permute-start(bf16[192,4096]{1,0:T(8,128)(2,1)S(1)} %pad_maximum_fusion.refs_6_), channel_id=1, source_target_pairs={{0,64},{2,66},{1,65},{3,67},{4,68},{6,70},{5,69},{7,71},{8,72},{10... | collective-permute-start | bytes 4718600 | tf_op jit(solution)/shard_map/ppermute | solution.py:49
  40.5 0.0 collective-permute-start.11
  40.5 0.5 collective-permute-start.12
  41.0 0.0 slice-start.1
  41.0 2.3 %collective-permute-start.13 = (bf16[80,2048]{1,0:T(8,128)(2,1)S(1)}, bf16[80,2048]{1,0:T(8,128)(2,1)S(1)}, u32[]{:S(2)}, u32[]{:S(2)}) collective-permute-start(bf16[80,2048]{1,0:T(8,128)(2,1)S(1)} %slice.12), channel_id=1, source_target_pairs={{0,12},{2,14},{1,13},{3,15},{4,0},{6,2},{5,1},{7,3},{8,4},{10,6},{... | collective-permute-start | bytes 983048 | tf_op jit(solution)/shard_map/ppermute | solution.py:49
  43.4 0.9 %collective-permute-done.11.refs_9_ = bf16[64,4096]{1,0:T(8,128)(2,1)S(1)} collective-permute-done((bf16[64,4096]{1,0:T(8,128)(2,1)S(1)}, bf16[64,4096]{1,0:T(8,128)(2,1)S(1)}, u32[]{:S(2)}, u32[]{:S(2)}) %collective-permute-start.11) | collective-permute-done | bytes 524320 | tf_op jit(solution)/shard_map/ppermute | solution.py:49
  44.3 0.0 collective-permute-done.10.refs_8_
  44.3 0.0 copy-done.2
  44.3 4.4 %project_first.1 = (f32[512,640]{1,0:T(8,128)S(1)}, bf16[512,4096]{1,0:T(8,128)(2,1)S(1)}) custom-call(s32[10]{0:T(128)S(1)} %stack.70.at_ref, f32[1,640]{1,0:T(1,128)S(1)} %reshape.28.bias_ref, bf16[80,4096]{1,0:T(8,128)(2,1)S(1)} %bitcast.24, bf16[80,4096]{1,0:T(8,128)(2,1)S(1)} %collective-permute-done.2.refs_1_, ...), custom_call_target="tpu_custom_call" | custom-call | flops 1 | bytes 1 | tf_op jit(solution)/shard_map/project_first/pallas_call | solution.py:138
  48.8 1.8 %collective-permute-done.12.refs_0_ = bf16[80,2048]{1,0:T(8,128)(2,1)S(1)} collective-permute-done((bf16[80,2048]{1,0:T(8,128)(2,1)S(1)}, bf16[80,2048]{1,0:T(8,128)(2,1)S(1)}, u32[]{:S(2)}, u32[]{:S(2)}) %collective-permute-start.12) | collective-permute-done | bytes 327712 | tf_op jit(solution)/shard_map/ppermute | solution.py:49
  50.6 0.0 collective-permute-done.13.refs_1_
  50.6 2.1 %project_last.1 = (bf16[64,640]{1,0:T(8,128)(2,1)S(1)}, bf16[64,640]{1,0:T(8,128)(2,1)S(1)}, bf16[64,640]{1,0:T(8,128)(2,1)S(1)}, bf16[64,640]{1,0:T(8,128)(2,1)...) custom-call(s32[10]{0:T(128)S(1)} %stack.70.at_ref, ...), custom_call_target="tpu_custom_call" | custom-call | flops 1 | bytes 1 | tf_op jit(solution)/shard_map/project_last/pallas_call | solution.py:138
  52.7 3.7 %collective-permute-start.14 = (bf16[64,640]{1,0:T(8,128)(2,1)S(1)}, bf16[64,640]{1,0:T(8,128)(2,1)S(1)}, u32[]{:S(2)}, u32[]{:S(2)}) collective-permute-start(bf16[64,640]{1,0:T(8,128)(2,1)S(1)} %get-tuple-element.54), channel_id=1, source_target_pairs={{0,32},{2,34},{1,33},{3,35},{4,36},{6,38},{5,37},{7,39},{8,40},{10... | collective-permute-start | bytes 245768 | tf_op jit(solution)/shard_map/ppermute | solution.py:49
  56.4 1.3 %collective-permute-start.15 = (bf16[64,640]{1,0:T(8,128)(2,1)S(1)}, bf16[64,640]{1,0:T(8,128)(2,1)S(1)}, u32[]{:S(2)}, u32[]{:S(2)}) collective-permute-start(bf16[64,640]{1,0:T(8,128)(2,1)S(1)} %get-tuple-element.55), channel_id=1, source_target_pairs={{0,96},{2,98},{1,97},{3,99},{4,100},{6,102},{5,101},{7,103},{8,104... | collective-permute-start | bytes 245768 | tf_op jit(solution)/shard_map/ppermute | solution.py:49
  57.7 3.3 %collective-permute-start.16 = (bf16[64,640]{1,0:T(8,128)(2,1)S(1)}, bf16[64,640]{1,0:T(8,128)(2,1)S(1)}, u32[]{:S(2)}, u32[]{:S(2)}) collective-permute-start(bf16[64,640]{1,0:T(8,128)(2,1)S(1)} %get-tuple-element.56), channel_id=1, source_target_pairs={{0,48},{2,50},{1,49},{3,51},{4,52},{6,54},{5,53},{7,55},{8,56},{10... | collective-permute-start | bytes 245768 | tf_op jit(solution)/shard_map/ppermute | solution.py:49
  61.0 0.0 collective-permute-start.17
  61.0 0.5 collective-permute-start.18
  61.5 0.0 collective-permute-done.14.refs_0_
  61.5 1.3 %collective-permute-start.19 = (bf16[64,640]{1,0:T(8,128)(2,1)S(1)}, bf16[64,640]{1,0:T(8,128)(2,1)S(1)}, u32[]{:S(2)}, u32[]{:S(2)}) collective-permute-start(bf16[64,640]{1,0:T(8,128)(2,1)S(1)} %get-tuple-element.59), channel_id=1, source_target_pairs={{0,80},{2,82},{1,81},{3,83},{4,84},{6,86},{5,85},{7,87},{8,88},{10... | collective-permute-start | bytes 245768 | tf_op jit(solution)/shard_map/ppermute | solution.py:49
  62.8 0.0 collective-permute-done.15.refs_1_
  62.8 0.6 collective-permute-start.20
  63.4 0.3 collective-permute-done.16.refs_2_
  63.7 2.6 %collective-permute-done.17.refs_3_ = bf16[64,640]{1,0:T(8,128)(2,1)S(1)} collective-permute-done((bf16[64,640]{1,0:T(8,128)(2,1)S(1)}, bf16[64,640]{1,0:T(8,128)(2,1)S(1)}, u32[]{:S(2)}, u32[]{:S(2)}) %collective-permute-start.17) | collective-permute-done | bytes 81952 | tf_op jit(solution)/shard_map/ppermute | solution.py:49
  66.3 0.0 collective-permute-done.18.refs_4_
  66.3 2.1 %collective-permute-done.19.refs_5_ = bf16[64,640]{1,0:T(8,128)(2,1)S(1)} collective-permute-done((bf16[64,640]{1,0:T(8,128)(2,1)S(1)}, bf16[64,640]{1,0:T(8,128)(2,1)S(1)}, u32[]{:S(2)}, u32[]{:S(2)}) %collective-permute-start.19) | collective-permute-done | bytes 81952 | tf_op jit(solution)/shard_map/ppermute | solution.py:49
  68.4 0.0 collective-permute-done.20.refs_6_
  68.4 0.0 slice-done
  68.4 0.0 slice-done.1
  68.4 6.3 %attend.1 = bf16[64,4096]{1,0:T(8,128)(2,1)} custom-call(s32[8]{0:T(128)S(1)} %stack.79.group_ref, s32[4]{0:T(128)S(1)} %and_select_fusion.length_ref, f32[64,128]{1,0:T(8,128)S(1)} %get-tuple-element.40.cos_ref, f32[64,128]{1,0:T(8,128)S(1)} %get-tuple-element.41.sin_ref, bf16[4,1024,1024]{2,1,0:T(8,128)(2,1)S(1)} %bitcast.20, ...), custom_call_target="tpu_custom_call" | custom-call | tf_op jit(solution)/shard_map/attend/pallas_call | solution.py:230
  (13 shorter events, 0.2 us)
Async XLA Ops:
  0.0 12.0 %copy-start = (s32[256]{0:T(256)S(1)}, s32[256]{0:T(256)}, u32[]{:S(2)}) copy-start(s32[256]{0:T(256)} %param.13) | copy-start | bytes 3076
  0.0 18.2 %collective-permute-start = (bf16[80,4096]{1,0:T(8,128)(2,1)}, bf16[80,4096]{1,0:T(8,128)(2,1)S(1)}, u32[]{:S(2)}, u32[]{:S(2)}) collective-permute-start(bf16[80,4096]{1,0:T(8,128)(2,1)} %bitcast.21), channel_id=1, source_target_pairs={{0,4},{2,6},{1,5},{3,7},{4,8},{6,10},{5,9},{7,11},{8,12},{10,14},{... | collective-permute-start | bytes 1966088 | tf_op jit(solution)/shard_map/ppermute | solution.py:49
  2.1 18.4 %collective-permute-start.2 = (bf16[80,4096]{1,0:T(8,128)(2,1)}, bf16[80,4096]{1,0:T(8,128)(2,1)S(1)}, u32[]{:S(2)}, u32[]{:S(2)}) collective-permute-start(bf16[80,4096]{1,0:T(8,128)(2,1)} %bitcast.22), channel_id=1, source_target_pairs={{0,2},{2,1},{1,3},{3,0},{4,6},{6,5},{5,7},{7,4},{8,10},{10,9},{9,1... | collective-permute-start | bytes 1966088 | tf_op jit(solution)/shard_map/ppermute | solution.py:49
  3.3 18.8 %collective-permute-start.5 = (bf16[80,4096]{1,0:T(8,128)(2,1)}, bf16[80,4096]{1,0:T(8,128)(2,1)S(1)}, u32[]{:S(2)}, u32[]{:S(2)}) collective-permute-start(bf16[80,4096]{1,0:T(8,128)(2,1)} %bitcast.23), channel_id=1, source_target_pairs={{0,12},{2,14},{1,13},{3,15},{4,0},{6,2},{5,1},{7,3},{8,4},{10,6},{... | collective-permute-start | bytes 1966088 | tf_op jit(solution)/shard_map/ppermute | solution.py:49
  4.9 2.2 %collective-permute-start.1 = (bf16[16,128]{1,0:T(8,128)(2,1)S(1)}, bf16[16,128]{1,0:T(8,128)(2,1)S(1)}, u32[]{:S(2)}, u32[]{:S(2)}) collective-permute-start(bf16[16,128]{1,0:T(8,128)(2,1)S(1)} %broadcast_in_dim.16), channel_id=1, source_target_pairs={{0,64},{2,66},{1,65},{3,67},{4,68},{6,70},{5,69},{7,71},{8,72},{10... | collective-permute-start | bytes 12296 | tf_op jit(solution)/shard_map/ppermute | solution.py:49
  7.1 1.0 %copy-start.1 = (bf16[64,4096]{1,0:T(8,128)(2,1)S(1)}, bf16[64,4096]{1,0:T(8,128)(2,1)}, u32[]{:S(2)}) copy-start(bf16[64,4096]{1,0:T(8,128)(2,1)} %rows.1) | copy-start | bytes 1572868
  8.2 36.1 %copy-start.2 = (bf16[4096,80]{0,1:T(8,128)(2,1)S(1)}, bf16[4096,80]{0,1:T(8,128)(2,1)}, u32[]{:S(2)}) copy-start(bf16[4096,80]{0,1:T(8,128)(2,1)} %param.9) | copy-start | bytes 1966084
  8.2 14.8 %collective-permute-start.9 = (bf16[64,4096]{1,0:T(8,128)(2,1)S(1)}, bf16[64,4096]{1,0:T(8,128)(2,1)}, u32[]{:S(2)}, u32[]{:S(2)}) collective-permute-start(bf16[64,4096]{1,0:T(8,128)(2,1)S(1)} %copy_rows.1), channel_id=1, source_target_pairs={{0,48},{2,50},{1,49},{3,51},{4,52},{6,54},{5,53},{7,55},{8,56},{10... | collective-permute-start | bytes 1572872 | tf_op jit(solution)/shard_map/ppermute | solution.py:49
  12.0 14.2 %collective-permute-start.8 = (bf16[64,4096]{1,0:T(8,128)(2,1)S(1)}, bf16[64,4096]{1,0:T(8,128)(2,1)}, u32[]{:S(2)}, u32[]{:S(2)}) collective-permute-start(bf16[64,4096]{1,0:T(8,128)(2,1)S(1)} %copy_rows.1), channel_id=1, source_target_pairs={{0,16},{2,18},{1,17},{3,19},{4,20},{6,22},{5,21},{7,23},{8,24},{10... | collective-permute-start | bytes 1572872 | tf_op jit(solution)/shard_map/ppermute | solution.py:49
  18.2 18.5 %collective-permute-start.4 = (bf16[80,4096]{1,0:T(8,128)(2,1)S(1)}, bf16[80,4096]{1,0:T(8,128)(2,1)S(1)}, u32[]{:S(2)}, u32[]{:S(2)}) collective-permute-start(bf16[80,4096]{1,0:T(8,128)(2,1)S(1)} %collective-permute-done.refs_2_), channel_id=1, source_target_pairs={{0,3},{2,0},{1,2},{3,1},{4,7},{6,4},{5,6},{7,5},{8,11},{10,8},{9,1... | collective-permute-start | bytes 1966088 | tf_op jit(solution)/shard_map/ppermute | solution.py:49
  20.6 16.1 %collective-permute-start.3 = (bf16[80,4096]{1,0:T(8,128)(2,1)S(1)}, bf16[80,4096]{1,0:T(8,128)(2,1)S(1)}, u32[]{:S(2)}, u32[]{:S(2)}) collective-permute-start(bf16[80,4096]{1,0:T(8,128)(2,1)S(1)} %collective-permute-done.2.refs_1_), channel_id=1, source_target_pairs={{0,8},{2,10},{1,9},{3,11},{4,12},{6,14},{5,13},{7,15},{8,0},{10,2}... | collective-permute-start | bytes 1966088 | tf_op jit(solution)/shard_map/ppermute | solution.py:49
  22.2 15.4 %collective-permute-start.6 = (bf16[80,4096]{1,0:T(8,128)(2,1)S(1)}, bf16[80,4096]{1,0:T(8,128)(2,1)S(1)}, u32[]{:S(2)}, u32[]{:S(2)}) collective-permute-start(bf16[80,4096]{1,0:T(8,128)(2,1)S(1)} %collective-permute-done.5.refs_4_), channel_id=1, source_target_pairs={{0,2},{2,1},{1,3},{3,0},{4,6},{6,5},{5,7},{7,4},{8,10},{10,9},{9,1... | collective-permute-start | bytes 1966088 | tf_op jit(solution)/shard_map/ppermute | solution.py:49
  23.0 13.3 %collective-permute-start.7 = (bf16[64,4096]{1,0:T(8,128)(2,1)S(1)}, bf16[64,4096]{1,0:T(8,128)(2,1)S(1)}, u32[]{:S(2)}, u32[]{:S(2)}) collective-permute-start(bf16[64,4096]{1,0:T(8,128)(2,1)S(1)} %copy_rows.1), channel_id=1, source_target_pairs={{0,32},{2,34},{1,33},{3,35},{4,36},{6,38},{5,37},{7,39},{8,40},{10... | collective-permute-start | bytes 1572872 | tf_op jit(solution)/shard_map/ppermute | solution.py:49
  37.6 6.7 %collective-permute-start.10 = (bf16[192,4096]{1,0:T(8,128)(2,1)S(1)}, bf16[192,4096]{1,0:T(8,128)(2,1)S(1)}, u32[]{:S(2)}, u32[]{:S(2)}) collective-permute-start(bf16[192,4096]{1,0:T(8,128)(2,1)S(1)} %pad_maximum_fusion.refs_6_), channel_id=1, source_target_pairs={{0,64},{2,66},{1,65},{3,67},{4,68},{6,70},{5,69},{7,71},{8,72},{10... | collective-permute-start | bytes 4718600 | tf_op jit(solution)/shard_map/ppermute | solution.py:49
  40.5 3.8 %collective-permute-start.11 = (bf16[64,4096]{1,0:T(8,128)(2,1)S(1)}, bf16[64,4096]{1,0:T(8,128)(2,1)S(1)}, u32[]{:S(2)}, u32[]{:S(2)}) collective-permute-start(bf16[64,4096]{1,0:T(8,128)(2,1)S(1)} %collective-permute-done.7.refs_7_), channel_id=1, source_target_pairs={{0,64},{2,66},{1,65},{3,67},{4,68},{6,70},{5,69},{7,71},{8,72},{10... | collective-permute-start | bytes 1572872 | tf_op jit(solution)/shard_map/ppermute | solution.py:49
  40.5 10.0 %collective-permute-start.12 = (bf16[80,2048]{1,0:T(8,128)(2,1)S(1)}, bf16[80,2048]{1,0:T(8,128)(2,1)S(1)}, u32[]{:S(2)}, u32[]{:S(2)}) collective-permute-start(bf16[80,2048]{1,0:T(8,128)(2,1)S(1)} %slice.6), channel_id=1, source_target_pairs={{0,4},{2,6},{1,5},{3,7},{4,8},{6,10},{5,9},{7,11},{8,12},{10,14},{... | collective-permute-start | bytes 983048 | tf_op jit(solution)/shard_map/ppermute | solution.py:49
  41.0 27.4 %slice-start = ((s8[8388608]{0:T(1024)(128)(4,1)}), s8[4194304]{0:T(1024)(128)(4,1)S(1)}, s32[]{:S(2)}) async-start(s8[8388608]{0:T(1024)(128)(4,1)} %bitcast.19), calls=%async_computation | async-start | bytes 8388608
  41.0 27.3 %slice-start.1 = ((s8[8388608]{0:T(1024)(128)(4,1)}), s8[4194304]{0:T(1024)(128)(4,1)S(1)}, s32[]{:S(2)}) async-start(s8[8388608]{0:T(1024)(128)(4,1)} %bitcast.19), calls=%async_computation.1 | async-start | bytes 8388608
  41.0 9.5 %collective-permute-start.13 = (bf16[80,2048]{1,0:T(8,128)(2,1)S(1)}, bf16[80,2048]{1,0:T(8,128)(2,1)S(1)}, u32[]{:S(2)}, u32[]{:S(2)}) collective-permute-start(bf16[80,2048]{1,0:T(8,128)(2,1)S(1)} %slice.12), channel_id=1, source_target_pairs={{0,12},{2,14},{1,13},{3,15},{4,0},{6,2},{5,1},{7,3},{8,4},{10,6},{... | collective-permute-start | bytes 983048 | tf_op jit(solution)/shard_map/ppermute | solution.py:49
  52.7 8.8 %collective-permute-start.14 = (bf16[64,640]{1,0:T(8,128)(2,1)S(1)}, bf16[64,640]{1,0:T(8,128)(2,1)S(1)}, u32[]{:S(2)}, u32[]{:S(2)}) collective-permute-start(bf16[64,640]{1,0:T(8,128)(2,1)S(1)} %get-tuple-element.54), channel_id=1, source_target_pairs={{0,32},{2,34},{1,33},{3,35},{4,36},{6,38},{5,37},{7,39},{8,40},{10... | collective-permute-start | bytes 245768 | tf_op jit(solution)/shard_map/ppermute | solution.py:49
  56.4 6.4 %collective-permute-start.15 = (bf16[64,640]{1,0:T(8,128)(2,1)S(1)}, bf16[64,640]{1,0:T(8,128)(2,1)S(1)}, u32[]{:S(2)}, u32[]{:S(2)}) collective-permute-start(bf16[64,640]{1,0:T(8,128)(2,1)S(1)} %get-tuple-element.55), channel_id=1, source_target_pairs={{0,96},{2,98},{1,97},{3,99},{4,100},{6,102},{5,101},{7,103},{8,104... | collective-permute-start | bytes 245768 | tf_op jit(solution)/shard_map/ppermute | solution.py:49
  57.7 6.0 %collective-permute-start.16 = (bf16[64,640]{1,0:T(8,128)(2,1)S(1)}, bf16[64,640]{1,0:T(8,128)(2,1)S(1)}, u32[]{:S(2)}, u32[]{:S(2)}) collective-permute-start(bf16[64,640]{1,0:T(8,128)(2,1)S(1)} %get-tuple-element.56), channel_id=1, source_target_pairs={{0,48},{2,50},{1,49},{3,51},{4,52},{6,54},{5,53},{7,55},{8,56},{10... | collective-permute-start | bytes 245768 | tf_op jit(solution)/shard_map/ppermute | solution.py:49
  61.0 5.3 %collective-permute-start.17 = (bf16[64,640]{1,0:T(8,128)(2,1)S(1)}, bf16[64,640]{1,0:T(8,128)(2,1)S(1)}, u32[]{:S(2)}, u32[]{:S(2)}) collective-permute-start(bf16[64,640]{1,0:T(8,128)(2,1)S(1)} %get-tuple-element.57), channel_id=1, source_target_pairs={{0,112},{2,114},{1,113},{3,115},{4,116},{6,118},{5,117},{7,119},{8... | collective-permute-start | bytes 245768 | tf_op jit(solution)/shard_map/ppermute | solution.py:49
  61.0 5.3 %collective-permute-start.18 = (bf16[64,640]{1,0:T(8,128)(2,1)S(1)}, bf16[64,640]{1,0:T(8,128)(2,1)S(1)}, u32[]{:S(2)}, u32[]{:S(2)}) collective-permute-start(bf16[64,640]{1,0:T(8,128)(2,1)S(1)} %get-tuple-element.58), channel_id=1, source_target_pairs={{0,16},{2,18},{1,17},{3,19},{4,20},{6,22},{5,21},{7,23},{8,24},{10... | collective-permute-start | bytes 245768 | tf_op jit(solution)/shard_map/ppermute | solution.py:49
  61.5 6.8 %collective-permute-start.19 = (bf16[64,640]{1,0:T(8,128)(2,1)S(1)}, bf16[64,640]{1,0:T(8,128)(2,1)S(1)}, u32[]{:S(2)}, u32[]{:S(2)}) collective-permute-start(bf16[64,640]{1,0:T(8,128)(2,1)S(1)} %get-tuple-element.59), channel_id=1, source_target_pairs={{0,80},{2,82},{1,81},{3,83},{4,84},{6,86},{5,85},{7,87},{8,88},{10... | collective-permute-start | bytes 245768 | tf_op jit(solution)/shard_map/ppermute | solution.py:49
  62.8 5.5 %collective-permute-start.20 = (bf16[64,640]{1,0:T(8,128)(2,1)S(1)}, bf16[64,640]{1,0:T(8,128)(2,1)S(1)}, u32[]{:S(2)}, u32[]{:S(2)}) collective-permute-start(bf16[64,640]{1,0:T(8,128)(2,1)S(1)} %get-tuple-element.60), channel_id=1, source_target_pairs={{0,64},{2,66},{1,65},{3,67},{4,68},{6,70},{5,69},{7,71},{8,72},{10... | collective-permute-start | bytes 245768 | tf_op jit(solution)/shard_map/ppermute | solution.py:49
